TPU v7x, 512 devices: a whole 4x4x16 slice. The times are simulated.
512 devices in a mesh: wide: 64 (over x, z), mp: 8 (over y, core).
Axes of the slice: x: 4, y: 4, z: 16, core: 2. Of those that a mesh axis runs over, the one named last changes fastest.
Arguments:
- inputs: bfloat16 [2, 128, 16384], P(None, None, 'wide'), may hold values from -6 to 6
- attn_gain: bfloat16 [16384], P('wide'), may hold values from 0.25 to 1.75
- w_query: bfloat16 [16384, 16384], P('wide', 'mp'), may hold values from -0.0473929 to 0.0473929
- w_keyval: bfloat16 [16384, 8, 256], P('wide', 'mp'), may hold values from -0.046875 to 0.046875
- w_out: bfloat16 [16384, 16384], P('mp', 'wide'), may hold values from -0.046875 to 0.046875
- ffn_gain: bfloat16 [16384], P('wide'), may hold values from 0.25 to 1.75
- w_gateup: bfloat16 [16384, 2, 6656], P('wide', None, 'mp'), may hold values from -0.046875 to 0.046875
- w_down: bfloat16 [6656, 16384], P('mp', 'wide'), may hold values from -0.078125 to 0.078125
- kv_cache: bfloat16 [128, 768, 8, 256], P('wide', None, 'mp'), may hold values from -11 to 11
- lengths: int32 [128], P('wide'), may hold values from 1 to 768, as said below
- positions: int32 [128], P('wide'), may hold values from 768 to 3071
Outputs:
- outputs: bfloat16 [2, 128, 16384], P(None, None, 'wide')
- new_entries: bfloat16 [2, 128, 8, 256], P(None, 'wide', 'mp')
Inputs may be any that keep to these rules, and one draw needn't show every extreme that they name: `lengths`: some row has exactly 768 valid positions and some row exactly 1.
All inputs are finite; a program needn't handle non-finite values.
Results may differ from a plain program's by a relative error of at most 0.012.
Values may be sent and summed in bfloat16 or wider, within the bound.
No kernel may reach another device: no remote copies, remote signals or barrier semaphores. Data moves between devices by JAX's collectives and lax.ppermute only.
A program may use at most 64 MiB of HBM per device.

v0:
```python
import jax
import jax.numpy as jnp
from jax import lax
from jax.sharding import PartitionSpec as P

D = 16384
STEPS = 2


epsilon = 1e-05
rope_base = 500000.0
masked_score = -1e30


def rotate(vectors, offsets):
    half_size = vectors.shape[-1] // 2
    freqs = rope_base ** (-(jnp.arange(half_size, dtype=jnp.float32) * 2.0 / vectors.shape[-1]))
    angles = offsets.astype(jnp.float32)[..., None] * freqs
    cosine = jnp.cos(angles)
    sine = jnp.sin(angles)
    first_half = vectors[..., :half_size]
    second_half = vectors[..., half_size:]
    return jnp.concatenate(
        [first_half * cosine - second_half * sine, second_half * cosine + first_half * sine],
        axis=-1,
    )


def full_attend(grouped, kv_cache, lengths, fresh_keys, fresh_values, score_scale):
    head_dim = grouped.shape[-1]
    scores = (
        jnp.einsum(
            "rkgd,rlkd->rkgl", grouped, kv_cache[..., :head_dim], preferred_element_type=jnp.float32
        )
        * score_scale
    )
    live = jnp.arange(kv_cache.shape[1])[None, None, None, :] < lengths[:, None, None, None]
    scores = jnp.where(live, scores, masked_score)
    fresh_scores = (
        jnp.einsum("rkgd,rtkd->rkgt", grouped, fresh_keys, preferred_element_type=jnp.float32)
        * score_scale
    )
    highest = jnp.maximum(jnp.max(scores, axis=-1), jnp.max(fresh_scores, axis=-1))[..., None]
    cache_weights = jnp.exp(scores - highest)
    fresh_weights = jnp.exp(fresh_scores - highest)
    total = jnp.sum(cache_weights, axis=-1, keepdims=True) + jnp.sum(
        fresh_weights, axis=-1, keepdims=True
    )
    cache_probs = (cache_weights / total).astype(jnp.bfloat16)
    fresh_probs = (fresh_weights / total).astype(jnp.bfloat16)
    mixed = jnp.einsum(
        "rkgl,rlkd->rkgd", cache_probs, kv_cache[..., head_dim:], preferred_element_type=jnp.float32
    )
    return mixed + jnp.einsum(
        "rkgt,rtkd->rkgd", fresh_probs, fresh_values, preferred_element_type=jnp.float32
    )


def body(
    inputs,
    attn_gain,
    w_query,
    w_keyval,
    w_out,
    ffn_gain,
    w_gateup,
    w_down,
    kv_cache,
    lengths,
    positions,
):
    local_width = inputs.shape[2]
    local_rows = kv_cache.shape[0]
    head_dim = kv_cache.shape[3] // 2
    local_kv = w_keyval.shape[1]
    local_queries = w_query.shape[1] // head_dim
    group_size = local_queries // local_kv
    local_hidden = w_down.shape[0]
    score_scale = head_dim ** (-0.5)
    keyval_weight = w_keyval.reshape(local_width, local_kv * 2 * head_dim)
    gateup_weight = w_gateup.reshape(local_width, 2 * local_hidden)
    attn_scale = attn_gain.astype(jnp.float32)
    ffn_scale = ffn_gain.astype(jnp.float32)
    fresh_list = []
    output_list = []
    for step_index in range(STEPS):
        current = inputs[step_index].astype(jnp.float32)
        squares = lax.psum(jnp.sum(current * current, axis=-1), "wide")
        normed = (current * lax.rsqrt(squares / D + epsilon)[:, None] * attn_scale).astype(
            jnp.bfloat16
        )
        query_sum, keyval_sum = (
            lax.psum_scatter(
                jnp.dot(normed, w_query, preferred_element_type=jnp.float32),
                "wide",
                scatter_dimension=0,
                tiled=True,
            ),
            lax.psum_scatter(
                jnp.dot(normed, keyval_weight, preferred_element_type=jnp.float32),
                "wide",
                scatter_dimension=0,
                tiled=True,
            ),
        )
        offsets = (positions + step_index)[:, None]
        queries = rotate(query_sum.reshape(local_rows, local_queries, head_dim), offsets).astype(
            jnp.bfloat16
        )
        keyval_heads = keyval_sum.reshape(local_rows, local_kv, 2 * head_dim)
        keys_new = rotate(keyval_heads[..., :head_dim], offsets).astype(jnp.bfloat16)
        values_new = keyval_heads[..., head_dim:].astype(jnp.bfloat16)
        fresh_list.append(jnp.concatenate([keys_new, values_new], axis=-1))
        fresh = jnp.stack(fresh_list, axis=1)
        grouped = queries.reshape(local_rows, local_kv, group_size, head_dim)
        mixed = full_attend(
            grouped, kv_cache, lengths, fresh[..., :head_dim], fresh[..., head_dim:], score_scale
        )
        heads = mixed.astype(jnp.bfloat16).reshape(local_rows, local_queries * head_dim)
        attn_terms = jnp.dot(
            lax.all_gather(heads, "wide", axis=0, tiled=True),
            w_out,
            preferred_element_type=jnp.float32,
        )
        hidden_state = current + lax.psum(attn_terms.astype(jnp.bfloat16), "mp").astype(jnp.float32)
        squares_ffn = lax.psum(jnp.sum(hidden_state * hidden_state, axis=-1), "wide")
        ffn_in = (hidden_state * lax.rsqrt(squares_ffn / D + epsilon)[:, None] * ffn_scale).astype(
            jnp.bfloat16
        )
        gateup_terms = jnp.dot(ffn_in, gateup_weight, preferred_element_type=jnp.float32)
        gateup = lax.psum_scatter(gateup_terms, "wide", scatter_dimension=0, tiled=True)
        activated = (jax.nn.silu(gateup[:, :local_hidden]) * gateup[:, local_hidden:]).astype(
            jnp.bfloat16
        )
        down_terms = jnp.dot(
            lax.all_gather(activated, "wide", axis=0, tiled=True),
            w_down,
            preferred_element_type=jnp.float32,
        )
        result = hidden_state + lax.psum(down_terms.astype(jnp.bfloat16), "mp").astype(jnp.float32)
        output_list.append(result.astype(jnp.bfloat16))
    return (jnp.stack(output_list), jnp.stack(fresh_list))


def solution(mesh):
    in_specs = (
        P(None, None, "wide"),
        P("wide"),
        P("wide", "mp"),
        P("wide", "mp", None),
        P("mp", "wide"),
        P("wide"),
        P("wide", None, "mp"),
        P("mp", "wide"),
        P("wide", None, "mp", None),
        P("wide"),
        P("wide"),
    )
    out_specs = (P(None, None, "wide"), P(None, "wide", "mp", None))
    return jax.shard_map(body, mesh=mesh, in_specs=in_specs, out_specs=out_specs, check_vma=False)
```

profile of v0, /device:TPU:1, one launch (start us, length us, event | category | flops | bytes accessed | tf_op | source)
XLA Modules:
  0.0 1361.7 jit_solution(17013066656325160782)
XLA Ops:
  7.2 1.1 fusion.11
  8.3 122.6 %all-reduce.7 = (f32[128]{0:T(128)S(1)}, f32[128]{0:T(128)S(1)}) all-reduce(f32[128]{0:T(128)S(1)} %get-tuple-element.5, f32[128]{0:T(128)S(1)} %get-tuple-element.4), channel_id=1, replica_groups=mesh['wide'=64,'mp'=8] {'wide'}, use_global_device_ids=true, to_apply=%region_12.13 | all-reduce | flops 256 | bytes 2048 | tf_op jit(solution)/shard_map/psum | solution.py:88
  131.0 1.3 fusion.33
  132.3 1.3 fusion.37
  133.7 0.9 fusion.21
  134.5 0.9 fusion.23
  135.4 0.0 all-reduce.23.cloned.1.call-start
  135.5 1.3 dynamic-slice
  137.5 0.6 copy-done.18
  138.1 0.6 copy-done.16
  138.8 0.1 iota_compare_fusion
  138.8 0.1 multiply_cosine_fusion.3
  139.0 284.6 %all-reduce.19.cloned.1.call-done = (f32[128,2048]{1,0:T(8,128)}, f32[128,256]{1,0:T(8,128)}, f32[128,256]{1,0:T(8,128)}, f32[128,2048]{1,0:T(8,128)}) async-done(((f32[128,2048]{1,0:T(8,128)}, f32[128,256]{1,0:T(8,128)}, f32[128,256]{1,0:T(8,128)}, f32[128,2048]{1,0:T(8,128)}), (f32[128,2048]{1,0:T(8,128)}, f32[128,256]{1,0:T(8,128)}, f32[128,256]{1,0:T(8,128)}, ...) | async-done | bytes 2359312
  423.6 0.7 dynamic-slice_bitcast_fusion.2
  424.3 0.7 dynamic-slice_bitcast_fusion.3
  425.0 0.1 fusion.93
  425.1 0.3 copy-done.10
  425.5 0.1 fusion.120
  425.6 0.9 dynamic-slice_bitcast_fusion.1
  426.4 0.1 subtract_convert_fusion.1
  426.5 0.2 fusion.67
  426.7 0.3 fusion.105
  427.0 0.2 fusion.25
  427.2 0.2 fusion.3
  427.5 73.1 %all-gather = bf16[64,2,2048]{2,1,0:T(2,128)(2,1)S(1)} all-gather(bf16[1,2,2048]{2,1,0:T(2,128)(2,1)S(1)} %reshape.517), channel_id=1, replica_groups=mesh['wide'=64,'mp'=8] {'wide'}, dimensions={0}, use_global_device_ids=true | all-gather | bytes 532480 | tf_op jit(solution)/shard_map/all_gather | solution.py:121
  500.6 0.2 reshape.518
  500.8 0.1 fusion.121
  500.9 0.8 dynamic-slice_bitcast_fusion
  501.8 0.1 subtract_convert_fusion
  501.9 0.3 fusion.103
  502.2 0.2 fusion.104
  502.5 0.2 fusion.26
  502.7 0.2 fusion.4
  502.9 0.3 copy-done.15
  503.2 0.2 fusion.2
  503.4 71.9 %all-gather.2 = bf16[64,2,2048]{2,1,0:T(2,128)(2,1)S(1)} all-gather(bf16[1,2,2048]{2,1,0:T(2,128)(2,1)S(1)} %reshape.521), channel_id=1, replica_groups=mesh['wide'=64,'mp'=8] {'wide'}, dimensions={0}, use_global_device_ids=true | all-gather | bytes 532480 | tf_op jit(solution)/shard_map/all_gather | solution.py:121
  575.3 1.0 reshape.522
  576.3 0.9 convolution_convert_fusion.3
  577.2 0.1 copy-done.4
  577.3 0.9 convolution_convert_fusion.1
  578.3 0.0 all-reduce.17.cloned.1.call-start
  578.4 0.6 copy-done.19
  578.9 128.6 %all-reduce.23.cloned.1.call-done = (bf16[128,256]{1,0:T(8,128)(2,1)}, bf16[128,256]{1,0:T(8,128)(2,1)}) async-done(((bf16[128,256]{1,0:T(8,128)(2,1)}, bf16[128,256]{1,0:T(8,128)(2,1)}), (bf16[128,256]{1,0:T(8,128)(2,1)}, bf16[128,256]{1,0:T(8,128)(2,1)})) %all-reduce.23.cloned.1.call-update) | async-done | bytes 131088 | tf_op jit(solution)/shard_map/psum | solution.py:125
  707.5 1.0 multiply_reduce_fusion.1
  708.5 116.0 %all-reduce.6 = (f32[128]{0:T(128)S(1)}, f32[128]{0:T(128)S(1)}) all-reduce(f32[128]{0:T(128)S(1)} %get-tuple-element.3, f32[128]{0:T(128)S(1)} %get-tuple-element.2), channel_id=1, replica_groups=mesh['wide'=64,'mp'=8] {'wide'}, use_global_device_ids=true, to_apply=%region_21.22 | all-reduce | flops 256 | bytes 2048 | tf_op jit(solution)/shard_map/psum | solution.py:126
  824.5 1.3 fusion.27
  825.9 1.4 fusion.29
  827.3 0.5 copy-done.11
  827.8 0.1 fusion.118
  827.9 0.5 copy-done.13
  828.4 0.1 fusion.119
  828.5 283.0 %all-reduce.17.cloned.1.call-done = (f32[128,1664]{1,0:T(8,128)}, f32[128,1664]{1,0:T(8,128)}) async-done(((f32[128,1664]{1,0:T(8,128)}, f32[128,1664]{1,0:T(8,128)}), (f32[128,1664]{1,0:T(8,128)}, f32[128,1664]{1,0:T(8,128)})) %all-reduce.17.cloned.1.call-update) | async-done | bytes 1703952
  1111.5 0.9 fusion.65
  1112.4 61.6 %all-gather.1 = bf16[64,2,832]{2,1,0:T(2,128)(2,1)S(1)} all-gather(bf16[1,2,832]{2,1,0:T(2,128)(2,1)S(1)} %fusion.65), channel_id=1, replica_groups=mesh['wide'=64,'mp'=8] {'wide'}, dimensions={0}, use_global_device_ids=true | all-gather | bytes 216320 | tf_op jit(solution)/shard_map/all_gather | solution.py:136
  1174.0 0.2 reshape.520
  1174.2 0.9 fusion.66
  1175.1 63.0 %all-gather.3 = bf16[64,2,832]{2,1,0:T(2,128)(2,1)S(1)} all-gather(bf16[1,2,832]{2,1,0:T(2,128)(2,1)S(1)} %fusion.66), channel_id=1, replica_groups=mesh['wide'=64,'mp'=8] {'wide'}, dimensions={0}, use_global_device_ids=true | all-gather | bytes 216320 | tf_op jit(solution)/shard_map/all_gather | solution.py:136
  1238.1 0.2 reshape.524
  1238.3 0.9 convolution_convert_fusion.2
  1239.1 0.9 convolution_convert_fusion
  1240.0 0.6 pad_maximum_fusion.3
  1240.6 113.0 %all-reduce.21.cloned.1.call-done = (bf16[128,256]{1,0:T(8,128)(2,1)}, bf16[128,256]{1,0:T(8,128)(2,1)}) async-done(((bf16[128,256]{1,0:T(8,128)(2,1)}, bf16[128,256]{1,0:T(8,128)(2,1)}), (bf16[128,256]{1,0:T(8,128)(2,1)}, bf16[128,256]{1,0:T(8,128)(2,1)})) %all-reduce.21.cloned.1.call-update) | async-done | bytes 131088 | tf_op jit(solution)/shard_map/psum | solution.py:140
  1353.6 0.9 fusion.28
  1354.5 0.7 pad_maximum_fusion
  (59 shorter events, 0.4 us)
Async XLA Ops:
  7.2 123.8 %copy-start = (bf16[256,2048]{1,0:T(8,128)(2,1)S(1)}, bf16[256,2048]{1,0:T(8,128)(2,1)}, u32[]{:S(2)}) copy-start(bf16[256,2048]{1,0:T(8,128)(2,1)} %param.13) | copy-start | bytes 3145732
  7.2 123.8 %copy-start.1 = (bf16[2,128,256]{2,1,0:T(8,128)(2,1)S(1)}, bf16[2,128,256]{2,1,0:T(8,128)(2,1)}, u32[]{:S(2)}) copy-start(bf16[2,128,256]{2,1,0:T(8,128)(2,1)} %param.11) | copy-start | bytes 393220
  7.2 1.1 copy-start.17
  7.2 416.4 %all-reduce.19.cloned.1.call-start = ((), (), s32[]{:S(2)}) async-start(), calls=%async_computation.1 | async-start | bytes 4718592
  132.3 1.3 copy-start.9
  135.4 291.3 %copy-start.6 = (bf16[2,768,1,256]{3,1,2,0:T(8,128)(2,1)S(1)}, bf16[2,768,1,256]{3,1,2,0:T(8,128)(2,1)}, u32[]{:S(2)}) copy-start(bf16[2,768,1,256]{3,1,2,0:T(8,128)(2,1)} %param.19) | copy-start | bytes 2359300
  135.4 572.1 %all-reduce.23.cloned.1.call-start = ((), (), s32[]{:S(2)}) async-start(), calls=%async_computation.3 | async-start | bytes 262144 | tf_op jit(solution)/shard_map/psum | solution.py:125
  137.5 0.7 copy-start.18
  138.1 0.7 copy-start.16
  425.0 0.5 copy-start.10
  425.1 75.7 %copy-start.12 = (bf16[2,1,128]{2,0,1:T(2,128)(2,1)}, bf16[2,1,128]{2,0,1:T(2,128)(2,1)S(1)}, u32[]{:S(2)}) copy-start(bf16[2,1,128]{2,0,1:T(2,128)(2,1)S(1)} %slice.184) | copy-start | bytes 1540
  425.6 76.6 %copy-start.14 = (bf16[2,1,1,256]{3,1,0,2:T(2,128)(2,1)}, bf16[2,1,1,256]{3,1,0,2:T(2,128)(2,1)S(1)}, u32[]{:S(2)}) copy-start(bf16[2,1,1,256]{3,1,0,2:T(2,128)(2,1)S(1)} %copy.29) | copy-start | bytes 3076
  502.5 0.7 copy-start.15
  502.7 73.6 %copy-start.2 = (bf16[2048,256]{1,0:T(8,128)(2,1)S(1)}, bf16[2048,256]{1,0:T(8,128)(2,1)}, u32[]{:S(2)}) copy-start(bf16[2048,256]{1,0:T(8,128)(2,1)} %param.15) | copy-start | bytes 3145732
  576.3 1.0 copy-start.4
  577.3 247.2 %copy-start.3 = (bf16[256,2,832]{0,2,1:T(8,128)(2,1)S(1)}, bf16[256,2,832]{0,2,1:T(8,128)(2,1)}, u32[]{:S(2)}) copy-start(bf16[256,2,832]{0,2,1:T(8,128)(2,1)} %param.17) | copy-start | bytes 2555908
  578.3 0.7 copy-start.19
  578.3 533.1 %all-reduce.17.cloned.1.call-start = ((), (), s32[]{:S(2)}) async-start(), calls=%async_computation | async-start | bytes 3407872
  707.5 117.0 %copy-start.8 = (bf16[128,256]{1,0:T(8,128)(2,1)S(1)}, bf16[128,256]{1,0:T(8,128)(2,1)}, u32[]{:S(2)}) copy-start(bf16[128,256]{1,0:T(8,128)(2,1)} %get-tuple-element.19) | copy-start | bytes 196612
  824.5 1.3 copy-start.7
  827.2 0.6 copy-start.11
  827.2 526.3 %all-reduce.21.cloned.1.call-start = ((), (), s32[]{:S(2)}) async-start(), calls=%async_computation.2 | async-start | bytes 262144 | tf_op jit(solution)/shard_map/psum | solution.py:140
  827.8 0.6 copy-start.13
  1174.1 64.1 %copy-start.5 = (bf16[832,256]{1,0:T(8,128)(2,1)S(1)}, bf16[832,256]{1,0:T(8,128)(2,1)}, u32[]{:S(2)}) copy-start(bf16[832,256]{1,0:T(8,128)(2,1)} %param.18) | copy-start | bytes 1277956
Sparse Core Ops, SparseCore 0:
  135.5 287.9 all-reduce.18
  578.4 129.0 all-reduce.22
  827.4 284.0 all-reduce.16
  1240.1 113.4 all-reduce.20
where the time goes:
time: 1360 us
  waiting for transfers between devices  809 us (59%)
  blocking collectives  508 us (37%)
  between operations  14.6 us (1%)
    unnamed x6, waiting for transfers between devices  568 us
    all_gather x2, blocking collectives, body(): lax.all_gather(heads, 'wide', axis=0, tiled=True)  145 us
    psum x1, waiting for transfers between devices, body(): lax.psum(attn_terms.astype(jnp.bfloat16), 'mp').astype(jnp.float32)  129 us
    all_gather x2, blocking collectives, body(): lax.all_gather(activated, 'wide', axis=0, tiled=True)  125 us
    psum x1, blocking collectives, body(): squares = lax.psum(jnp.sum(current * current, axis=-1), 'wide')  123 us
    psum x1, blocking collectives, body(): lax.psum(jnp.sum(hidden_state * hidden_state, axis=-1), 'wide')  116 us
    psum x1, waiting for transfers between devices, body(): lax.psum(down_terms.astype(jnp.bfloat16), 'mp').astype(jnp.float32)  113 us
  transfers between devices with their start and end apart: 4, of which 4 were waited for; matrix products, arithmetic and copies ran while one was open for 0% of the time, Pallas kernels for 0%

commit v1 on v0

v1 whole, which is shorter than its diff:
```python
import jax
import jax.numpy as jnp
from jax import lax
from jax.sharding import Mesh, PartitionSpec as P

D = 16384
STEPS = 2

epsilon = 1e-05
rope_base = 500000.0
masked_score = -1e30

WIDE = ("x", "zh", "zl")
MP = ("y", "core")
REDUCE_ORDER = ("x", "zl", "zh")
GATHER_ORDER = ("zh", "zl", "x")
SIZES = {"x": 4, "zh": 4, "zl": 4, "y": 4, "core": 2}


def rotate(vectors, offsets):
    half_size = vectors.shape[-1] // 2
    freqs = rope_base ** (-(jnp.arange(half_size, dtype=jnp.float32) * 2.0 / vectors.shape[-1]))
    angles = offsets.astype(jnp.float32)[..., None] * freqs
    cosine = jnp.cos(angles)
    sine = jnp.sin(angles)
    first_half = vectors[..., :half_size]
    second_half = vectors[..., half_size:]
    return jnp.concatenate(
        [first_half * cosine - second_half * sine, second_half * cosine + first_half * sine],
        axis=-1,
    )


def exchange(blocks, axis):
    return lax.all_to_all(blocks, axis, 0, 0, tiled=True)


def spread_sum(terms):
    rows, columns = terms.shape
    for axis in REDUCE_ORDER:
        size = SIZES[axis]
        rows //= size
        received = exchange(terms.astype(jnp.bfloat16).reshape(size, rows, columns), axis)
        terms = jnp.sum(received.astype(jnp.float32), axis=0)
    return terms


def collect(block):
    for axis in GATHER_ORDER:
        size = SIZES[axis]
        rows, columns = block.shape
        copies = jnp.broadcast_to(block[None], (size, rows, columns))
        block = exchange(copies, axis).reshape(size * rows, columns)
    return block


def group_sum(terms, base):
    rows, columns = terms.shape
    received = exchange(terms.astype(jnp.bfloat16).reshape(8, rows // 8, columns), MP)
    return base + jnp.sum(received.astype(jnp.float32), axis=0)


def group_collect(block):
    rows, columns = block.shape
    copies = jnp.broadcast_to(block[None], (8, rows, columns))
    return exchange(copies, MP).reshape(8 * rows, columns)


def lane_squares(values):
    squares = values * values
    return squares[:, :128] + squares[:, 128:]


def attend(queries, kv_cache, lengths, fresh_keys, fresh_values, score_scale):
    rows, steps, heads, head_dim = queries.shape
    merged = queries.reshape(rows, steps * heads, head_dim)
    scores = (
        jnp.einsum("rgd,rld->rgl", merged, kv_cache[..., :head_dim], preferred_element_type=jnp.float32)
        * score_scale
    )
    live = jnp.arange(kv_cache.shape[1])[None, None, :] < lengths[:, None, None]
    scores = jnp.where(live, scores, masked_score)
    fresh_scores = (
        jnp.einsum("rgd,rtd->rgt", merged, fresh_keys, preferred_element_type=jnp.float32) * score_scale
    )
    query_step = jnp.arange(steps * heads) // heads
    seen = jnp.arange(steps)[None, None, :] <= query_step[None, :, None]
    fresh_scores = jnp.where(seen, fresh_scores, masked_score)
    highest = jnp.maximum(jnp.max(scores, axis=-1), jnp.max(fresh_scores, axis=-1))[..., None]
    cache_weights = jnp.exp(scores - highest)
    fresh_weights = jnp.exp(fresh_scores - highest)
    total = jnp.sum(cache_weights, axis=-1, keepdims=True) + jnp.sum(
        fresh_weights, axis=-1, keepdims=True
    )
    cache_probs = (cache_weights / total).astype(jnp.bfloat16)
    fresh_probs = (fresh_weights / total).astype(jnp.bfloat16)
    mixed = jnp.einsum(
        "rgl,rld->rgd", cache_probs, kv_cache[..., head_dim:], preferred_element_type=jnp.float32
    ) + jnp.einsum("rgt,rtd->rgd", fresh_probs, fresh_values, preferred_element_type=jnp.float32)
    return mixed.reshape(rows, steps, heads, head_dim)


def body(
    inputs,
    attn_gain,
    w_query,
    w_keyval,
    w_out,
    ffn_gain,
    w_gateup,
    w_down,
    kv_cache,
    lengths,
    positions,
):
    steps, all_rows, local_width = inputs.shape
    local_rows = kv_cache.shape[0]
    head_dim = kv_cache.shape[3] // 2
    local_queries = w_query.shape[1] // head_dim
    local_hidden = w_down.shape[0]
    score_scale = head_dim ** (-0.5)
    keyval_weight = w_keyval.reshape(local_width, 2 * head_dim)
    gateup_weight = w_gateup.reshape(local_width, 2 * local_hidden)
    keyvals_at = local_queries * head_dim
    squares_at = keyvals_at + 2 * head_dim

    current = (
        inputs.reshape(steps, 4, 4, 4, local_rows, local_width)
        .transpose(1, 3, 2, 0, 4, 5)
        .reshape(steps * all_rows, local_width)
        .astype(jnp.float32)
    )
    scaled = (current * attn_gain.astype(jnp.float32)).astype(jnp.bfloat16)
    terms = jnp.concatenate(
        [
            jnp.dot(scaled, w_query, preferred_element_type=jnp.float32),
            jnp.dot(scaled, keyval_weight, preferred_element_type=jnp.float32),
            lane_squares(current),
        ],
        axis=1,
    )
    sums = spread_sum(terms)
    mean = jnp.sum(sums[:, squares_at:], axis=-1, keepdims=True) / D
    sums = (sums[:, :squares_at] * lax.rsqrt(mean + epsilon)).reshape(steps, local_rows, squares_at)
    offsets = positions[None, :] + jnp.arange(steps)[:, None]
    queries = rotate(
        sums[..., :keyvals_at].reshape(steps, local_rows, local_queries, head_dim), offsets[..., None]
    ).astype(jnp.bfloat16)
    keys_new = rotate(sums[..., keyvals_at : keyvals_at + head_dim], offsets).astype(jnp.bfloat16)
    values_new = sums[..., keyvals_at + head_dim :].astype(jnp.bfloat16)
    new_entries = jnp.concatenate([keys_new, values_new], axis=-1)[:, :, None, :]
    mixed = attend(
        queries.transpose(1, 0, 2, 3),
        kv_cache.reshape(local_rows, -1, 2 * head_dim),
        lengths,
        keys_new.transpose(1, 0, 2),
        values_new.transpose(1, 0, 2),
        score_scale,
    )
    heads = mixed.astype(jnp.bfloat16).transpose(1, 0, 2, 3).reshape(steps * local_rows, keyvals_at)

    attn_terms = jnp.dot(collect(heads), w_out, preferred_element_type=jnp.float32)
    own = lax.axis_index(MP) * (steps * all_rows // 8)
    residual = lax.dynamic_slice_in_dim(current, own, steps * all_rows // 8, axis=0)
    own_state = group_sum(attn_terms, residual)
    hidden_state = group_collect(own_state.astype(jnp.bfloat16)).astype(jnp.float32)
    ffn_in = (hidden_state * ffn_gain.astype(jnp.float32)).astype(jnp.bfloat16)
    gateup_terms = jnp.concatenate(
        [
            jnp.dot(ffn_in, gateup_weight, preferred_element_type=jnp.float32),
            lane_squares(hidden_state),
        ],
        axis=1,
    )
    gateup = spread_sum(gateup_terms)
    mean = jnp.sum(gateup[:, 2 * local_hidden :], axis=-1, keepdims=True) / D
    gateup = gateup[:, : 2 * local_hidden] * lax.rsqrt(mean + epsilon)
    activated = (jax.nn.silu(gateup[:, :local_hidden]) * gateup[:, local_hidden:]).astype(jnp.bfloat16)
    down_terms = jnp.dot(collect(activated), w_down, preferred_element_type=jnp.float32)
    result = group_collect(group_sum(down_terms, own_state).astype(jnp.bfloat16))
    outputs = (
        result.reshape(4, 4, 4, steps, local_rows, local_width)
        .transpose(3, 0, 2, 1, 4, 5)
        .reshape(steps, all_rows, local_width)
    )
    return (outputs, new_entries)


def solution(mesh):
    fine = Mesh(mesh.devices.reshape(4, 4, 4, 4, 2), ("x", "zh", "zl", "y", "core"))
    in_specs = (
        P(None, None, WIDE),
        P(WIDE),
        P(WIDE, MP),
        P(WIDE, MP, None),
        P(MP, WIDE),
        P(WIDE),
        P(WIDE, None, MP),
        P(MP, WIDE),
        P(WIDE, None, MP, None),
        P(WIDE),
        P(WIDE),
    )
    out_specs = (P(None, None, WIDE), P(None, WIDE, MP, None))
    return jax.shard_map(body, mesh=fine, in_specs=in_specs, out_specs=out_specs, check_vma=False)
```

time: 1360 us -> 228 us (0.17)
  waiting for transfers between devices: 809 us -> 32.8 us
  blocking collectives: 508 us -> 139 us
  starting transfers between devices: 0.16 us -> 41.7 us
  between operations: 14.6 us -> 1 us
    unnamed x6 -> x0, waiting for transfers between devices: 568 us -> none
    all_gather x4 -> x0, blocking collectives: 270 us -> none  [the longest x2 145 us: body(): lax.all_gather(heads, 'wide', axis=0, tiled=True)]
    psum x2 -> x0, waiting for transfers between devices: 242 us -> none  [the longest x1 129 us: body(): lax.psum(attn_terms.astype(jnp.bfloat16), 'mp').astype(jnp.float32)]
    psum x2 -> x0, blocking collectives: 239 us -> none  [the longest x1 123 us: body(): squares = lax.psum(jnp.sum(current * current, axis=-1), 'wide')]
    all_to_all x0 -> x11, blocking collectives: none -> 139 us  [exchange(): return lax.all_to_all(blocks, axis, 0, 0, tiled=True)]
    all_to_all x0 -> x5, starting transfers between devices: none -> 41.7 us  [exchange(): return lax.all_to_all(blocks, axis, 0, 0, tiled=True)]
    all_to_all x0 -> x5, waiting for transfers between devices: none -> 32.8 us  [exchange(): return lax.all_to_all(blocks, axis, 0, 0, tiled=True)]
  transfers between devices with their start and end apart: 4 -> 5, of which waited for: 4 -> 5; matrix products, arithmetic and copies ran while one was open for 0% -> 0% of each run, Pallas kernels for 0% -> 0%
where the time goes in v1:
time: 228 us; the launch traced here: 227 us
  blocking collectives  139 us (61%)
  starting transfers between devices  41.7 us (18%)
  waiting for transfers between devices  32.8 us (14%)
  local copies, waits for them, and re-layouts  6.24 us (3%)
  matrix products  3.43 us (2%)
  other arithmetic  2.9 us (1%)
    all_to_all x11, blocking collectives, exchange(): return lax.all_to_all(blocks, axis, 0, 0, tiled=True)  139 us
    all_to_all x5, starting transfers between devices, exchange(): return lax.all_to_all(blocks, axis, 0, 0, tiled=True)  41.7 us
    all_to_all x5, waiting for transfers between devices, exchange(): return lax.all_to_all(blocks, axis, 0, 0, tiled=True)  32.8 us
  transfers between devices with their start and end apart: 5, of which 5 were waited for; matrix products, arithmetic and copies ran while one was open for 0% of the time, Pallas kernels for 0%

profile of v1, /device:TPU:1, one launch (start us, length us, event | category | flops | bytes accessed | tf_op | source)
XLA Modules:
  0.0 226.6 jit_solution(15755276463478944844)
XLA Ops:
  0.6 1.1 reshape.271
  1.8 0.1 copy.42
  1.8 0.2 reshape.268
  2.0 0.2 reshape.269
  2.3 0.1 copy-done.7
  2.4 0.1 fusion.9
  2.5 0.1 copy.44
  2.6 0.1 dot_general.32
  2.7 0.4 convolution_convert_fusion.1
  3.2 0.4 copy-done.5
  3.6 0.2 convolution_convert_fusion.3
  3.8 0.1 pad_maximum_fusion
  3.9 17.0 %all_to_all.80 = bf16[4,64,2432]{2,1,0:T(8,128)(2,1)S(1)} all-to-all(bf16[4,64,2432]{2,1,0:T(8,128)(2,1)S(1)} %pad_maximum_fusion), channel_id=1, replica_groups=mesh['x'=4,'zh'=4,'zl'=4,'y'=4,'core'=2] {'x'}, dimensions={0} | all-to-all | bytes 2490368 | tf_op jit(solution)/shard_map/all_to_all | solution.py:35
  21.0 1.0 reduce_sum.120
  21.9 9.4 %all-to-all-start.1 = ((bf16[4,16,2432]{2,1,0:T(8,128)(2,1)}), bf16[4,16,2432]{2,1,0:T(8,128)(2,1)S(1)}, u32[]{:S(2)}, u32[]{:S(2)}) async-start(bf16[4,16,2432]{2,1,0:T(8,128)(2,1)} %bitcast.6), calls=%async_computation.1 | async-start | bytes 622592 | tf_op jit(solution)/shard_map/all_to_all | solution.py:35
  31.3 0.1 add_convert_fusion.3
  31.4 6.0 %all-to-all-done.1 = bf16[4,16,2432]{2,1,0:T(8,128)(2,1)S(1)} async-done(((bf16[4,16,2432]{2,1,0:T(8,128)(2,1)}), bf16[4,16,2432]{2,1,0:T(8,128)(2,1)S(1)}, u32[]{:S(2)}, u32[]{:S(2)}) %all-to-all-start.1) | async-done | bytes 311328 | tf_op jit(solution)/shard_map/all_to_all | solution.py:35
  37.4 0.7 reshape.255
  38.0 12.6 %all-to-all-start.2 = ((bf16[4,4,2432]{2,1,0:T(4,128)(2,1)}), bf16[4,4,2432]{2,1,0:T(4,128)(2,1)S(1)}, u32[]{:S(2)}, u32[]{:S(2)}) async-start(bf16[4,4,2432]{2,1,0:T(4,128)(2,1)} %reshape.255), calls=%async_computation.2 | async-start | bytes 155648 | tf_op jit(solution)/shard_map/all_to_all | solution.py:35
  50.7 0.1 iota_compare_fusion
  50.8 11.7 %all-to-all-done.2 = bf16[4,4,2432]{2,1,0:T(4,128)(2,1)S(1)} async-done(((bf16[4,4,2432]{2,1,0:T(4,128)(2,1)}), bf16[4,4,2432]{2,1,0:T(4,128)(2,1)S(1)}, u32[]{:S(2)}, u32[]{:S(2)}) %all-to-all-start.2) | async-done | bytes 77856 | tf_op jit(solution)/shard_map/all_to_all | solution.py:35
  62.5 0.1 slice_reduce_fusion.1
  62.6 0.1 slice_multiply_fusion
  62.7 0.1 fusion.26
  62.8 0.1 fusion.27
  62.9 0.1 subtract_convert_fusion.1
  63.1 0.1 pad_maximum_fusion.2
  63.2 0.3 fusion.28
  63.5 0.2 fusion.29
  63.7 0.2 fusion.8
  63.9 0.2 fusion.4
  64.2 0.2 fusion.1
  64.4 14.1 %all_to_all.81 = bf16[4,4,2048]{2,1,0:T(4,128)(2,1)S(1)} all-to-all(bf16[4,4,2048]{2,1,0:T(4,128)(2,1)S(1)} %broadcast_in_dim.57), channel_id=1, replica_groups=mesh['x'=4,'zh'=4,'zl'=4,'y'=4,'core'=2] {'zh'}, dimensions={0} | all-to-all | bytes 131072 | tf_op jit(solution)/shard_map/all_to_all | solution.py:35
  78.6 11.5 %all_to_all.82 = bf16[4,16,2048]{2,1,0:T(8,128)(2,1)S(1)} all-to-all(bf16[4,16,2048]{2,1,0:T(8,128)(2,1)S(1)} %broadcast_in_dim.59), channel_id=1, replica_groups=mesh['x'=4,'zh'=4,'zl'=4,'y'=4,'core'=2] {'zl'}, dimensions={0} | all-to-all | bytes 524288 | tf_op jit(solution)/shard_map/all_to_all | solution.py:35
  90.1 0.1 broadcast_in_dim.61
  90.2 12.3 %all_to_all.83 = bf16[4,64,2048]{2,1,0:T(8,128)(2,1)S(1)} all-to-all(bf16[4,64,2048]{2,1,0:T(8,128)(2,1)S(1)} %broadcast_in_dim.61), channel_id=1, replica_groups=mesh['x'=4,'zh'=4,'zl'=4,'y'=4,'core'=2] {'x'}, dimensions={0} | all-to-all | bytes 2097152 | tf_op jit(solution)/shard_map/all_to_all | solution.py:35
  102.5 1.1 convolution_convert_fusion.4
  103.6 11.4 %all-to-all-start.6 = ((bf16[8,32,256]{2,1,0:T(8,128)(2,1)}), bf16[8,32,256]{2,1,0:T(8,128)(2,1)S(1)}, u32[]{:S(2)}, u32[]{:S(2)}) async-start(bf16[8,32,256]{2,1,0:T(8,128)(2,1)} %bitcast.17), calls=%async_computation.6 | async-start | bytes 262144 | tf_op jit(solution)/shard_map/all_to_all | solution.py:35
  115.0 5.3 %all-to-all-done.6 = bf16[8,32,256]{2,1,0:T(8,128)(2,1)S(1)} async-done(((bf16[8,32,256]{2,1,0:T(8,128)(2,1)}), bf16[8,32,256]{2,1,0:T(8,128)(2,1)S(1)}, u32[]{:S(2)}, u32[]{:S(2)}) %all-to-all-start.6) | async-done | bytes 131104 | tf_op jit(solution)/shard_map/all_to_all | solution.py:35
  120.4 0.7 broadcast_in_dim.108
  121.0 4.1 %all-to-all-start.7 = ((bf16[8,32,256]{2,1,0:T(8,128)(2,1)}), bf16[8,32,256]{2,1,0:T(8,128)(2,1)S(1)}, u32[]{:S(2)}, u32[]{:S(2)}) async-start(bf16[8,32,256]{2,1,0:T(8,128)(2,1)} %broadcast_in_dim.108), calls=%async_computation.7 | async-start | bytes 262144 | tf_op jit(solution)/shard_map/all_to_all | solution.py:35
  125.2 5.3 %all-to-all-done.7 = bf16[8,32,256]{2,1,0:T(8,128)(2,1)S(1)} async-done(((bf16[8,32,256]{2,1,0:T(8,128)(2,1)}), bf16[8,32,256]{2,1,0:T(8,128)(2,1)S(1)}, u32[]{:S(2)}, u32[]{:S(2)}) %all-to-all-start.7) | async-done | bytes 131104 | tf_op jit(solution)/shard_map/all_to_all | solution.py:35
  130.5 0.4 convolution_convert_fusion
  131.0 0.1 pad_maximum_fusion.1
  131.1 15.2 %all_to_all.84 = bf16[4,64,1792]{2,1,0:T(8,128)(2,1)S(1)} all-to-all(bf16[4,64,1792]{2,1,0:T(8,128)(2,1)S(1)} %pad_maximum_fusion.1), channel_id=1, replica_groups=mesh['x'=4,'zh'=4,'zl'=4,'y'=4,'core'=2] {'x'}, dimensions={0} | all-to-all | bytes 1835008 | tf_op jit(solution)/shard_map/all_to_all | solution.py:35
  146.3 0.2 reduce_sum.127
  146.4 8.2 %all_to_all.85 = bf16[4,16,1792]{2,1,0:T(8,128)(2,1)S(1)} all-to-all(bf16[4,16,1792]{2,1,0:T(8,128)(2,1)S(1)} %bitcast.62), channel_id=1, replica_groups=mesh['x'=4,'zh'=4,'zl'=4,'y'=4,'core'=2] {'zl'}, dimensions={0} | all-to-all | bytes 458752 | tf_op jit(solution)/shard_map/all_to_all | solution.py:35
  154.8 14.3 %all_to_all.86 = bf16[4,4,1792]{2,1,0:T(4,128)(2,1)S(1)} all-to-all(bf16[4,4,1792]{2,1,0:T(4,128)(2,1)S(1)} %reshape.264), channel_id=1, replica_groups=mesh['x'=4,'zh'=4,'zl'=4,'y'=4,'core'=2] {'zh'}, dimensions={0} | all-to-all | bytes 114688 | tf_op jit(solution)/shard_map/all_to_all | solution.py:35
  169.1 0.1 slice_reduce_fusion
  169.2 0.1 slice_multiply_fusion.1
  169.3 0.1 fusion.17
  169.4 13.8 %all_to_all.87 = bf16[4,4,832]{2,1,0:T(4,128)(2,1)S(1)} all-to-all(bf16[4,4,832]{2,1,0:T(4,128)(2,1)S(1)} %broadcast_in_dim.109), channel_id=1, replica_groups=mesh['x'=4,'zh'=4,'zl'=4,'y'=4,'core'=2] {'zh'}, dimensions={0} | all-to-all | bytes 53248 | tf_op jit(solution)/shard_map/all_to_all | solution.py:35
  183.3 7.3 %all_to_all.88 = bf16[4,16,832]{2,1,0:T(8,128)(2,1)S(1)} all-to-all(bf16[4,16,832]{2,1,0:T(8,128)(2,1)S(1)} %broadcast_in_dim.111), channel_id=1, replica_groups=mesh['x'=4,'zh'=4,'zl'=4,'y'=4,'core'=2] {'zl'}, dimensions={0} | all-to-all | bytes 212992 | tf_op jit(solution)/shard_map/all_to_all | solution.py:35
  190.6 9.0 %all_to_all.89 = bf16[4,64,832]{2,1,0:T(8,128)(2,1)S(1)} all-to-all(bf16[4,64,832]{2,1,0:T(8,128)(2,1)S(1)} %broadcast_in_dim.113), channel_id=1, replica_groups=mesh['x'=4,'zh'=4,'zl'=4,'y'=4,'core'=2] {'x'}, dimensions={0} | all-to-all | bytes 851968 | tf_op jit(solution)/shard_map/all_to_all | solution.py:35
  199.6 0.3 convolution_convert_fusion.2
  199.9 15.8 %all_to_all.90 = bf16[8,32,256]{2,1,0:T(8,128)(2,1)S(1)} all-to-all(bf16[8,32,256]{2,1,0:T(8,128)(2,1)S(1)} %bitcast.67), channel_id=1, replica_groups=mesh['x'=4,'zh'=4,'zl'=4,'y'=4,'core'=2] {'y','core'}, dimensions={0} | all-to-all | bytes 262144 | tf_op jit(solution)/shard_map/all_to_all | solution.py:35
  215.7 0.7 broadcast_in_dim.114
  216.3 4.1 %all-to-all-start.15 = ((bf16[8,32,256]{2,1,0:T(8,128)(2,1)}), bf16[8,32,256]{2,1,0:T(8,128)(2,1)S(1)}, u32[]{:S(2)}, u32[]{:S(2)}) async-start(bf16[8,32,256]{2,1,0:T(8,128)(2,1)} %broadcast_in_dim.114), calls=%async_computation.15 | async-start | bytes 262144 | tf_op jit(solution)/shard_map/all_to_all | solution.py:35
  220.5 0.1 maximum_bitcast_fusion
  220.6 0.6 copy.54
  221.1 4.6 %all-to-all-done.15 = bf16[8,32,256]{2,1,0:T(8,128)(2,1)S(1)} async-done(((bf16[8,32,256]{2,1,0:T(8,128)(2,1)}), bf16[8,32,256]{2,1,0:T(8,128)(2,1)S(1)}, u32[]{:S(2)}, u32[]{:S(2)}) %all-to-all-start.15) | async-done | bytes 131104 | tf_op jit(solution)/shard_map/all_to_all | solution.py:35
  225.8 0.1 reshape_reshape.3
  225.8 0.1 copy.52
  225.9 0.7 copy.53
  (56 shorter events, 0.7 us)
Async XLA Ops:
  0.6 2.1 copy-start
  1.8 0.7 copy-start.7
  2.7 0.9 copy-start.5
  21.0 10.3 %copy-start.8 = (s32[2]{0:T(128)S(1)}, s32[2]{0:T(128)}, u32[]{:S(2)}) copy-start(s32[2]{0:T(128)} %param.21) | copy-start | bytes 28
  21.0 29.7 %copy-start.6 = (s32[2]{0:T(128)S(1)}, s32[2]{0:T(128)}, u32[]{:S(2)}) copy-start(s32[2]{0:T(128)} %param.20) | copy-start | bytes 28
  21.9 41.2 %copy-start.4 = (bf16[2,768,1,256]{3,1,2,0:T(8,128)(2,1)S(1)}, bf16[2,768,1,256]{3,1,2,0:T(8,128)(2,1)}, u32[]{:S(2)}) copy-start(bf16[2,768,1,256]{3,1,2,0:T(8,128)(2,1)} %param.19) | copy-start | bytes 2359300
  21.9 15.4 %all-to-all-start.1 = ((bf16[4,16,2432]{2,1,0:T(8,128)(2,1)}), bf16[4,16,2432]{2,1,0:T(8,128)(2,1)S(1)}, u32[]{:S(2)}, u32[]{:S(2)}) async-start(bf16[4,16,2432]{2,1,0:T(8,128)(2,1)} %bitcast.6), calls=%async_computation.1 | async-start | bytes 622592 | tf_op jit(solution)/shard_map/all_to_all | solution.py:35
  38.0 24.4 %all-to-all-start.2 = ((bf16[4,4,2432]{2,1,0:T(4,128)(2,1)}), bf16[4,4,2432]{2,1,0:T(4,128)(2,1)S(1)}, u32[]{:S(2)}, u32[]{:S(2)}) async-start(bf16[4,4,2432]{2,1,0:T(4,128)(2,1)} %reshape.255), calls=%async_computation.2 | async-start | bytes 155648 | tf_op jit(solution)/shard_map/all_to_all | solution.py:35
  90.2 12.3 %copy-start.1 = (bf16[2048,256]{1,0:T(8,128)(2,1)S(1)}, bf16[2048,256]{1,0:T(8,128)(2,1)}, u32[]{:S(2)}) copy-start(bf16[2048,256]{1,0:T(8,128)(2,1)} %param.15) | copy-start | bytes 3145732
  102.5 22.7 %copy-start.9 = (bf16[256]{0:T(256)(128)(2,1)S(1)}, bf16[256]{0:T(256)(128)(2,1)}, u32[]{:S(2)}) copy-start(bf16[256]{0:T(256)(128)(2,1)} %param.16) | copy-start | bytes 1540
  103.6 26.9 %copy-start.2 = (bf16[256,2,832]{0,2,1:T(8,128)(2,1)S(1)}, bf16[256,2,832]{0,2,1:T(8,128)(2,1)}, u32[]{:S(2)}) copy-start(bf16[256,2,832]{0,2,1:T(8,128)(2,1)} %param.17) | copy-start | bytes 2555908
  103.6 16.7 %all-to-all-start.6 = ((bf16[8,32,256]{2,1,0:T(8,128)(2,1)}), bf16[8,32,256]{2,1,0:T(8,128)(2,1)S(1)}, u32[]{:S(2)}, u32[]{:S(2)}) async-start(bf16[8,32,256]{2,1,0:T(8,128)(2,1)} %bitcast.17), calls=%async_computation.6 | async-start | bytes 262144 | tf_op jit(solution)/shard_map/all_to_all | solution.py:35
  121.0 9.4 %all-to-all-start.7 = ((bf16[8,32,256]{2,1,0:T(8,128)(2,1)}), bf16[8,32,256]{2,1,0:T(8,128)(2,1)S(1)}, u32[]{:S(2)}, u32[]{:S(2)}) async-start(bf16[8,32,256]{2,1,0:T(8,128)(2,1)} %broadcast_in_dim.108), calls=%async_computation.7 | async-start | bytes 262144 | tf_op jit(solution)/shard_map/all_to_all | solution.py:35
  154.7 44.8 %copy-start.3 = (bf16[832,256]{1,0:T(8,128)(2,1)S(1)}, bf16[832,256]{1,0:T(8,128)(2,1)}, u32[]{:S(2)}) copy-start(bf16[832,256]{1,0:T(8,128)(2,1)} %param.18) | copy-start | bytes 1277956
  216.3 9.4 %all-to-all-start.15 = ((bf16[8,32,256]{2,1,0:T(8,128)(2,1)}), bf16[8,32,256]{2,1,0:T(8,128)(2,1)S(1)}, u32[]{:S(2)}, u32[]{:S(2)}) async-start(bf16[8,32,256]{2,1,0:T(8,128)(2,1)} %broadcast_in_dim.114), calls=%async_computation.15 | async-start | bytes 262144 | tf_op jit(solution)/shard_map/all_to_all | solution.py:35

commit v2 on v1

--- a/solution.py
+++ b/solution.py
@@ -10,11 +10,9 @@
 rope_base = 500000.0
 masked_score = -1e30
 
-WIDE = ("x", "zh", "zl")
+WIDE = ("x", "z")
 MP = ("y", "core")
-REDUCE_ORDER = ("x", "zl", "zh")
-GATHER_ORDER = ("zh", "zl", "x")
-SIZES = {"x": 4, "zh": 4, "zl": 4, "y": 4, "core": 2}
+XS, ZS, YS, CORES = 4, 16, 4, 2
 
 
 def rotate(vectors, offsets):
@@ -35,40 +33,25 @@
     return lax.all_to_all(blocks, axis, 0, 0, tiled=True)
 
 
-def spread_sum(terms):
+def sum_over(terms, axis, size):
     rows, columns = terms.shape
-    for axis in REDUCE_ORDER:
-        size = SIZES[axis]
-        rows //= size
-        received = exchange(terms.astype(jnp.bfloat16).reshape(size, rows, columns), axis)
-        terms = jnp.sum(received.astype(jnp.float32), axis=0)
-    return terms
-
-
-def collect(block):
-    for axis in GATHER_ORDER:
-        size = SIZES[axis]
-        rows, columns = block.shape
-        copies = jnp.broadcast_to(block[None], (size, rows, columns))
-        block = exchange(copies, axis).reshape(size * rows, columns)
-    return block
-
-
-def group_sum(terms, base):
-    rows, columns = terms.shape
-    received = exchange(terms.astype(jnp.bfloat16).reshape(8, rows // 8, columns), MP)
-    return base + jnp.sum(received.astype(jnp.float32), axis=0)
-
-
-def group_collect(block):
-    rows, columns = block.shape
-    copies = jnp.broadcast_to(block[None], (8, rows, columns))
-    return exchange(copies, MP).reshape(8 * rows, columns)
+    received = exchange(terms.astype(jnp.bfloat16).reshape(size, rows // size, columns), axis)
+    return jnp.sum(received.astype(jnp.float32), axis=0)
+
+
+def collect(block, axis, size):
+    return exchange(jnp.broadcast_to(block[None], (size,) + block.shape), axis)
+
+
+def wide_dot(rows, weights):
+    return jnp.concatenate(
+        [jnp.dot(rows, weights[at], preferred_element_type=jnp.float32) for at in range(XS)], axis=1
+    )
 
 
 def lane_squares(values):
     squares = values * values
-    return squares[:, :128] + squares[:, 128:]
+    return sum(squares[:, at : at + 128] for at in range(0, values.shape[1], 128))
 
 
 def attend(queries, kv_cache, lengths, fresh_keys, fresh_values, score_scale):
@@ -124,9 +107,17 @@
     keyvals_at = local_queries * head_dim
     squares_at = keyvals_at + 2 * head_dim
 
+    with jax.named_scope("gather_weights"):
+        gains = jnp.broadcast_to(ffn_gain[None], (16, local_width))
+        lines = jnp.concatenate([inputs.reshape(steps * all_rows, local_width), gains], axis=0)
+        lines = lax.all_gather(lines, "x", axis=0, tiled=False)
+        out_weights = lax.all_gather(w_out, "x", axis=0, tiled=False)
+        gateup_weights = lax.all_gather(gateup_weight, "x", axis=0, tiled=True)
+        down_weights = lax.all_gather(w_down, "x", axis=0, tiled=False)
+
     current = (
-        inputs.reshape(steps, 4, 4, 4, local_rows, local_width)
-        .transpose(1, 3, 2, 0, 4, 5)
+        inputs.reshape(steps, XS * ZS, local_rows, local_width)
+        .transpose(1, 0, 2, 3)
         .reshape(steps * all_rows, local_width)
         .astype(jnp.float32)
     )
@@ -139,7 +130,7 @@
         ],
         axis=1,
     )
-    sums = spread_sum(terms)
+    sums = sum_over(sum_over(terms, "x", XS), "z", ZS)
     mean = jnp.sum(sums[:, squares_at:], axis=-1, keepdims=True) / D
     sums = (sums[:, :squares_at] * lax.rsqrt(mean + epsilon)).reshape(steps, local_rows, squares_at)
     offsets = positions[None, :] + jnp.arange(steps)[:, None]
@@ -159,35 +150,52 @@
     )
     heads = mixed.astype(jnp.bfloat16).transpose(1, 0, 2, 3).reshape(steps * local_rows, keyvals_at)
 
-    attn_terms = jnp.dot(collect(heads), w_out, preferred_element_type=jnp.float32)
-    own = lax.axis_index(MP) * (steps * all_rows // 8)
-    residual = lax.dynamic_slice_in_dim(current, own, steps * all_rows // 8, axis=0)
-    own_state = group_sum(attn_terms, residual)
-    hidden_state = group_collect(own_state.astype(jnp.bfloat16)).astype(jnp.float32)
-    ffn_in = (hidden_state * ffn_gain.astype(jnp.float32)).astype(jnp.bfloat16)
+    x_rows = steps * all_rows // XS
+    half = x_rows // CORES
+    width = XS * local_width
+    residual = (
+        lax.dynamic_index_in_dim(
+            lines[:, : steps * all_rows].reshape(XS, steps, XS, CORES, half // (steps * local_rows), local_rows, local_width),
+            lax.axis_index("x"), 2, keepdims=False,
+        )
+    )
+    residual = lax.dynamic_index_in_dim(residual, lax.axis_index("core"), 2, keepdims=False)
+    residual = residual.transpose(2, 1, 3, 0, 4).reshape(half, width).astype(jnp.float32)
+    gain = lines[:, steps * all_rows].reshape(1, width).astype(jnp.float32)
+
+    attn_terms = wide_dot(collect(heads, "z", ZS).reshape(x_rows, keyvals_at), out_weights)
+    pair_terms = sum_over(attn_terms, "core", CORES).astype(jnp.bfloat16)
+    own_state = residual + jnp.sum(collect(pair_terms, "y", YS).astype(jnp.float32), axis=0)
+    hidden_state = lax.all_gather(own_state.astype(jnp.bfloat16), "core", axis=0, tiled=True).astype(jnp.float32)
+    ffn_in = (hidden_state * gain).astype(jnp.bfloat16)
     gateup_terms = jnp.concatenate(
         [
-            jnp.dot(ffn_in, gateup_weight, preferred_element_type=jnp.float32),
+            jnp.dot(ffn_in, gateup_weights, preferred_element_type=jnp.float32),
             lane_squares(hidden_state),
         ],
         axis=1,
     )
-    gateup = spread_sum(gateup_terms)
+    gateup = sum_over(gateup_terms, "z", ZS)
     mean = jnp.sum(gateup[:, 2 * local_hidden :], axis=-1, keepdims=True) / D
     gateup = gateup[:, : 2 * local_hidden] * lax.rsqrt(mean + epsilon)
     activated = (jax.nn.silu(gateup[:, :local_hidden]) * gateup[:, local_hidden:]).astype(jnp.bfloat16)
-    down_terms = jnp.dot(collect(activated), w_down, preferred_element_type=jnp.float32)
-    result = group_collect(group_sum(down_terms, own_state).astype(jnp.bfloat16))
+    down_terms = wide_dot(collect(activated, "z", ZS).reshape(x_rows, local_hidden), down_weights)
+    pair_terms = (sum_over(down_terms, "core", CORES) + own_state * (1.0 / YS)).astype(jnp.bfloat16)
+    blocks = pair_terms.reshape(half, XS, local_width).transpose(1, 0, 2)
+    blocks = jnp.broadcast_to(blocks[:, None], (XS, YS, half, local_width))
+    received = exchange(blocks.reshape(XS * YS, half, local_width), ("x", "y"))
+    result = jnp.sum(received.reshape(XS, YS, half, local_width).astype(jnp.float32), axis=1)
+    result = lax.all_gather(result.astype(jnp.bfloat16), "core", axis=0, tiled=False)
     outputs = (
-        result.reshape(4, 4, 4, steps, local_rows, local_width)
-        .transpose(3, 0, 2, 1, 4, 5)
+        result.reshape(CORES, XS, half // (steps * local_rows), steps, local_rows, local_width)
+        .transpose(3, 1, 0, 2, 4, 5)
         .reshape(steps, all_rows, local_width)
     )
     return (outputs, new_entries)
 
 
 def solution(mesh):
-    fine = Mesh(mesh.devices.reshape(4, 4, 4, 4, 2), ("x", "zh", "zl", "y", "core"))
+    fine = Mesh(mesh.devices.reshape(XS, ZS, YS, CORES), ("x", "z", "y", "core"))
     in_specs = (
         P(None, None, WIDE),
         P(WIDE),

time: 228 us -> 214 us (0.939)
  blocking collectives: 139 us -> 59.6 us
  waiting for transfers between devices: 32.8 us -> 55.6 us
  starting transfers between devices: 41.7 us -> 56.5 us
  between operations: 1 us -> 14.3 us
  matrix products: 3.43 us -> 15.8 us
    all_to_all x11 -> x3, blocking collectives: 139 us -> 41.7 us  [exchange(): return lax.all_to_all(blocks, axis, 0, 0, tiled=True)]
    all_gather x0 -> x3, blocking collectives: none -> 17.9 us  [the longest x1 11.1 us: body(): lines = lax.all_gather(lines, 'x', axis=0, tiled=False)]
    all_to_all x5 -> x6, waiting for transfers between devices: 32.8 us -> 48.7 us  [exchange(): return lax.all_to_all(blocks, axis, 0, 0, tiled=True)]
    all_to_all x5 -> x6, starting transfers between devices: 41.7 us -> 56.4 us  [exchange(): return lax.all_to_all(blocks, axis, 0, 0, tiled=True)]
    dot_general x3 -> x9, matrix products: 1.84 us -> 14.2 us  [the longest x8 11.1 us: wide_dot(): jnp.dot(rows, weights[at], preferred_element_type=jnp.float32)]
    all_gather x0 -> x3, waiting for transfers between devices: none -> 4.83 us  [the longest x1 4.79 us: body(): gateup_weights = lax.all_gather(gateup_weight, 'x', axis=0, tiled=True)]
  transfers between devices with their start and end apart: 5 -> 9, of which waited for: 5 -> 7; matrix products, arithmetic and copies ran while one was open for 0% -> 10% of each run, Pallas kernels for 0% -> 0%
where the time goes in v2:
time: 214 us; the launch traced here: 213 us
  blocking collectives  59.6 us (28%)
  starting transfers between devices  56.5 us (26%)
  waiting for transfers between devices  55.6 us (26%)
  matrix products  15.8 us (7%)
  between operations  14.3 us (7%)
  local copies, waits for them, and re-layouts  8.06 us (4%)
  other arithmetic  3.42 us (2%)
    all_to_all x6, starting transfers between devices, exchange(): return lax.all_to_all(blocks, axis, 0, 0, tiled=True)  56.4 us
    all_to_all x6, waiting for transfers between devices, exchange(): return lax.all_to_all(blocks, axis, 0, 0, tiled=True)  48.7 us
    all_to_all x3, blocking collectives, exchange(): return lax.all_to_all(blocks, axis, 0, 0, tiled=True)  41.7 us
    all_gather x1, blocking collectives, body(): lines = lax.all_gather(lines, 'x', axis=0, tiled=False)  11.1 us
    dot_general x8, matrix products, wide_dot(): jnp.dot(rows, weights[at], preferred_element_type=jnp.float32)  11.1 us
    all_gather x1, waiting for transfers between devices, body(): gateup_weights = lax.all_gather(gateup_weight, 'x', axis=0, tiled=True)  4.79 us
  transfers between devices with their start and end apart: 9, of which 7 were waited for; matrix products, arithmetic and copies ran while one was open for 10% of the time, Pallas kernels for 0%

profile of v2, /device:TPU:1, one launch (start us, length us, event | category | flops | bytes accessed | tf_op | source)
XLA Modules:
  0.0 213.3 jit_solution(8218137805308990580)
XLA Ops:
  7.2 0.7 all-gather.10.cloned.1.call-update
  7.9 1.1 reshape.304
  9.1 0.2 reshape.299
  9.3 0.1 fusion.9
  9.4 0.1 copy.124
  9.6 0.1 mul.157
  9.8 0.2 mul.159
  10.0 0.2 convolution_convert_fusion.2
  10.2 0.5 convolution_convert_fusion
  10.7 1.2 pad_maximum_fusion
  11.9 5.0 %all-to-all-start = ((bf16[4,64,2432]{2,1,0:T(8,128)(2,1)}), bf16[4,64,2432]{2,1,0:T(8,128)(2,1)S(1)}, u32[]{:S(2)}, u32[]{:S(2)}) async-start(bf16[4,64,2432]{2,1,0:T(8,128)(2,1)} %pad_maximum_fusion), calls=%async_computation | async-start | bytes 2490368 | tf_op jit(solution)/shard_map/all_to_all | solution.py:33
  16.9 0.7 all-gather.8.cloned.1.call-update
  17.7 10.7 %all-to-all-done = bf16[4,64,2432]{2,1,0:T(8,128)(2,1)S(1)} async-done(((bf16[4,64,2432]{2,1,0:T(8,128)(2,1)}), bf16[4,64,2432]{2,1,0:T(8,128)(2,1)S(1)}, u32[]{:S(2)}, u32[]{:S(2)}) %all-to-all-start) | async-done | bytes 1245216 | tf_op jit(solution)/shard_map/all_to_all | solution.py:33
  28.3 0.2 reduce_sum.112
  28.5 0.8 reshape.288
  29.3 19.9 %all-to-all-start.1 = ((bf16[16,4,2432]{2,1,0:T(4,128)(2,1)}), bf16[16,4,2432]{2,1,0:T(4,128)(2,1)S(1)}, u32[]{:S(2)}, u32[]{:S(2)}) async-start(bf16[16,4,2432]{2,1,0:T(4,128)(2,1)} %reshape.288), calls=%async_computation.1 | async-start | bytes 622592 | tf_op jit(solution)/shard_map/all_to_all | solution.py:33
  49.5 13.2 %all-to-all-done.1 = bf16[16,4,2432]{2,1,0:T(4,128)(2,1)S(1)} async-done(((bf16[16,4,2432]{2,1,0:T(4,128)(2,1)}), bf16[16,4,2432]{2,1,0:T(4,128)(2,1)S(1)}, u32[]{:S(2)}, u32[]{:S(2)}) %all-to-all-start.1) | async-done | bytes 311328 | tf_op jit(solution)/shard_map/all_to_all | solution.py:33
  62.6 0.1 convert_reduce_fusion
  62.8 0.1 slice_reduce_fusion.1
  63.1 0.1 subtract_convert_fusion.1
  63.4 0.1 pad_maximum_fusion.5
  63.4 0.2 fusion.33
  63.7 0.3 fusion.32
  64.0 0.2 fusion.8
  64.2 0.2 fusion.4
  64.5 0.2 fusion.1
  64.7 0.8 broadcast_in_dim.44
  65.5 12.1 %all-to-all-start.2 = ((bf16[16,4,2048]{2,1,0:T(4,128)(2,1)}), bf16[16,4,2048]{2,1,0:T(4,128)(2,1)S(1)}, u32[]{:S(2)}, u32[]{:S(2)}) async-start(bf16[16,4,2048]{2,1,0:T(4,128)(2,1)} %broadcast_in_dim.44), calls=%async_computation.2 | async-start | bytes 524288 | tf_op jit(solution)/shard_map/all_to_all | solution.py:33
  77.7 0.7 all-gather.12.cloned.1.call-update
  78.4 11.1 %all-gather = bf16[1088,256]{1,0:T(8,128)(2,1)S(1)} all-gather(bf16[272,256]{1,0:T(8,128)(2,1)S(1)} %pad_maximum_fusion.2), channel_id=2, replica_groups=mesh['x'=4,'z'=16,'y'=4,'core'=2] {'x'}, dimensions={0}, use_global_device_ids=true | all-gather | bytes 696320 | tf_op jit(solution)/shard_map/gather_weights/all_gather | solution.py:113
  89.6 0.4 copy.121
  90.1 0.3 all-to-all-done.2
  90.5 1.6 convolution_convert_fusion.3
  92.1 1.5 convolution_convert_fusion.4
  93.7 1.5 convolution_convert_fusion.5
  95.2 1.5 convolution_convert_fusion.6
  96.8 10.1 %all_to_all.45 = bf16[2,32,1024]{2,1,0:T(8,128)(2,1)S(1)} all-to-all(bf16[2,32,1024]{2,1,0:T(8,128)(2,1)S(1)} %pad_maximum_fusion.3), channel_id=1, replica_groups=mesh['x'=4,'z'=16,'y'=4,'core'=2] {'core'}, dimensions={0} | all-to-all | bytes 262144 | tf_op jit(solution)/shard_map/all_to_all | solution.py:33
  107.0 0.7 broadcast_in_dim.45
  107.7 4.4 %all-to-all-start.4 = ((bf16[4,32,1024]{2,1,0:T(8,128)(2,1)}), bf16[4,32,1024]{2,1,0:T(8,128)(2,1)S(1)}, u32[]{:S(2)}, u32[]{:S(2)}) async-start(bf16[4,32,1024]{2,1,0:T(8,128)(2,1)} %broadcast_in_dim.45), calls=%async_computation.4 | async-start | bytes 524288 | tf_op jit(solution)/shard_map/all_to_all | solution.py:33
  112.1 5.8 %all-to-all-done.4 = bf16[4,32,1024]{2,1,0:T(8,128)(2,1)S(1)} async-done(((bf16[4,32,1024]{2,1,0:T(8,128)(2,1)}), bf16[4,32,1024]{2,1,0:T(8,128)(2,1)S(1)}, u32[]{:S(2)}, u32[]{:S(2)}) %all-to-all-start.4) | async-done | bytes 262176 | tf_op jit(solution)/shard_map/all_to_all | solution.py:33
  117.9 3.3 %all_gather.34 = bf16[64,1024]{1,0:T(8,128)(2,1)S(1)} all-gather(bf16[32,1024]{1,0:T(8,128)(2,1)S(1)} %add_convert_fusion), channel_id=1, replica_groups=mesh['x'=4,'z'=16,'y'=4,'core'=2] {'core'}, dimensions={0}, use_global_device_ids=true | all-gather | bytes 196608 | tf_op jit(solution)/shard_map/all_gather | solution.py:169
  121.3 4.8 %all-gather.8.cloned.1.call-done = bf16[1024,1664]{0,1:T(8,128)(2,1)} async-done(((bf16[256,1664]{0,1:T(8,128)(2,1)}), bf16[1024,1664]{0,1:T(8,128)(2,1)}) %all-gather.8.cloned.1.call-update) | async-done | bytes 3407888 | tf_op jit(solution)/shard_map/gather_weights/all_gather | solution.py:115
  126.1 3.1 %convolution_convert_fusion.1 = bf16[64,1664]{1,0:T(8,128)(2,1)S(1)} fusion(bf16[1024,1664]{0,1:T(8,128)(2,1)} %all-gather.8.cloned.1.call-done, bf16[64,1024]{1,0:T(8,128)(2,1)S(1)} %all_gather.34, f32[1024]{0:T(1024)S(1)} %bitcast.118), kind=kOutput, calls=%fused_computation.1 | convolution fusion | flops 218406912 | bytes 3756032 | tf_op jit(solution)/shard_map/dot_general | solution.py:173
  129.3 0.1 pad_maximum_fusion.1
  129.4 24.4 %all_to_all.46 = bf16[16,4,1792]{2,1,0:T(4,128)(2,1)S(1)} all-to-all(bf16[16,4,1792]{2,1,0:T(4,128)(2,1)S(1)} %pad_maximum_fusion.1), channel_id=1, replica_groups=mesh['x'=4,'z'=16,'y'=4,'core'=2] {'z'}, dimensions={0} | all-to-all | bytes 458752 | tf_op jit(solution)/shard_map/all_to_all | solution.py:33
  153.8 0.1 convert_reduce_fusion.2
  153.9 0.1 slice_reduce_fusion
  154.1 0.1 fusion.22
  154.2 0.7 broadcast_in_dim.46
  154.9 8.8 %all-to-all-start.6 = ((bf16[16,4,832]{2,1,0:T(4,128)(2,1)}), bf16[16,4,832]{2,1,0:T(4,128)(2,1)S(1)}, u32[]{:S(2)}, u32[]{:S(2)}) async-start(bf16[16,4,832]{2,1,0:T(4,128)(2,1)} %broadcast_in_dim.46), calls=%async_computation.6 | async-start | bytes 229376 | tf_op jit(solution)/shard_map/all_to_all | solution.py:33
  163.8 11.8 %all-to-all-done.6 = bf16[16,4,832]{2,1,0:T(4,128)(2,1)S(1)} async-done(((bf16[16,4,832]{2,1,0:T(4,128)(2,1)}), bf16[16,4,832]{2,1,0:T(4,128)(2,1)S(1)}, u32[]{:S(2)}, u32[]{:S(2)}) %all-to-all-start.6) | async-done | bytes 106528 | tf_op jit(solution)/shard_map/all_to_all | solution.py:33
  175.7 1.2 convolution_convert_fusion.10
  176.9 1.2 convolution_convert_fusion.7
  178.1 1.2 convolution_convert_fusion.8
  179.3 1.2 convolution_convert_fusion.9
  180.6 7.2 %all_to_all.47 = bf16[2,32,1024]{2,1,0:T(8,128)(2,1)S(1)} all-to-all(bf16[2,32,1024]{2,1,0:T(8,128)(2,1)S(1)} %pad_maximum_fusion.4), channel_id=1, replica_groups=mesh['x'=4,'z'=16,'y'=4,'core'=2] {'core'}, dimensions={0} | all-to-all | bytes 262144 | tf_op jit(solution)/shard_map/all_to_all | solution.py:33
  187.9 0.7 broadcast_in_dim.47
  188.6 6.3 %all-to-all-start.8 = ((bf16[16,32,256]{2,1,0:T(8,128)(2,1)}), bf16[16,32,256]{2,1,0:T(8,128)(2,1)S(1)}, u32[]{:S(2)}, u32[]{:S(2)}) async-start(bf16[16,32,256]{2,1,0:T(8,128)(2,1)} %bitcast.34), calls=%async_computation.8 | async-start | bytes 524288 | tf_op jit(solution)/shard_map/all_to_all | solution.py:33
  194.9 0.1 maximum_bitcast_fusion
  195.0 0.6 copy.137
  195.6 6.9 %all-to-all-done.8 = bf16[16,32,256]{2,1,0:T(8,128)(2,1)S(1)} async-done(((bf16[16,32,256]{2,1,0:T(8,128)(2,1)}), bf16[16,32,256]{2,1,0:T(8,128)(2,1)S(1)}, u32[]{:S(2)}, u32[]{:S(2)}) %all-to-all-start.8) | async-done | bytes 262176 | tf_op jit(solution)/shard_map/all_to_all | solution.py:33
  202.5 3.4 %all-gather.3 = bf16[8,32,256]{2,1,0:T(8,128)(2,1)S(1)} all-gather(bf16[4,32,256]{2,1,0:T(8,128)(2,1)S(1)} %bitcast_reduce_fusion), channel_id=5, replica_groups=mesh['x'=4,'z'=16,'y'=4,'core'=2] {'core'}, dimensions={0}, use_global_device_ids=true | all-gather | bytes 196608 | tf_op jit(solution)/shard_map/all_gather | solution.py:188
  206.0 0.1 copy.135
  206.1 0.7 copy.136
  (73 shorter events, 1.7 us)
Async XLA Ops:
  7.2 3.1 %copy-start = (bf16[256,2048]{1,0:T(8,128)(2,1)S(1)}, bf16[256,2048]{1,0:T(8,128)(2,1)}, u32[]{:S(2)}) copy-start(bf16[256,2048]{1,0:T(8,128)(2,1)} %param.13) | copy-start | bytes 3145732
  7.2 2.4 %copy-start.1 = (bf16[2,128,256]{2,1,0:T(8,128)(2,1)S(1)}, bf16[2,128,256]{2,1,0:T(8,128)(2,1)}, u32[]{:S(2)}) copy-start(bf16[2,128,256]{2,1,0:T(8,128)(2,1)} %param.11) | copy-start | bytes 393220
  7.2 2.1 copy-start.6
  7.2 83.3 %all-gather.10.cloned.1.call-start = ((), (), s32[]{:S(2)}) async-start(), calls=%async_computation.10 | async-start | bytes 5242880 | tf_op jit(solution)/shard_map/gather_weights/all_gather | solution.py:114
  7.9 2.1 copy-start.3
  11.9 37.4 %copy-start.7 = (s32[2]{0:T(128)S(1)}, s32[2]{0:T(128)}, u32[]{:S(2)}) copy-start(s32[2]{0:T(128)} %param.21) | copy-start | bytes 28
  11.9 37.5 %copy-start.4 = (s32[2]{0:T(128)S(1)}, s32[2]{0:T(128)}, u32[]{:S(2)}) copy-start(s32[2]{0:T(128)} %param.20) | copy-start | bytes 28
  11.9 16.4 %all-to-all-start = ((bf16[4,64,2432]{2,1,0:T(8,128)(2,1)}), bf16[4,64,2432]{2,1,0:T(8,128)(2,1)S(1)}, u32[]{:S(2)}, u32[]{:S(2)}) async-start(bf16[4,64,2432]{2,1,0:T(8,128)(2,1)} %pad_maximum_fusion), calls=%async_computation | async-start | bytes 2490368 | tf_op jit(solution)/shard_map/all_to_all | solution.py:33
  16.9 46.7 %copy-start.2 = (bf16[2,768,1,256]{3,1,2,0:T(8,128)(2,1)S(1)}, bf16[2,768,1,256]{3,1,2,0:T(8,128)(2,1)}, u32[]{:S(2)}) copy-start(bf16[2,768,1,256]{3,1,2,0:T(8,128)(2,1)} %param.19) | copy-start | bytes 2359300
  16.9 109.2 %all-gather.8.cloned.1.call-start = ((), (), s32[]{:S(2)}) async-start(), calls=%async_computation.9 | async-start | bytes 4259840 | tf_op jit(solution)/shard_map/gather_weights/all_gather | solution.py:115
  29.3 49.1 %copy-start.5 = (bf16[256]{0:T(256)(128)(2,1)S(1)}, bf16[256]{0:T(256)(128)(2,1)}, u32[]{:S(2)}) copy-start(bf16[256]{0:T(256)(128)(2,1)} %param.16) | copy-start | bytes 1540
  29.3 33.3 %all-to-all-start.1 = ((bf16[16,4,2432]{2,1,0:T(4,128)(2,1)}), bf16[16,4,2432]{2,1,0:T(4,128)(2,1)S(1)}, u32[]{:S(2)}, u32[]{:S(2)}) async-start(bf16[16,4,2432]{2,1,0:T(4,128)(2,1)} %reshape.288), calls=%async_computation.1 | async-start | bytes 622592 | tf_op jit(solution)/shard_map/all_to_all | solution.py:33
  65.5 24.9 %all-to-all-start.2 = ((bf16[16,4,2048]{2,1,0:T(4,128)(2,1)}), bf16[16,4,2048]{2,1,0:T(4,128)(2,1)S(1)}, u32[]{:S(2)}, u32[]{:S(2)}) async-start(bf16[16,4,2048]{2,1,0:T(4,128)(2,1)} %broadcast_in_dim.44), calls=%async_computation.2 | async-start | bytes 524288 | tf_op jit(solution)/shard_map/all_to_all | solution.py:33
  77.7 98.0 %all-gather.12.cloned.1.call-start = ((), (), s32[]{:S(2)}) async-start(), calls=%async_computation.11 | async-start | bytes 2129920 | tf_op jit(solution)/shard_map/gather_weights/all_gather | solution.py:116
  107.7 10.2 %all-to-all-start.4 = ((bf16[4,32,1024]{2,1,0:T(8,128)(2,1)}), bf16[4,32,1024]{2,1,0:T(8,128)(2,1)S(1)}, u32[]{:S(2)}, u32[]{:S(2)}) async-start(bf16[4,32,1024]{2,1,0:T(8,128)(2,1)} %broadcast_in_dim.45), calls=%async_computation.4 | async-start | bytes 524288 | tf_op jit(solution)/shard_map/all_to_all | solution.py:33
  154.9 20.7 %all-to-all-start.6 = ((bf16[16,4,832]{2,1,0:T(4,128)(2,1)}), bf16[16,4,832]{2,1,0:T(4,128)(2,1)S(1)}, u32[]{:S(2)}, u32[]{:S(2)}) async-start(bf16[16,4,832]{2,1,0:T(4,128)(2,1)} %broadcast_in_dim.46), calls=%async_computation.6 | async-start | bytes 229376 | tf_op jit(solution)/shard_map/all_to_all | solution.py:33
  188.6 13.8 %all-to-all-start.8 = ((bf16[16,32,256]{2,1,0:T(8,128)(2,1)}), bf16[16,32,256]{2,1,0:T(8,128)(2,1)S(1)}, u32[]{:S(2)}, u32[]{:S(2)}) async-start(bf16[16,32,256]{2,1,0:T(8,128)(2,1)} %bitcast.34), calls=%async_computation.8 | async-start | bytes 524288 | tf_op jit(solution)/shard_map/all_to_all | solution.py:33
Sparse Core Ops, SparseCore 0:
  10.1 61.2 all-gather.9
  73.5 52.5 all-gather.7
  128.2 37.1 all-gather.11

commit v3 on v2

--- a/solution.py
+++ b/solution.py
@@ -43,15 +43,41 @@
     return exchange(jnp.broadcast_to(block[None], (size,) + block.shape), axis)
 
 
-def wide_dot(rows, weights):
-    return jnp.concatenate(
-        [jnp.dot(rows, weights[at], preferred_element_type=jnp.float32) for at in range(XS)], axis=1
-    )
-
-
-def lane_squares(values):
+def shift(block, by):
+    return lax.ppermute(block, "x", [(at, (at + by) % XS) for at in range(XS)])
+
+
+def both_ways(block):
+    return shift(block, -1), shift(block, 1)
+
+
+def far_block(after, before):
+    return shift(before[0], 1), shift(after[1], -1)
+
+
+def core_sum(terms):
+    received = exchange(terms.astype(jnp.bfloat16).transpose(1, 0, 2, 3), "core")
+    return jnp.sum(received.astype(jnp.float32), axis=0)
+
+
+def across(blocks):
+    shape = blocks.shape
+    copies = jnp.broadcast_to(blocks.astype(jnp.bfloat16)[:, None], (XS, YS) + shape[1:])
+    received = exchange(copies.reshape((XS * YS,) + shape[1:]), ("x", "y"))
+    return jnp.sum(received.reshape((XS, YS) + shape[1:]).astype(jnp.float32), axis=1)
+
+
+def turn(blocks, by):
+    return lax.dynamic_slice_in_dim(jnp.concatenate([blocks, blocks], axis=0), by, XS, axis=0)
+
+
+def together(*values):
+    return lax.optimization_barrier(values)
+
+
+def lane_squares(values, lanes):
     squares = values * values
-    return sum(squares[:, at : at + 128] for at in range(0, values.shape[1], 128))
+    return sum(squares[:, at : at + lanes] for at in range(0, values.shape[1], lanes))
 
 
 def attend(queries, kv_cache, lengths, fresh_keys, fresh_values, score_scale):
@@ -103,22 +129,18 @@
     local_hidden = w_down.shape[0]
     score_scale = head_dim ** (-0.5)
     keyval_weight = w_keyval.reshape(local_width, 2 * head_dim)
-    gateup_weight = w_gateup.reshape(local_width, 2 * local_hidden)
     keyvals_at = local_queries * head_dim
     squares_at = keyvals_at + 2 * head_dim
-
-    with jax.named_scope("gather_weights"):
-        gains = jnp.broadcast_to(ffn_gain[None], (16, local_width))
-        lines = jnp.concatenate([inputs.reshape(steps * all_rows, local_width), gains], axis=0)
-        lines = lax.all_gather(lines, "x", axis=0, tiled=False)
-        out_weights = lax.all_gather(w_out, "x", axis=0, tiled=False)
-        gateup_weights = lax.all_gather(gateup_weight, "x", axis=0, tiled=True)
-        down_weights = lax.all_gather(w_down, "x", axis=0, tiled=False)
+    rows = steps * all_rows
+    x_rows = rows // XS
+    half = x_rows // CORES
+    gateup = w_gateup.transpose(1, 2, 0).astype(jnp.float32) * ffn_gain.astype(jnp.float32)
+    gateup = gateup.astype(jnp.bfloat16)
 
     current = (
-        inputs.reshape(steps, XS * ZS, local_rows, local_width)
+        inputs.reshape(steps, XS, all_rows // XS, local_width)
         .transpose(1, 0, 2, 3)
-        .reshape(steps * all_rows, local_width)
+        .reshape(rows, local_width)
         .astype(jnp.float32)
     )
     scaled = (current * attn_gain.astype(jnp.float32)).astype(jnp.bfloat16)
@@ -126,11 +148,19 @@
         [
             jnp.dot(scaled, w_query, preferred_element_type=jnp.float32),
             jnp.dot(scaled, keyval_weight, preferred_element_type=jnp.float32),
-            lane_squares(current),
+            lane_squares(current, 128),
         ],
         axis=1,
     )
-    sums = sum_over(sum_over(terms, "x", XS), "z", ZS)
+    sums = sum_over(terms, "x", XS).astype(jnp.bfloat16)
+    sums, gateup = together(sums, gateup)
+    gateup_after, gateup_before = both_ways(gateup)
+    sums = sums.reshape(steps, ZS, local_rows, -1).transpose(1, 0, 2, 3).reshape(x_rows, -1)
+    sums = sum_over(sums, "z", ZS)
+    sums, gateup_after, gateup_before, w_down = together(sums, gateup_after, gateup_before, w_down)
+    gateup_far = far_block(gateup_after, gateup_before)
+    down = w_down.reshape(2, local_hidden // 2, local_width)
+    down_after, down_before = both_ways(down)
     mean = jnp.sum(sums[:, squares_at:], axis=-1, keepdims=True) / D
     sums = (sums[:, :squares_at] * lax.rsqrt(mean + epsilon)).reshape(steps, local_rows, squares_at)
     offsets = positions[None, :] + jnp.arange(steps)[:, None]
@@ -150,41 +180,60 @@
     )
     heads = mixed.astype(jnp.bfloat16).transpose(1, 0, 2, 3).reshape(steps * local_rows, keyvals_at)
 
-    x_rows = steps * all_rows // XS
-    half = x_rows // CORES
-    width = XS * local_width
-    residual = (
-        lax.dynamic_index_in_dim(
-            lines[:, : steps * all_rows].reshape(XS, steps, XS, CORES, half // (steps * local_rows), local_rows, local_width),
-            lax.axis_index("x"), 2, keepdims=False,
+    all_heads = collect(collect(heads, "z", ZS).reshape(x_rows, keyvals_at), "x", XS)
+    all_heads, gateup_far, down_after, down_before = together(
+        all_heads, gateup_far, down_after, down_before
+    )
+    attn_terms = jnp.dot(
+        all_heads.reshape(rows, keyvals_at), w_out, preferred_element_type=jnp.float32
+    ).reshape(XS, CORES, half, local_width)
+    residual = lax.dynamic_index_in_dim(
+        inputs.reshape(steps, XS, CORES, ZS // CORES, local_rows, local_width),
+        lax.axis_index("core"), 2, keepdims=False,
+    )
+    residual = residual.transpose(1, 2, 0, 3, 4).reshape(XS, half, local_width).astype(jnp.float32)
+    state = across(core_sum(attn_terms) + residual * (1.0 / YS))
+    state = turn(state, lax.axis_index("x"))
+    ffn_in = lax.all_gather(state.astype(jnp.bfloat16), "core", axis=0, tiled=False)
+    ffn_in, w_down = together(ffn_in, w_down)
+    ffn_in = ffn_in.transpose(1, 0, 2, 3).reshape(XS, x_rows, local_width)
+    squares = ffn_in.astype(jnp.float32)
+    squares = jnp.sum(squares * squares, axis=0)
+    halves = []
+    for part in range(2):
+        pieces = (gateup[part], gateup_after[part], gateup_far[part], gateup_before[part])
+        halves.append(
+            sum(
+                lax.dot_general(
+                    ffn_in[at], piece, (((1,), (1,)), ((), ())), preferred_element_type=jnp.float32
+                )
+                for at, piece in enumerate(pieces)
+            )
         )
-    )
-    residual = lax.dynamic_index_in_dim(residual, lax.axis_index("core"), 2, keepdims=False)
-    residual = residual.transpose(2, 1, 3, 0, 4).reshape(half, width).astype(jnp.float32)
-    gain = lines[:, steps * all_rows].reshape(1, width).astype(jnp.float32)
-
-    attn_terms = wide_dot(collect(heads, "z", ZS).reshape(x_rows, keyvals_at), out_weights)
-    pair_terms = sum_over(attn_terms, "core", CORES).astype(jnp.bfloat16)
-    own_state = residual + jnp.sum(collect(pair_terms, "y", YS).astype(jnp.float32), axis=0)
-    hidden_state = lax.all_gather(own_state.astype(jnp.bfloat16), "core", axis=0, tiled=True).astype(jnp.float32)
-    ffn_in = (hidden_state * gain).astype(jnp.bfloat16)
-    gateup_terms = jnp.concatenate(
-        [
-            jnp.dot(ffn_in, gateup_weights, preferred_element_type=jnp.float32),
-            lane_squares(hidden_state),
-        ],
-        axis=1,
-    )
-    gateup = sum_over(gateup_terms, "z", ZS)
-    mean = jnp.sum(gateup[:, 2 * local_hidden :], axis=-1, keepdims=True) / D
-    gateup = gateup[:, : 2 * local_hidden] * lax.rsqrt(mean + epsilon)
-    activated = (jax.nn.silu(gateup[:, :local_hidden]) * gateup[:, local_hidden:]).astype(jnp.bfloat16)
-    down_terms = wide_dot(collect(activated, "z", ZS).reshape(x_rows, local_hidden), down_weights)
-    pair_terms = (sum_over(down_terms, "core", CORES) + own_state * (1.0 / YS)).astype(jnp.bfloat16)
-    blocks = pair_terms.reshape(half, XS, local_width).transpose(1, 0, 2)
-    blocks = jnp.broadcast_to(blocks[:, None], (XS, YS, half, local_width))
-    received = exchange(blocks.reshape(XS * YS, half, local_width), ("x", "y"))
-    result = jnp.sum(received.reshape(XS, YS, half, local_width).astype(jnp.float32), axis=1)
+        lanes = squares[:, 128 * part : 128 * part + 128]
+        halves.append(lanes[:, :64] + lanes[:, 64:])
+    terms = jnp.concatenate(halves, axis=1).astype(jnp.bfloat16)
+    terms, down_after, down_before = together(terms, down_after, down_before)
+    down_far = far_block(down_after, down_before)
+    sums = sum_over(terms, "z", ZS)
+    sums, down_far = together(sums, down_far)
+    padded = local_hidden + 64
+    gate, up = sums[:, :padded], sums[:, padded:]
+    mean = jnp.sum(gate[:, local_hidden:] + up[:, local_hidden:], axis=-1, keepdims=True) / D
+    scale = lax.rsqrt(mean + epsilon)
+    activated = jax.nn.silu(gate[:, :local_hidden] * scale) * (up[:, :local_hidden] * scale)
+    hidden = collect(activated.astype(jnp.bfloat16), "z", ZS).reshape(x_rows, local_hidden)
+    pieces = (
+        w_down,
+        down_after.reshape(local_hidden, local_width),
+        jnp.concatenate(down_far, axis=0),
+        down_before.reshape(local_hidden, local_width),
+    )
+    down_terms = jnp.stack(
+        [jnp.dot(hidden, piece, preferred_element_type=jnp.float32) for piece in pieces]
+    ).reshape(XS, CORES, half, local_width)
+    last = core_sum(down_terms) + state * (1.0 / YS)
+    result = across(turn(last.astype(jnp.bfloat16), (XS - lax.axis_index("x")) % XS))
     result = lax.all_gather(result.astype(jnp.bfloat16), "core", axis=0, tiled=False)
     outputs = (
         result.reshape(CORES, XS, half // (steps * local_rows), steps, local_rows, local_width)

time: 214 us -> 237 us (1.11)
  starting transfers between devices: 56.5 us -> 79.7 us
  waiting for transfers between devices: 55.6 us -> 73.9 us
  blocking collectives: 59.6 us -> 45.9 us
  between operations: 14.3 us -> 1.32 us
  local copies, waits for them, and re-layouts: 8.06 us -> 13.7 us
  other arithmetic: 3.42 us -> 6.56 us
    ppermute x0 -> x8, starting transfers between devices: none -> 23.5 us  [shift(): return lax.ppermute(block, 'x', [(at, (at + by) % XS) for at in range(XS)])]
    ppermute x0 -> x8, waiting for transfers between devices: none -> 23.4 us  [shift(): return lax.ppermute(block, 'x', [(at, (at + by) % XS) for at in range(XS)])]
    all_gather x2 -> x1, blocking collectives: 14.5 us -> 3.43 us  [body(): lax.all_gather(state.astype(jnp.bfloat16), 'core', axis=0, tiled=False)]
    all_gather x3 -> x0, waiting for transfers between devices: 4.83 us -> none  [the longest x1 4.79 us: body(): gateup_weights = lax.all_gather(gateup_weight, 'x', axis=0, tiled=True)]
    squeeze x0 -> x4, local copies, waits for them, and re-layouts: none -> 4.6 us  [far_block(): return (shift(before[0], 1), shift(after[1], -1))]
    dot_general x9 -> x13, matrix products: 14.2 us -> 10.7 us  [the longest x8 6.21 us: body(): lax.dot_general(ffn_in[at], piece, (((1,), (1,)), ((), ())), preferred_el...]
    all_to_all x3, blocking collectives: 41.7 us -> 39 us  [exchange(): return lax.all_to_all(blocks, axis, 0, 0, tiled=True)]
    all_to_all x6 -> x7, waiting for transfers between devices: 48.7 us -> 50.5 us  [exchange(): return lax.all_to_all(blocks, axis, 0, 0, tiled=True)]
  transfers between devices with their start and end apart: 9 -> 15, of which waited for: 7 -> 11; matrix products, arithmetic and copies ran while one was open for 10% -> 4% of each run, Pallas kernels for 0% -> 0%
where the time goes in v3:
time: 237 us; the launch traced here: 235 us
  starting transfers between devices  79.7 us (34%)
  waiting for transfers between devices  73.9 us (31%)
  blocking collectives  45.9 us (19%)
  matrix products  14.3 us (6%)
  local copies, waits for them, and re-layouts  13.7 us (6%)
  other arithmetic  6.56 us (3%)
    all_to_all x7, starting transfers between devices, exchange(): return lax.all_to_all(blocks, axis, 0, 0, tiled=True)  56.1 us
    all_to_all x7, waiting for transfers between devices, exchange(): return lax.all_to_all(blocks, axis, 0, 0, tiled=True)  50.5 us
    all_to_all x3, blocking collectives, exchange(): return lax.all_to_all(blocks, axis, 0, 0, tiled=True)  39 us
    ppermute x8, starting transfers between devices, shift(): return lax.ppermute(block, 'x', [(at, (at + by) % XS) for at in range(XS)])  23.5 us
    ppermute x8, waiting for transfers between devices, shift(): return lax.ppermute(block, 'x', [(at, (at + by) % XS) for at in range(XS)])  23.4 us
    dot_general x8, matrix products, body(): lax.dot_general(ffn_in[at], piece, (((1,), (1,)), ((), ())), preferred_el...  6.21 us
  transfers between devices with their start and end apart: 15, of which 11 were waited for; matrix products, arithmetic and copies ran while one was open for 4% of the time, Pallas kernels for 0%

profile of v3, /device:TPU:1, one launch (start us, length us, event | category | flops | bytes accessed | tf_op | source)
XLA Modules:
  0.0 235.3 jit_solution(11119466374958248765)
XLA Ops:
  0.7 1.0 convert_element_type.178
  1.7 0.9 convert_multiply_fusion.1
  2.8 0.4 convolution_convert_fusion
  3.3 0.4 copy-done.4
  3.9 1.1 pad_maximum_fusion
  5.0 5.0 %all-to-all-start = ((bf16[4,64,2432]{2,1,0:T(8,128)(2,1)}), bf16[4,64,2432]{2,1,0:T(8,128)(2,1)S(1)}, u32[]{:S(2)}, u32[]{:S(2)}) async-start(bf16[4,64,2432]{2,1,0:T(8,128)(2,1)} %pad_maximum_fusion), calls=%async_computation | async-start | bytes 2490368 | tf_op jit(solution)/shard_map/all_to_all | solution.py:33
  10.0 1.3 fusion.14
  11.3 10.1 %all-to-all-done = bf16[4,64,2432]{2,1,0:T(8,128)(2,1)S(1)} async-done(((bf16[4,64,2432]{2,1,0:T(8,128)(2,1)}), bf16[4,64,2432]{2,1,0:T(8,128)(2,1)S(1)}, u32[]{:S(2)}, u32[]{:S(2)}) %all-to-all-start) | async-done | bytes 1245216 | tf_op jit(solution)/shard_map/all_to_all | solution.py:33
  21.4 0.2 reduce_sum.116
  21.8 0.8 copy.67
  22.6 19.8 %all-to-all-start.1 = ((bf16[16,4,2432]{2,1,0:T(4,128)(2,1)}), bf16[16,4,2432]{2,1,0:T(4,128)(2,1)S(1)}, u32[]{:S(2)}, u32[]{:S(2)}) async-start(bf16[16,4,2432]{2,1,0:T(4,128)(2,1)} %copy.67), calls=%async_computation.1 | async-start | bytes 622592 | tf_op jit(solution)/shard_map/all_to_all | solution.py:33
  42.5 2.8 %collective-permute-start = (bf16[2,832,256]{2,1,0:T(8,128)(2,1)S(1)}, bf16[2,832,256]{2,1,0:T(8,128)(2,1)S(1)}, u32[]{:S(2)}, u32[]{:S(2)}) collective-permute-start(bf16[2,832,256]{2,1,0:T(8,128)(2,1)S(1)} %fusion.14), channel_id=1, source_target_pairs={{0,384},{128,0},{256,128},{384,256},{1,385},{129,1},{257,129},{385... | collective-permute-start | bytes 2555912 | tf_op jit(solution)/shard_map/ppermute | solution.py:47
  45.3 2.5 %collective-permute-start.1 = (bf16[2,832,256]{2,1,0:T(8,128)(2,1)S(1)}, bf16[2,832,256]{2,1,0:T(8,128)(2,1)}, u32[]{:S(2)}, u32[]{:S(2)}) collective-permute-start(bf16[2,832,256]{2,1,0:T(8,128)(2,1)S(1)} %fusion.14), channel_id=1, source_target_pairs={{0,128},{128,256},{256,384},{384,0},{1,129},{129,257},{257,385},{3... | collective-permute-start | bytes 2555912 | tf_op jit(solution)/shard_map/ppermute | solution.py:47
  48.0 8.1 %all-to-all-done.1 = bf16[16,4,2432]{2,1,0:T(4,128)(2,1)S(1)} async-done(((bf16[16,4,2432]{2,1,0:T(4,128)(2,1)}), bf16[16,4,2432]{2,1,0:T(4,128)(2,1)S(1)}, u32[]{:S(2)}, u32[]{:S(2)}) %all-to-all-start.1) | async-done | bytes 311328 | tf_op jit(solution)/shard_map/all_to_all | solution.py:33
  56.2 6.6 %collective-permute-done = bf16[2,832,256]{2,1,0:T(8,128)(2,1)S(1)} collective-permute-done((bf16[2,832,256]{2,1,0:T(8,128)(2,1)S(1)}, bf16[2,832,256]{2,1,0:T(8,128)(2,1)S(1)}, u32[]{:S(2)}, u32[]{:S(2)}) %collective-permute-start) | collective-permute-done | bytes 852000 | tf_op jit(solution)/shard_map/ppermute | solution.py:47
  62.8 3.7 %collective-permute-done.1 = bf16[2,832,256]{2,1,0:T(8,128)(2,1)} collective-permute-done((bf16[2,832,256]{2,1,0:T(8,128)(2,1)S(1)}, bf16[2,832,256]{2,1,0:T(8,128)(2,1)}, u32[]{:S(2)}, u32[]{:S(2)}) %collective-permute-start.1) | collective-permute-done | bytes 852000 | tf_op jit(solution)/shard_map/ppermute | solution.py:47
  67.2 1.3 fusion.59
  68.5 0.2 fusion.60
  68.9 1.2 fusion.29
  70.5 23.8 %all_to_all.50 = bf16[16,4,2048]{2,1,0:T(4,128)(2,1)S(1)} all-to-all(bf16[16,4,2048]{2,1,0:T(4,128)(2,1)S(1)} %broadcast_in_dim.45), channel_id=1, replica_groups=mesh['x'=4,'z'=16,'y'=4,'core'=2] {'z'}, dimensions={0} | all-to-all | bytes 524288 | tf_op jit(solution)/shard_map/all_to_all | solution.py:33
  94.3 1.1 broadcast_in_dim.47
  95.5 3.5 %all-to-all-start.3 = ((bf16[4,64,2048]{2,1,0:T(8,128)(2,1)}), bf16[4,64,2048]{2,1,0:T(8,128)(2,1)S(1)}, u32[]{:S(2)}, u32[]{:S(2)}) async-start(bf16[4,64,2048]{2,1,0:T(8,128)(2,1)} %broadcast_in_dim.47), calls=%async_computation.3 | async-start | bytes 2097152 | tf_op jit(solution)/shard_map/all_to_all | solution.py:33
  99.0 1.8 slice_bitcast_fusion.1
  100.8 3.3 %collective-permute-start.2 = (bf16[832,256]{1,0:T(8,128)(2,1)}, bf16[832,256]{1,0:T(8,128)(2,1)}, u32[]{:S(2)}, u32[]{:S(2)}) collective-permute-start(bf16[832,256]{1,0:T(8,128)(2,1)} %slice_bitcast_fusion.1), channel_id=1, source_target_pairs={{0,128},{128,256},{256,384},{384,0},{1,129},{129,257},{257,385},{3... | collective-permute-start | bytes 1277960 | tf_op jit(solution)/shard_map/ppermute | solution.py:47
  104.1 1.8 slice_bitcast_fusion
  106.0 3.2 %collective-permute-start.3 = (bf16[832,256]{1,0:T(8,128)(2,1)}, bf16[832,256]{1,0:T(8,128)(2,1)}, u32[]{:S(2)}, u32[]{:S(2)}) collective-permute-start(bf16[832,256]{1,0:T(8,128)(2,1)} %slice_bitcast_fusion), channel_id=1, source_target_pairs={{0,384},{128,0},{256,128},{384,256},{1,385},{129,1},{257,129},{385... | collective-permute-start | bytes 1277960 | tf_op jit(solution)/shard_map/ppermute | solution.py:47
  109.1 3.3 %collective-permute-start.4 = (bf16[2,416,256]{2,1,0:T(8,128)(2,1)}, bf16[2,416,256]{2,1,0:T(8,128)(2,1)S(1)}, u32[]{:S(2)}, u32[]{:S(2)}) collective-permute-start(bf16[2,416,256]{2,1,0:T(8,128)(2,1)} %bitcast.25), channel_id=1, source_target_pairs={{0,384},{128,0},{256,128},{384,256},{1,385},{129,1},{257,129},{385... | collective-permute-start | bytes 1277960 | tf_op jit(solution)/shard_map/ppermute | solution.py:47
  112.5 2.0 collective-permute-start.5
  114.4 0.7 reshape.314
  115.1 0.9 constant_dynamic-slice_fusion
  116.2 3.8 %collective-permute-done.3 = bf16[832,256]{1,0:T(8,128)(2,1)} collective-permute-done((bf16[832,256]{1,0:T(8,128)(2,1)}, bf16[832,256]{1,0:T(8,128)(2,1)}, u32[]{:S(2)}, u32[]{:S(2)}) %collective-permute-start.3) | collective-permute-done | bytes 426016 | tf_op jit(solution)/shard_map/ppermute | solution.py:47
  120.0 9.1 %collective-permute-done.4 = bf16[2,416,256]{2,1,0:T(8,128)(2,1)S(1)} collective-permute-done((bf16[2,416,256]{2,1,0:T(8,128)(2,1)}, bf16[2,416,256]{2,1,0:T(8,128)(2,1)S(1)}, u32[]{:S(2)}, u32[]{:S(2)}) %collective-permute-start.4) | collective-permute-done | bytes 426016 | tf_op jit(solution)/shard_map/ppermute | solution.py:47
  129.1 1.7 fusion.5
  130.8 8.3 %all_to_all.51 = bf16[2,4,32,256]{3,2,1,0:T(8,128)(2,1)S(1)} all-to-all(bf16[2,4,32,256]{3,2,1,0:T(8,128)(2,1)S(1)} %copy.74), channel_id=1, replica_groups=mesh['x'=4,'z'=16,'y'=4,'core'=2] {'core'}, dimensions={0} | all-to-all | bytes 262144 | tf_op jit(solution)/shard_map/all_to_all | solution.py:33
  139.2 0.7 broadcast_in_dim.48
  139.9 6.4 %all-to-all-start.5 = ((bf16[16,32,256]{2,1,0:T(8,128)(2,1)}), bf16[16,32,256]{2,1,0:T(8,128)(2,1)S(1)}, u32[]{:S(2)}, u32[]{:S(2)}) async-start(bf16[16,32,256]{2,1,0:T(8,128)(2,1)} %bitcast.33), calls=%async_computation.5 | async-start | bytes 524288 | tf_op jit(solution)/shard_map/all_to_all | solution.py:33
  146.3 7.6 %all-to-all-done.5 = bf16[16,32,256]{2,1,0:T(8,128)(2,1)S(1)} async-done(((bf16[16,32,256]{2,1,0:T(8,128)(2,1)}), bf16[16,32,256]{2,1,0:T(8,128)(2,1)S(1)}, u32[]{:S(2)}, u32[]{:S(2)}) %all-to-all-start.5) | async-done | bytes 262176 | tf_op jit(solution)/shard_map/all_to_all | solution.py:33
  153.9 3.4 %all-gather = bf16[8,32,256]{2,1,0:T(8,128)(2,1)S(1)} all-gather(bf16[4,32,256]{2,1,0:T(8,128)(2,1)S(1)} %fusion.46), channel_id=2, replica_groups=mesh['x'=4,'z'=16,'y'=4,'core'=2] {'core'}, dimensions={0}, use_global_device_ids=true | all-gather | bytes 196608 | tf_op jit(solution)/shard_map/all_gather | solution.py:197
  157.4 0.3 fusion.20
  157.7 0.3 fusion.23
  157.9 1.3 fusion.18
  159.2 1.3 fusion.55
  160.5 0.3 convolution_add_fusion.1
  160.8 0.3 convolution_add_fusion.3
  161.2 1.3 fusion.4
  162.5 1.3 fusion.3
  163.9 0.7 reshape.316
  164.6 6.8 %all-to-all-start.6 = ((bf16[16,4,1792]{2,1,0:T(4,128)(2,1)}), bf16[16,4,1792]{2,1,0:T(4,128)(2,1)S(1)}, u32[]{:S(2)}, u32[]{:S(2)}) async-start(bf16[16,4,1792]{2,1,0:T(4,128)(2,1)} %reshape.316), calls=%async_computation.6 | async-start | bytes 458752 | tf_op jit(solution)/shard_map/all_to_all | solution.py:33
  171.5 0.9 slice_bitcast_fusion.3
  172.4 1.9 collective-permute-start.6
  174.4 4.6 %collective-permute-start.7 = (bf16[416,256]{1,0:T(8,128)(2,1)S(1)}, bf16[416,256]{1,0:T(8,128)(2,1)S(1)}, u32[]{:S(2)}, u32[]{:S(2)}) collective-permute-start(bf16[416,256]{1,0:T(8,128)(2,1)S(1)} %slice_bitcast_fusion.2), channel_id=1, source_target_pairs={{0,384},{128,0},{256,128},{384,256},{1,385},{129,1},{257,129},{385... | collective-permute-start | bytes 638984 | tf_op jit(solution)/shard_map/ppermute | solution.py:47
  178.9 5.9 %all-to-all-done.6 = bf16[16,4,1792]{2,1,0:T(4,128)(2,1)S(1)} async-done(((bf16[16,4,1792]{2,1,0:T(4,128)(2,1)}), bf16[16,4,1792]{2,1,0:T(4,128)(2,1)S(1)}, u32[]{:S(2)}, u32[]{:S(2)}) %all-to-all-start.6) | async-done | bytes 229408 | tf_op jit(solution)/shard_map/all_to_all | solution.py:33
  185.3 0.7 broadcast_in_dim.49
  186.0 9.3 %all-to-all-start.7 = ((bf16[16,4,832]{2,1,0:T(4,128)(2,1)}), bf16[16,4,832]{2,1,0:T(4,128)(2,1)S(1)}, u32[]{:S(2)}, u32[]{:S(2)}) async-start(bf16[16,4,832]{2,1,0:T(4,128)(2,1)} %broadcast_in_dim.49), calls=%async_computation.7 | async-start | bytes 229376 | tf_op jit(solution)/shard_map/all_to_all | solution.py:33
  195.3 12.0 %all-to-all-done.7 = bf16[16,4,832]{2,1,0:T(4,128)(2,1)S(1)} async-done(((bf16[16,4,832]{2,1,0:T(4,128)(2,1)}), bf16[16,4,832]{2,1,0:T(4,128)(2,1)S(1)}, u32[]{:S(2)}, u32[]{:S(2)}) %all-to-all-start.7) | async-done | bytes 106528 | tf_op jit(solution)/shard_map/all_to_all | solution.py:33
  207.4 1.2 fusion.6
  208.8 1.2 fusion.9
  210.3 7.0 %all_to_all.52 = bf16[2,4,32,256]{3,2,1,0:T(8,128)(2,1)S(1)} all-to-all(bf16[2,4,32,256]{3,2,1,0:T(8,128)(2,1)S(1)} %copy.78), channel_id=1, replica_groups=mesh['x'=4,'z'=16,'y'=4,'core'=2] {'core'}, dimensions={0} | all-to-all | bytes 262144 | tf_op jit(solution)/shard_map/all_to_all | solution.py:33
  217.4 0.7 broadcast_in_dim.50
  218.1 5.3 %all-to-all-start.9 = ((bf16[16,32,256]{2,1,0:T(8,128)(2,1)}), bf16[16,32,256]{2,1,0:T(8,128)(2,1)S(1)}, u32[]{:S(2)}, u32[]{:S(2)}) async-start(bf16[16,32,256]{2,1,0:T(8,128)(2,1)} %bitcast.59), calls=%async_computation.9 | async-start | bytes 524288 | tf_op jit(solution)/shard_map/all_to_all | solution.py:33
  223.5 0.6 copy.81
  224.1 6.9 %all-to-all-done.9 = bf16[16,32,256]{2,1,0:T(8,128)(2,1)S(1)} async-done(((bf16[16,32,256]{2,1,0:T(8,128)(2,1)}), bf16[16,32,256]{2,1,0:T(8,128)(2,1)S(1)}, u32[]{:S(2)}, u32[]{:S(2)}) %all-to-all-start.9) | async-done | bytes 262176 | tf_op jit(solution)/shard_map/all_to_all | solution.py:33
  231.0 3.4 %all-gather.1 = bf16[8,32,256]{2,1,0:T(8,128)(2,1)S(1)} all-gather(bf16[4,32,256]{2,1,0:T(8,128)(2,1)S(1)} %bitcast_reduce_fusion), channel_id=3, replica_groups=mesh['x'=4,'z'=16,'y'=4,'core'=2] {'core'}, dimensions={0}, use_global_device_ids=true | all-gather | bytes 196608 | tf_op jit(solution)/shard_map/all_gather | solution.py:237
  234.6 0.7 copy.80
  (88 shorter events, 3.8 us)
Async XLA Ops:
  0.6 2.2 copy-start
  0.6 2.0 copy-start.6
  2.8 0.9 copy-start.4
  5.0 5.0 %copy-start.7 = (bf16[256]{0:T(256)(128)(2,1)S(1)}, bf16[256]{0:T(256)(128)(2,1)}, u32[]{:S(2)}) copy-start(bf16[256]{0:T(256)(128)(2,1)} %param.16) | copy-start | bytes 1540
  5.0 16.4 %all-to-all-start = ((bf16[4,64,2432]{2,1,0:T(8,128)(2,1)}), bf16[4,64,2432]{2,1,0:T(8,128)(2,1)S(1)}, u32[]{:S(2)}, u32[]{:S(2)}) async-start(bf16[4,64,2432]{2,1,0:T(8,128)(2,1)} %pad_maximum_fusion), calls=%async_computation | async-start | bytes 2490368 | tf_op jit(solution)/shard_map/all_to_all | solution.py:33
  21.6 26.2 %copy-start.8 = (s32[2]{0:T(128)S(1)}, s32[2]{0:T(128)}, u32[]{:S(2)}) copy-start(s32[2]{0:T(128)} %param.21) | copy-start | bytes 28
  21.6 26.2 %copy-start.5 = (s32[2]{0:T(128)S(1)}, s32[2]{0:T(128)}, u32[]{:S(2)}) copy-start(s32[2]{0:T(128)} %param.20) | copy-start | bytes 28
  22.6 33.4 %all-to-all-start.1 = ((bf16[16,4,2432]{2,1,0:T(4,128)(2,1)}), bf16[16,4,2432]{2,1,0:T(4,128)(2,1)S(1)}, u32[]{:S(2)}, u32[]{:S(2)}) async-start(bf16[16,4,2432]{2,1,0:T(4,128)(2,1)} %copy.67), calls=%async_computation.1 | async-start | bytes 622592 | tf_op jit(solution)/shard_map/all_to_all | solution.py:33
  42.5 20.3 %collective-permute-start = (bf16[2,832,256]{2,1,0:T(8,128)(2,1)S(1)}, bf16[2,832,256]{2,1,0:T(8,128)(2,1)S(1)}, u32[]{:S(2)}, u32[]{:S(2)}) collective-permute-start(bf16[2,832,256]{2,1,0:T(8,128)(2,1)S(1)} %fusion.14), channel_id=1, source_target_pairs={{0,384},{128,0},{256,128},{384,256},{1,385},{129,1},{257,129},{385... | collective-permute-start | bytes 2555912 | tf_op jit(solution)/shard_map/ppermute | solution.py:47
  45.3 21.2 %collective-permute-start.1 = (bf16[2,832,256]{2,1,0:T(8,128)(2,1)S(1)}, bf16[2,832,256]{2,1,0:T(8,128)(2,1)}, u32[]{:S(2)}, u32[]{:S(2)}) collective-permute-start(bf16[2,832,256]{2,1,0:T(8,128)(2,1)S(1)} %fusion.14), channel_id=1, source_target_pairs={{0,128},{128,256},{256,384},{384,0},{1,129},{129,257},{257,385},{3... | collective-permute-start | bytes 2555912 | tf_op jit(solution)/shard_map/ppermute | solution.py:47
  62.8 7.4 %copy-start.1 = (bf16[2,832,256]{2,1,0:T(8,128)(2,1)}, bf16[2,832,256]{2,1,0:T(8,128)(2,1)S(1)}, u32[]{:S(2)}) copy-start(bf16[2,832,256]{2,1,0:T(8,128)(2,1)S(1)} %collective-permute-done) | copy-start | bytes 2555908
  95.5 33.7 %all-to-all-start.3 = ((bf16[4,64,2048]{2,1,0:T(8,128)(2,1)}), bf16[4,64,2048]{2,1,0:T(8,128)(2,1)S(1)}, u32[]{:S(2)}, u32[]{:S(2)}) async-start(bf16[4,64,2048]{2,1,0:T(8,128)(2,1)} %broadcast_in_dim.47), calls=%async_computation.3 | async-start | bytes 2097152 | tf_op jit(solution)/shard_map/all_to_all | solution.py:33
  99.0 15.4 %copy-start.3 = (bf16[2,128,256]{2,1,0:T(8,128)(2,1)S(1)}, bf16[2,128,256]{2,1,0:T(8,128)(2,1)}, u32[]{:S(2)}) copy-start(bf16[2,128,256]{2,1,0:T(8,128)(2,1)} %param.11) | copy-start | bytes 393220
  100.8 15.3 %collective-permute-start.2 = (bf16[832,256]{1,0:T(8,128)(2,1)}, bf16[832,256]{1,0:T(8,128)(2,1)}, u32[]{:S(2)}, u32[]{:S(2)}) collective-permute-start(bf16[832,256]{1,0:T(8,128)(2,1)} %slice_bitcast_fusion.1), channel_id=1, source_target_pairs={{0,128},{128,256},{256,384},{384,0},{1,129},{129,257},{257,385},{3... | collective-permute-start | bytes 1277960 | tf_op jit(solution)/shard_map/ppermute | solution.py:47
  106.0 14.0 %collective-permute-start.3 = (bf16[832,256]{1,0:T(8,128)(2,1)}, bf16[832,256]{1,0:T(8,128)(2,1)}, u32[]{:S(2)}, u32[]{:S(2)}) collective-permute-start(bf16[832,256]{1,0:T(8,128)(2,1)} %slice_bitcast_fusion), channel_id=1, source_target_pairs={{0,384},{128,0},{256,128},{384,256},{1,385},{129,1},{257,129},{385... | collective-permute-start | bytes 1277960 | tf_op jit(solution)/shard_map/ppermute | solution.py:47
  109.1 20.0 %collective-permute-start.4 = (bf16[2,416,256]{2,1,0:T(8,128)(2,1)}, bf16[2,416,256]{2,1,0:T(8,128)(2,1)S(1)}, u32[]{:S(2)}, u32[]{:S(2)}) collective-permute-start(bf16[2,416,256]{2,1,0:T(8,128)(2,1)} %bitcast.25), channel_id=1, source_target_pairs={{0,384},{128,0},{256,128},{384,256},{1,385},{129,1},{257,129},{385... | collective-permute-start | bytes 1277960 | tf_op jit(solution)/shard_map/ppermute | solution.py:47
  112.5 16.7 %collective-permute-start.5 = (bf16[2,416,256]{2,1,0:T(8,128)(2,1)}, bf16[2,416,256]{2,1,0:T(8,128)(2,1)}, u32[]{:S(2)}, u32[]{:S(2)}) collective-permute-start(bf16[2,416,256]{2,1,0:T(8,128)(2,1)} %bitcast.25), channel_id=1, source_target_pairs={{0,128},{128,256},{256,384},{384,0},{1,129},{129,257},{257,385},{3... | collective-permute-start | bytes 1277960 | tf_op jit(solution)/shard_map/ppermute | solution.py:47
  139.9 14.0 %all-to-all-start.5 = ((bf16[16,32,256]{2,1,0:T(8,128)(2,1)}), bf16[16,32,256]{2,1,0:T(8,128)(2,1)S(1)}, u32[]{:S(2)}, u32[]{:S(2)}) async-start(bf16[16,32,256]{2,1,0:T(8,128)(2,1)} %bitcast.33), calls=%async_computation.5 | async-start | bytes 524288 | tf_op jit(solution)/shard_map/all_to_all | solution.py:33
  157.6 2.9 %copy-start.2 = (bf16[2,832,256]{2,1,0:T(8,128)(2,1)S(1)}, bf16[2,832,256]{2,1,0:T(8,128)(2,1)}, u32[]{:S(2)}) copy-start(bf16[2,832,256]{2,1,0:T(8,128)(2,1)} %copy-done.1) | copy-start | bytes 2555908
  164.6 20.2 %all-to-all-start.6 = ((bf16[16,4,1792]{2,1,0:T(4,128)(2,1)}), bf16[16,4,1792]{2,1,0:T(4,128)(2,1)S(1)}, u32[]{:S(2)}, u32[]{:S(2)}) async-start(bf16[16,4,1792]{2,1,0:T(4,128)(2,1)} %reshape.316), calls=%async_computation.6 | async-start | bytes 458752 | tf_op jit(solution)/shard_map/all_to_all | solution.py:33
  172.4 12.5 %collective-permute-start.6 = (bf16[416,256]{1,0:T(8,128)(2,1)S(1)}, bf16[416,256]{1,0:T(8,128)(2,1)S(1)}, u32[]{:S(2)}, u32[]{:S(2)}) collective-permute-start(bf16[416,256]{1,0:T(8,128)(2,1)S(1)} %slice_bitcast_fusion.3), channel_id=1, source_target_pairs={{0,128},{128,256},{256,384},{384,0},{1,129},{129,257},{257,385},{3... | collective-permute-start | bytes 638984 | tf_op jit(solution)/shard_map/ppermute | solution.py:47
  174.4 10.6 %collective-permute-start.7 = (bf16[416,256]{1,0:T(8,128)(2,1)S(1)}, bf16[416,256]{1,0:T(8,128)(2,1)S(1)}, u32[]{:S(2)}, u32[]{:S(2)}) collective-permute-start(bf16[416,256]{1,0:T(8,128)(2,1)S(1)} %slice_bitcast_fusion.2), channel_id=1, source_target_pairs={{0,384},{128,0},{256,128},{384,256},{1,385},{129,1},{257,129},{385... | collective-permute-start | bytes 638984 | tf_op jit(solution)/shard_map/ppermute | solution.py:47
  186.0 21.3 %all-to-all-start.7 = ((bf16[16,4,832]{2,1,0:T(4,128)(2,1)}), bf16[16,4,832]{2,1,0:T(4,128)(2,1)S(1)}, u32[]{:S(2)}, u32[]{:S(2)}) async-start(bf16[16,4,832]{2,1,0:T(4,128)(2,1)} %broadcast_in_dim.49), calls=%async_computation.7 | async-start | bytes 229376 | tf_op jit(solution)/shard_map/all_to_all | solution.py:33
  218.1 12.8 %all-to-all-start.9 = ((bf16[16,32,256]{2,1,0:T(8,128)(2,1)}), bf16[16,32,256]{2,1,0:T(8,128)(2,1)S(1)}, u32[]{:S(2)}, u32[]{:S(2)}) async-start(bf16[16,32,256]{2,1,0:T(8,128)(2,1)} %bitcast.59), calls=%async_computation.9 | async-start | bytes 524288 | tf_op jit(solution)/shard_map/all_to_all | solution.py:33

commit v4 on v3

--- a/solution.py
+++ b/solution.py
@@ -43,36 +43,10 @@
     return exchange(jnp.broadcast_to(block[None], (size,) + block.shape), axis)
 
 
-def shift(block, by):
-    return lax.ppermute(block, "x", [(at, (at + by) % XS) for at in range(XS)])
-
-
-def both_ways(block):
-    return shift(block, -1), shift(block, 1)
-
-
-def far_block(after, before):
-    return shift(before[0], 1), shift(after[1], -1)
-
-
-def core_sum(terms):
-    received = exchange(terms.astype(jnp.bfloat16).transpose(1, 0, 2, 3), "core")
-    return jnp.sum(received.astype(jnp.float32), axis=0)
-
-
-def across(blocks):
-    shape = blocks.shape
-    copies = jnp.broadcast_to(blocks.astype(jnp.bfloat16)[:, None], (XS, YS) + shape[1:])
-    received = exchange(copies.reshape((XS * YS,) + shape[1:]), ("x", "y"))
-    return jnp.sum(received.reshape((XS, YS) + shape[1:]).astype(jnp.float32), axis=1)
-
-
-def turn(blocks, by):
-    return lax.dynamic_slice_in_dim(jnp.concatenate([blocks, blocks], axis=0), by, XS, axis=0)
-
-
-def together(*values):
-    return lax.optimization_barrier(values)
+def group_sum(terms, base):
+    rows, columns = terms.shape
+    pair = sum_over(terms, "core", CORES).astype(jnp.bfloat16)
+    return base + jnp.sum(collect(pair, "y", YS).astype(jnp.float32), axis=0)
 
 
 def lane_squares(values, lanes):
@@ -133,7 +107,7 @@
     squares_at = keyvals_at + 2 * head_dim
     rows = steps * all_rows
     x_rows = rows // XS
-    half = x_rows // CORES
+    half = rows // CORES
     gateup = w_gateup.transpose(1, 2, 0).astype(jnp.float32) * ffn_gain.astype(jnp.float32)
     gateup = gateup.astype(jnp.bfloat16)
 
@@ -153,14 +127,8 @@
         axis=1,
     )
     sums = sum_over(terms, "x", XS).astype(jnp.bfloat16)
-    sums, gateup = together(sums, gateup)
-    gateup_after, gateup_before = both_ways(gateup)
     sums = sums.reshape(steps, ZS, local_rows, -1).transpose(1, 0, 2, 3).reshape(x_rows, -1)
     sums = sum_over(sums, "z", ZS)
-    sums, gateup_after, gateup_before, w_down = together(sums, gateup_after, gateup_before, w_down)
-    gateup_far = far_block(gateup_after, gateup_before)
-    down = w_down.reshape(2, local_hidden // 2, local_width)
-    down_after, down_before = both_ways(down)
     mean = jnp.sum(sums[:, squares_at:], axis=-1, keepdims=True) / D
     sums = (sums[:, :squares_at] * lax.rsqrt(mean + epsilon)).reshape(steps, local_rows, squares_at)
     offsets = positions[None, :] + jnp.arange(steps)[:, None]
@@ -181,63 +149,42 @@
     heads = mixed.astype(jnp.bfloat16).transpose(1, 0, 2, 3).reshape(steps * local_rows, keyvals_at)
 
     all_heads = collect(collect(heads, "z", ZS).reshape(x_rows, keyvals_at), "x", XS)
-    all_heads, gateup_far, down_after, down_before = together(
-        all_heads, gateup_far, down_after, down_before
-    )
     attn_terms = jnp.dot(
         all_heads.reshape(rows, keyvals_at), w_out, preferred_element_type=jnp.float32
-    ).reshape(XS, CORES, half, local_width)
+    )
     residual = lax.dynamic_index_in_dim(
-        inputs.reshape(steps, XS, CORES, ZS // CORES, local_rows, local_width),
-        lax.axis_index("core"), 2, keepdims=False,
-    )
-    residual = residual.transpose(1, 2, 0, 3, 4).reshape(XS, half, local_width).astype(jnp.float32)
-    state = across(core_sum(attn_terms) + residual * (1.0 / YS))
-    state = turn(state, lax.axis_index("x"))
-    ffn_in = lax.all_gather(state.astype(jnp.bfloat16), "core", axis=0, tiled=False)
-    ffn_in, w_down = together(ffn_in, w_down)
-    ffn_in = ffn_in.transpose(1, 0, 2, 3).reshape(XS, x_rows, local_width)
+        inputs.reshape(steps, CORES, all_rows // CORES // local_rows, local_rows, local_width),
+        lax.axis_index("core"), 1, keepdims=False,
+    )
+    residual = residual.transpose(1, 0, 2, 3).reshape(half, local_width).astype(jnp.float32)
+    state = group_sum(attn_terms, residual)
+    ffn_in = lax.all_gather(state.astype(jnp.bfloat16), "core", axis=0, tiled=True)
     squares = ffn_in.astype(jnp.float32)
-    squares = jnp.sum(squares * squares, axis=0)
+    squares = squares * squares
     halves = []
     for part in range(2):
-        pieces = (gateup[part], gateup_after[part], gateup_far[part], gateup_before[part])
         halves.append(
-            sum(
-                lax.dot_general(
-                    ffn_in[at], piece, (((1,), (1,)), ((), ())), preferred_element_type=jnp.float32
-                )
-                for at, piece in enumerate(pieces)
+            lax.dot_general(
+                ffn_in, gateup[part], (((1,), (1,)), ((), ())), preferred_element_type=jnp.float32
             )
         )
         lanes = squares[:, 128 * part : 128 * part + 128]
         halves.append(lanes[:, :64] + lanes[:, 64:])
-    terms = jnp.concatenate(halves, axis=1).astype(jnp.bfloat16)
-    terms, down_after, down_before = together(terms, down_after, down_before)
-    down_far = far_block(down_after, down_before)
-    sums = sum_over(terms, "z", ZS)
-    sums, down_far = together(sums, down_far)
+    terms = jnp.concatenate(halves, axis=1)
+    sums = sum_over(sum_over(terms, "x", XS), "z", ZS)
     padded = local_hidden + 64
     gate, up = sums[:, :padded], sums[:, padded:]
     mean = jnp.sum(gate[:, local_hidden:] + up[:, local_hidden:], axis=-1, keepdims=True) / D
     scale = lax.rsqrt(mean + epsilon)
     activated = jax.nn.silu(gate[:, :local_hidden] * scale) * (up[:, :local_hidden] * scale)
     hidden = collect(activated.astype(jnp.bfloat16), "z", ZS).reshape(x_rows, local_hidden)
-    pieces = (
-        w_down,
-        down_after.reshape(local_hidden, local_width),
-        jnp.concatenate(down_far, axis=0),
-        down_before.reshape(local_hidden, local_width),
-    )
-    down_terms = jnp.stack(
-        [jnp.dot(hidden, piece, preferred_element_type=jnp.float32) for piece in pieces]
-    ).reshape(XS, CORES, half, local_width)
-    last = core_sum(down_terms) + state * (1.0 / YS)
-    result = across(turn(last.astype(jnp.bfloat16), (XS - lax.axis_index("x")) % XS))
-    result = lax.all_gather(result.astype(jnp.bfloat16), "core", axis=0, tiled=False)
+    hidden = collect(hidden, "x", XS).reshape(rows, local_hidden)
+    down_terms = jnp.dot(hidden, w_down, preferred_element_type=jnp.float32)
+    result = group_sum(down_terms, state).astype(jnp.bfloat16)
+    result = lax.all_gather(result, "core", axis=0, tiled=True)
     outputs = (
-        result.reshape(CORES, XS, half // (steps * local_rows), steps, local_rows, local_width)
-        .transpose(3, 1, 0, 2, 4, 5)
+        result.reshape(XS * ZS, steps, local_rows, local_width)
+        .transpose(1, 0, 2, 3)
         .reshape(steps, all_rows, local_width)
     )
     return (outputs, new_entries)

time: 237 us -> 214 us (0.903)
  blocking collectives: 45.9 us -> 134 us
  starting transfers between devices: 79.7 us -> 29.7 us
  waiting for transfers between devices: 73.9 us -> 33.6 us
  matrix products: 14.3 us -> 2.99 us
  local copies, waits for them, and re-layouts: 13.7 us -> 6.54 us
    all_to_all x3 -> x8, blocking collectives: 39 us -> 128 us  [exchange(): return lax.all_to_all(blocks, axis, 0, 0, tiled=True)]
    all_to_all x7 -> x4, starting transfers between devices: 56.1 us -> 29.7 us  [exchange(): return lax.all_to_all(blocks, axis, 0, 0, tiled=True)]
    ppermute x8 -> x0, starting transfers between devices: 23.5 us -> none  [shift(): return lax.ppermute(block, 'x', [(at, (at + by) % XS) for at in range(XS)])]
    ppermute x8 -> x0, waiting for transfers between devices: 23.4 us -> none  [shift(): return lax.ppermute(block, 'x', [(at, (at + by) % XS) for at in range(XS)])]
    all_to_all x7 -> x4, waiting for transfers between devices: 50.5 us -> 33.6 us  [exchange(): return lax.all_to_all(blocks, axis, 0, 0, tiled=True)]
    dot_general x12 -> x3, matrix products: 9.04 us -> 0.96 us  [the longest x2 0.66 us: body(): lax.dot_general(ffn_in, gateup[part], (((1,), (1,)), ((), ())), preferred...]
    squeeze x4 -> x0, local copies, waits for them, and re-layouts: 4.6 us -> none  [far_block(): return (shift(before[0], 1), shift(after[1], -1))]
  transfers between devices with their start and end apart: 15 -> 4, of which waited for: 11 -> 4; matrix products, arithmetic and copies ran while one was open for 4% -> 1% of each run, Pallas kernels for 0% -> 0%
where the time goes in v4:
time: 214 us; the launch traced here: 213 us
  blocking collectives  134 us (63%)
  waiting for transfers between devices  33.6 us (16%)
  starting transfers between devices  29.7 us (14%)
  local copies, waits for them, and re-layouts  6.54 us (3%)
  other arithmetic  4.43 us (2%)
  matrix products  2.99 us (1%)
    all_to_all x8, blocking collectives, exchange(): return lax.all_to_all(blocks, axis, 0, 0, tiled=True)  128 us
    all_to_all x4, waiting for transfers between devices, exchange(): return lax.all_to_all(blocks, axis, 0, 0, tiled=True)  33.6 us
    all_to_all x4, starting transfers between devices, exchange(): return lax.all_to_all(blocks, axis, 0, 0, tiled=True)  29.7 us
  transfers between devices with their start and end apart: 4, of which 4 were waited for; matrix products, arithmetic and copies ran while one was open for 1% of the time, Pallas kernels for 0%

profile of v4, /device:TPU:1, one launch (start us, length us, event | category | flops | bytes accessed | tf_op | source)
XLA Modules:
  0.0 212.9 jit_solution(16380484983491564376)
XLA Ops:
  0.7 1.0 convert_element_type.171
  1.7 0.9 convert_multiply_fusion.1
  2.8 0.4 convolution_convert_fusion
  3.3 0.4 copy-done.6
  3.7 0.2 convolution_convert_fusion.4
  3.9 0.1 pad_maximum_fusion
  4.0 17.0 %all_to_all.60 = bf16[4,64,2432]{2,1,0:T(8,128)(2,1)S(1)} all-to-all(bf16[4,64,2432]{2,1,0:T(8,128)(2,1)S(1)} %pad_maximum_fusion), channel_id=1, replica_groups=mesh['x'=4,'z'=16,'y'=4,'core'=2] {'x'}, dimensions={0} | all-to-all | bytes 2490368 | tf_op jit(solution)/shard_map/all_to_all | solution.py:33
  21.0 0.2 reduce_sum.120
  21.3 0.1 reshape.249
  21.5 0.8 copy.107
  22.3 18.5 %all-to-all-start.1 = ((bf16[16,4,2432]{2,1,0:T(4,128)(2,1)}), bf16[16,4,2432]{2,1,0:T(4,128)(2,1)S(1)}, u32[]{:S(2)}, u32[]{:S(2)}) async-start(bf16[16,4,2432]{2,1,0:T(4,128)(2,1)} %copy.107), calls=%async_computation.1 | async-start | bytes 622592 | tf_op jit(solution)/shard_map/all_to_all | solution.py:33
  40.9 0.1 add_convert_fusion.3
  40.9 0.1 iota_compare_fusion
  41.0 13.1 %all-to-all-done.1 = bf16[16,4,2432]{2,1,0:T(4,128)(2,1)S(1)} async-done(((bf16[16,4,2432]{2,1,0:T(4,128)(2,1)}), bf16[16,4,2432]{2,1,0:T(4,128)(2,1)S(1)}, u32[]{:S(2)}, u32[]{:S(2)}) %all-to-all-start.1) | async-done | bytes 311328 | tf_op jit(solution)/shard_map/all_to_all | solution.py:33
  54.1 0.1 convert_reduce_fusion
  54.2 0.1 slice_reduce_fusion
  54.4 0.1 slice_multiply_fusion
  54.5 0.1 fusion.28
  54.6 0.1 fusion.29
  54.7 0.1 subtract_convert_fusion.1
  54.8 0.1 pad_maximum_fusion.1
  54.9 0.3 fusion.30
  55.2 0.2 fusion.31
  55.5 0.2 fusion.9
  55.7 0.2 fusion.5
  55.9 0.2 fusion.1
  56.2 0.1 broadcast_in_dim.49
  56.3 24.6 %all_to_all.61 = bf16[16,4,2048]{2,1,0:T(4,128)(2,1)S(1)} all-to-all(bf16[16,4,2048]{2,1,0:T(4,128)(2,1)S(1)} %broadcast_in_dim.49), channel_id=1, replica_groups=mesh['x'=4,'z'=16,'y'=4,'core'=2] {'z'}, dimensions={0} | all-to-all | bytes 524288 | tf_op jit(solution)/shard_map/all_to_all | solution.py:33
  80.8 0.1 broadcast_in_dim.50
  80.9 1.1 broadcast_in_dim.51
  82.0 3.6 %all-to-all-start.3 = ((bf16[4,64,2048]{2,1,0:T(8,128)(2,1)}), bf16[4,64,2048]{2,1,0:T(8,128)(2,1)S(1)}, u32[]{:S(2)}, u32[]{:S(2)}) async-start(bf16[4,64,2048]{2,1,0:T(8,128)(2,1)} %broadcast_in_dim.51), calls=%async_computation.3 | async-start | bytes 2097152 | tf_op jit(solution)/shard_map/all_to_all | solution.py:33
  85.7 0.1 reshape.247
  85.8 0.1 reshape.261
  85.9 9.4 %all-to-all-done.3 = bf16[4,64,2048]{2,1,0:T(8,128)(2,1)S(1)} async-done(((bf16[4,64,2048]{2,1,0:T(8,128)(2,1)}), bf16[4,64,2048]{2,1,0:T(8,128)(2,1)S(1)}, u32[]{:S(2)}, u32[]{:S(2)}) %all-to-all-start.3) | async-done | bytes 1048608 | tf_op jit(solution)/shard_map/all_to_all | solution.py:33
  95.4 0.4 convolution_convert_fusion.5
  95.8 11.5 %all_to_all.62 = bf16[2,128,256]{2,1,0:T(8,128)(2,1)S(1)} all-to-all(bf16[2,128,256]{2,1,0:T(8,128)(2,1)S(1)} %bitcast.91), channel_id=1, replica_groups=mesh['x'=4,'z'=16,'y'=4,'core'=2] {'core'}, dimensions={0} | all-to-all | bytes 262144 | tf_op jit(solution)/shard_map/all_to_all | solution.py:33
  107.4 0.7 broadcast_in_dim.52
  108.1 4.2 %all-to-all-start.5 = ((bf16[4,128,256]{2,1,0:T(8,128)(2,1)}), bf16[4,128,256]{2,1,0:T(8,128)(2,1)S(1)}, u32[]{:S(2)}, u32[]{:S(2)}) async-start(bf16[4,128,256]{2,1,0:T(8,128)(2,1)} %broadcast_in_dim.52), calls=%async_computation.5 | async-start | bytes 524288 | tf_op jit(solution)/shard_map/all_to_all | solution.py:33
  112.3 0.2 fusion.4
  112.4 5.7 %all-to-all-done.5 = bf16[4,128,256]{2,1,0:T(8,128)(2,1)S(1)} async-done(((bf16[4,128,256]{2,1,0:T(8,128)(2,1)}), bf16[4,128,256]{2,1,0:T(8,128)(2,1)S(1)}, u32[]{:S(2)}, u32[]{:S(2)}) %all-to-all-start.5) | async-done | bytes 262176 | tf_op jit(solution)/shard_map/all_to_all | solution.py:33
  118.2 3.3 %all_gather.6 = bf16[256,256]{1,0:T(8,128)(2,1)S(1)} all-gather(bf16[128,256]{1,0:T(8,128)(2,1)S(1)} %get-tuple-element.18), channel_id=1, replica_groups=mesh['x'=4,'z'=16,'y'=4,'core'=2] {'core'}, dimensions={0}, use_global_device_ids=true | all-gather | bytes 196608 | tf_op jit(solution)/shard_map/all_gather | solution.py:161
  121.5 0.3 convolution_convert_fusion.1
  121.8 0.3 convolution_convert_fusion.2
  122.2 0.1 fusion.11
  122.3 0.3 concatenate.34
  122.7 15.9 %all_to_all.63 = bf16[4,64,1792]{2,1,0:T(8,128)(2,1)S(1)} all-to-all(bf16[4,64,1792]{2,1,0:T(8,128)(2,1)S(1)} %concatenate.34), channel_id=1, replica_groups=mesh['x'=4,'z'=16,'y'=4,'core'=2] {'x'}, dimensions={0} | all-to-all | bytes 1835008 | tf_op jit(solution)/shard_map/all_to_all | solution.py:33
  138.6 0.2 reduce_sum.127
  138.7 0.1 reshape.256
  138.8 20.7 %all_to_all.64 = bf16[16,4,1792]{2,1,0:T(4,128)(2,1)S(1)} all-to-all(bf16[16,4,1792]{2,1,0:T(4,128)(2,1)S(1)} %reshape.256), channel_id=1, replica_groups=mesh['x'=4,'z'=16,'y'=4,'core'=2] {'z'}, dimensions={0} | all-to-all | bytes 458752 | tf_op jit(solution)/shard_map/all_to_all | solution.py:33
  159.5 0.1 convert_reduce_fusion.3
  159.6 0.2 fusion.19
  159.8 0.1 fusion.18
  159.9 21.4 %all_to_all.65 = bf16[16,4,832]{2,1,0:T(4,128)(2,1)S(1)} all-to-all(bf16[16,4,832]{2,1,0:T(4,128)(2,1)S(1)} %broadcast_in_dim.53), channel_id=1, replica_groups=mesh['x'=4,'z'=16,'y'=4,'core'=2] {'z'}, dimensions={0} | all-to-all | bytes 212992 | tf_op jit(solution)/shard_map/all_to_all | solution.py:33
  181.5 9.0 %all_to_all.66 = bf16[4,64,832]{2,1,0:T(8,128)(2,1)S(1)} all-to-all(bf16[4,64,832]{2,1,0:T(8,128)(2,1)S(1)} %broadcast_in_dim.55), channel_id=1, replica_groups=mesh['x'=4,'z'=16,'y'=4,'core'=2] {'x'}, dimensions={0} | all-to-all | bytes 851968 | tf_op jit(solution)/shard_map/all_to_all | solution.py:33
  190.4 0.3 convolution_convert_fusion.3
  190.7 7.9 %all_to_all.67 = bf16[2,128,256]{2,1,0:T(8,128)(2,1)S(1)} all-to-all(bf16[2,128,256]{2,1,0:T(8,128)(2,1)S(1)} %bitcast.93), channel_id=1, replica_groups=mesh['x'=4,'z'=16,'y'=4,'core'=2] {'core'}, dimensions={0} | all-to-all | bytes 262144 | tf_op jit(solution)/shard_map/all_to_all | solution.py:33
  198.7 0.7 broadcast_in_dim.96
  199.4 3.4 %all-to-all-start.11 = ((bf16[4,128,256]{2,1,0:T(8,128)(2,1)}), bf16[4,128,256]{2,1,0:T(8,128)(2,1)S(1)}, u32[]{:S(2)}, u32[]{:S(2)}) async-start(bf16[4,128,256]{2,1,0:T(8,128)(2,1)} %broadcast_in_dim.96), calls=%async_computation.11 | async-start | bytes 524288 | tf_op jit(solution)/shard_map/all_to_all | solution.py:33
  202.8 0.1 maximum_bitcast_fusion
  202.9 0.6 copy.116
  203.5 5.4 %all-to-all-done.11 = bf16[4,128,256]{2,1,0:T(8,128)(2,1)S(1)} async-done(((bf16[4,128,256]{2,1,0:T(8,128)(2,1)}), bf16[4,128,256]{2,1,0:T(8,128)(2,1)S(1)}, u32[]{:S(2)}, u32[]{:S(2)}) %all-to-all-start.11) | async-done | bytes 262176 | tf_op jit(solution)/shard_map/all_to_all | solution.py:33
  209.0 3.0 %all_gather.7 = bf16[256,256]{1,0:T(8,128)(2,1)S(1)} all-gather(bf16[128,256]{1,0:T(8,128)(2,1)S(1)} %add_convert_fusion), channel_id=1, replica_groups=mesh['x'=4,'z'=16,'y'=4,'core'=2] {'core'}, dimensions={0}, use_global_device_ids=true | all-gather | bytes 196608 | tf_op jit(solution)/shard_map/all_gather | solution.py:184
  212.1 0.1 copy.115
  212.2 0.7 reshape.260
  (58 shorter events, 0.8 us)
Async XLA Ops:
  0.6 2.2 %copy-start = (bf16[256,2048]{1,0:T(8,128)(2,1)S(1)}, bf16[256,2048]{1,0:T(8,128)(2,1)}, u32[]{:S(2)}) copy-start(bf16[256,2048]{1,0:T(8,128)(2,1)} %param.13) | copy-start | bytes 3145732
  0.6 2.0 copy-start.8
  2.8 0.9 copy-start.6
  21.2 19.6 %copy-start.9 = (s32[2]{0:T(128)S(1)}, s32[2]{0:T(128)}, u32[]{:S(2)}) copy-start(s32[2]{0:T(128)} %param.21) | copy-start | bytes 28
  21.3 19.7 %copy-start.7 = (s32[2]{0:T(128)S(1)}, s32[2]{0:T(128)}, u32[]{:S(2)}) copy-start(s32[2]{0:T(128)} %param.20) | copy-start | bytes 28
  21.4 33.5 %copy-start.5 = (bf16[2,768,1,256]{3,1,2,0:T(8,128)(2,1)S(1)}, bf16[2,768,1,256]{3,1,2,0:T(8,128)(2,1)}, u32[]{:S(2)}) copy-start(bf16[2,768,1,256]{3,1,2,0:T(8,128)(2,1)} %param.19) | copy-start | bytes 2359300
  22.3 31.8 %all-to-all-start.1 = ((bf16[16,4,2432]{2,1,0:T(4,128)(2,1)}), bf16[16,4,2432]{2,1,0:T(4,128)(2,1)S(1)}, u32[]{:S(2)}, u32[]{:S(2)}) async-start(bf16[16,4,2432]{2,1,0:T(4,128)(2,1)} %copy.107), calls=%async_computation.1 | async-start | bytes 622592 | tf_op jit(solution)/shard_map/all_to_all | solution.py:33
  82.0 3.7 %copy-start.1 = (bf16[2,128,256]{2,1,0:T(8,128)(2,1)S(1)}, bf16[2,128,256]{2,1,0:T(8,128)(2,1)}, u32[]{:S(2)}) copy-start(bf16[2,128,256]{2,1,0:T(8,128)(2,1)} %param.11) | copy-start | bytes 393220
  82.0 3.9 %copy-start.10 = (bf16[256]{0:T(256)(128)(2,1)S(1)}, bf16[256]{0:T(256)(128)(2,1)}, u32[]{:S(2)}) copy-start(bf16[256]{0:T(256)(128)(2,1)} %param.16) | copy-start | bytes 1540
  82.0 13.4 %copy-start.2 = (bf16[2048,256]{1,0:T(8,128)(2,1)S(1)}, bf16[2048,256]{1,0:T(8,128)(2,1)}, u32[]{:S(2)}) copy-start(bf16[2048,256]{1,0:T(8,128)(2,1)} %param.15) | copy-start | bytes 3145732
  82.0 13.4 %all-to-all-start.3 = ((bf16[4,64,2048]{2,1,0:T(8,128)(2,1)}), bf16[4,64,2048]{2,1,0:T(8,128)(2,1)S(1)}, u32[]{:S(2)}, u32[]{:S(2)}) async-start(bf16[4,64,2048]{2,1,0:T(8,128)(2,1)} %broadcast_in_dim.51), calls=%async_computation.3 | async-start | bytes 2097152 | tf_op jit(solution)/shard_map/all_to_all | solution.py:33
  95.8 16.4 %copy-start.3 = (bf16[256,2,832]{0,2,1:T(8,128)(2,1)S(1)}, bf16[256,2,832]{0,2,1:T(8,128)(2,1)}, u32[]{:S(2)}) copy-start(bf16[256,2,832]{0,2,1:T(8,128)(2,1)} %param.17) | copy-start | bytes 2555908
  108.1 10.0 %all-to-all-start.5 = ((bf16[4,128,256]{2,1,0:T(8,128)(2,1)}), bf16[4,128,256]{2,1,0:T(8,128)(2,1)S(1)}, u32[]{:S(2)}, u32[]{:S(2)}) async-start(bf16[4,128,256]{2,1,0:T(8,128)(2,1)} %broadcast_in_dim.52), calls=%async_computation.5 | async-start | bytes 524288 | tf_op jit(solution)/shard_map/all_to_all | solution.py:33
  159.5 30.9 %copy-start.4 = (bf16[832,256]{1,0:T(8,128)(2,1)S(1)}, bf16[832,256]{1,0:T(8,128)(2,1)}, u32[]{:S(2)}) copy-start(bf16[832,256]{1,0:T(8,128)(2,1)} %param.18) | copy-start | bytes 1277956
  199.4 9.5 %all-to-all-start.11 = ((bf16[4,128,256]{2,1,0:T(8,128)(2,1)}), bf16[4,128,256]{2,1,0:T(8,128)(2,1)S(1)}, u32[]{:S(2)}, u32[]{:S(2)}) async-start(bf16[4,128,256]{2,1,0:T(8,128)(2,1)} %broadcast_in_dim.96), calls=%async_computation.11 | async-start | bytes 524288 | tf_op jit(solution)/shard_map/all_to_all | solution.py:33

commit v5 on v4

--- a/solution.py
+++ b/solution.py
@@ -1,6 +1,8 @@
 import jax
 import jax.numpy as jnp
 from jax import lax
+from jax.experimental import pallas as pl
+from jax.experimental.pallas import tpu as pltpu
 from jax.sharding import Mesh, PartitionSpec as P
 
 D = 16384
@@ -43,15 +45,109 @@
     return exchange(jnp.broadcast_to(block[None], (size,) + block.shape), axis)
 
 
-def group_sum(terms, base):
-    rows, columns = terms.shape
-    pair = sum_over(terms, "core", CORES).astype(jnp.bfloat16)
-    return base + jnp.sum(collect(pair, "y", YS).astype(jnp.float32), axis=0)
-
-
-def lane_squares(values, lanes):
-    squares = values * values
-    return sum(squares[:, at : at + lanes] for at in range(0, values.shape[1], lanes))
+def group_terms(terms):
+    total = jnp.sum(collect(terms.astype(jnp.bfloat16), "y", YS).astype(jnp.float32), axis=0)
+    return lax.all_gather(total.astype(jnp.bfloat16), "core", axis=0, tiled=False)
+
+
+def to_row_order(count, back):
+    dims = (count, count)
+    mixed = lax.broadcasted_iota(jnp.int32, dims, 1 if back else 0)
+    plain = lax.broadcasted_iota(jnp.int32, dims, 0 if back else 1)
+    source = (mixed >> 2) * 2 + (mixed & 1) + ((mixed >> 1) & 1) * (count // 2)
+    return jnp.where(source == plain, 1.0, 0.0).astype(jnp.bfloat16)
+
+
+def first_kernel(inputs_ref, gain_ref, query_ref, keyval_ref, terms_ref, rows_ref):
+    group = inputs_ref.shape[1] // XS
+    order = to_row_order(2 * group, False)
+    gain = gain_ref[...].astype(jnp.float32)
+    queries = query_ref.shape[1]
+    keyvals = keyval_ref.shape[1]
+    scaled = []
+    for at in range(XS):
+        block = jnp.concatenate([inputs_ref[step, group * at : group * (at + 1)] for step in range(2)], axis=0)
+        values = jnp.dot(order, block, preferred_element_type=jnp.float32)
+        rows_ref[2 * group * at : 2 * group * (at + 1)] = values.astype(jnp.bfloat16)
+        squares = values * values
+        terms_ref[at, :, queries + keyvals :] = (squares[:, :128] + squares[:, 128:]).astype(jnp.bfloat16)
+        scaled.append((values * gain).astype(jnp.bfloat16))
+    scaled = jnp.concatenate(scaled, axis=0)
+    for weights_ref, base in ((query_ref, 0), (keyval_ref, queries)):
+        for start in range(0, weights_ref.shape[1], 256):
+            product = jnp.dot(scaled, weights_ref[:, start : start + 256], preferred_element_type=jnp.float32)
+            product = product.astype(jnp.bfloat16).reshape(XS, 2 * group, 256)
+            terms_ref[:, :, base + start : base + start + 256] = product
+
+
+def first_terms(inputs, gain, w_query, w_keyval):
+    steps, all_rows, width = inputs.shape
+    columns = w_query.shape[1] + w_keyval.shape[1] + 128
+    return pl.pallas_call(
+        first_kernel,
+        out_shape=(
+            jax.ShapeDtypeStruct((XS, steps * all_rows // XS, columns), jnp.bfloat16),
+            jax.ShapeDtypeStruct((steps * all_rows, width), jnp.bfloat16),
+        ),
+        compiler_params=pltpu.CompilerParams(vmem_limit_bytes=24 * 1024 * 1024),
+        name="first_terms",
+    )(inputs, gain.reshape(1, width), w_query, w_keyval)
+
+
+def gateup_kernel(pair_ref, rows_ref, weights_ref, terms_ref, state_ref):
+    state = (
+        pair_ref[0].astype(jnp.float32) + pair_ref[1].astype(jnp.float32) + rows_ref[...].astype(jnp.float32)
+    )
+    state_ref[...] = state
+    squares = state * state
+    squares = squares[:, :128] + squares[:, 128:]
+    hidden = weights_ref.shape[0]
+    terms_ref[:, :, hidden:] = squares.astype(jnp.bfloat16).reshape(XS, -1, 128)
+    state = state.astype(jnp.bfloat16)
+    for start in range(0, hidden, 128):
+        product = lax.dot_general(
+            state,
+            weights_ref[start : start + 128],
+            (((1,), (1,)), ((), ())),
+            preferred_element_type=jnp.float32,
+        )
+        terms_ref[:, :, start : start + 128] = product.astype(jnp.bfloat16).reshape(XS, -1, 128)
+
+
+def gateup_terms(pair, rows, weights):
+    count, width = rows.shape
+    return pl.pallas_call(
+        gateup_kernel,
+        out_shape=(
+            jax.ShapeDtypeStruct((XS, count // XS, weights.shape[0] + 128), jnp.bfloat16),
+            jax.ShapeDtypeStruct((count, width), jnp.float32),
+        ),
+        compiler_params=pltpu.CompilerParams(vmem_limit_bytes=24 * 1024 * 1024),
+        name="gateup_terms",
+    )(pair, rows, weights)
+
+
+def last_kernel(pair_ref, state_ref, outputs_ref):
+    group = outputs_ref.shape[1] // XS
+    order = to_row_order(2 * group, True)
+    for at in range(XS):
+        here = slice(2 * group * at, 2 * group * (at + 1))
+        values = (
+            pair_ref[0, here].astype(jnp.float32) + pair_ref[1, here].astype(jnp.float32) + state_ref[here]
+        )
+        values = jnp.dot(order, values.astype(jnp.bfloat16), preferred_element_type=jnp.float32)
+        values = values.astype(jnp.bfloat16)
+        for step in range(2):
+            outputs_ref[step, group * at : group * (at + 1)] = values[group * step : group * (step + 1)]
+
+
+def last_sum(pair, state, steps):
+    count, width = state.shape
+    return pl.pallas_call(
+        last_kernel,
+        out_shape=jax.ShapeDtypeStruct((steps, count // steps, width), jnp.bfloat16),
+        name="last_sum",
+    )(pair, state)
 
 
 def attend(queries, kv_cache, lengths, fresh_keys, fresh_values, score_scale):
@@ -107,27 +203,11 @@
     squares_at = keyvals_at + 2 * head_dim
     rows = steps * all_rows
     x_rows = rows // XS
-    half = rows // CORES
     gateup = w_gateup.transpose(1, 2, 0).astype(jnp.float32) * ffn_gain.astype(jnp.float32)
-    gateup = gateup.astype(jnp.bfloat16)
-
-    current = (
-        inputs.reshape(steps, XS, all_rows // XS, local_width)
-        .transpose(1, 0, 2, 3)
-        .reshape(rows, local_width)
-        .astype(jnp.float32)
-    )
-    scaled = (current * attn_gain.astype(jnp.float32)).astype(jnp.bfloat16)
-    terms = jnp.concatenate(
-        [
-            jnp.dot(scaled, w_query, preferred_element_type=jnp.float32),
-            jnp.dot(scaled, keyval_weight, preferred_element_type=jnp.float32),
-            lane_squares(current, 128),
-        ],
-        axis=1,
-    )
-    sums = sum_over(terms, "x", XS).astype(jnp.bfloat16)
-    sums = sums.reshape(steps, ZS, local_rows, -1).transpose(1, 0, 2, 3).reshape(x_rows, -1)
+    gateup = gateup.astype(jnp.bfloat16).reshape(2 * local_hidden, local_width)
+
+    terms, input_rows = first_terms(inputs, attn_gain, w_query, keyval_weight)
+    sums = jnp.sum(exchange(terms, "x").astype(jnp.float32), axis=0)
     sums = sum_over(sums, "z", ZS)
     mean = jnp.sum(sums[:, squares_at:], axis=-1, keepdims=True) / D
     sums = (sums[:, :squares_at] * lax.rsqrt(mean + epsilon)).reshape(steps, local_rows, squares_at)
@@ -152,41 +232,16 @@
     attn_terms = jnp.dot(
         all_heads.reshape(rows, keyvals_at), w_out, preferred_element_type=jnp.float32
     )
-    residual = lax.dynamic_index_in_dim(
-        inputs.reshape(steps, CORES, all_rows // CORES // local_rows, local_rows, local_width),
-        lax.axis_index("core"), 1, keepdims=False,
-    )
-    residual = residual.transpose(1, 0, 2, 3).reshape(half, local_width).astype(jnp.float32)
-    state = group_sum(attn_terms, residual)
-    ffn_in = lax.all_gather(state.astype(jnp.bfloat16), "core", axis=0, tiled=True)
-    squares = ffn_in.astype(jnp.float32)
-    squares = squares * squares
-    halves = []
-    for part in range(2):
-        halves.append(
-            lax.dot_general(
-                ffn_in, gateup[part], (((1,), (1,)), ((), ())), preferred_element_type=jnp.float32
-            )
-        )
-        lanes = squares[:, 128 * part : 128 * part + 128]
-        halves.append(lanes[:, :64] + lanes[:, 64:])
-    terms = jnp.concatenate(halves, axis=1)
-    sums = sum_over(sum_over(terms, "x", XS), "z", ZS)
-    padded = local_hidden + 64
-    gate, up = sums[:, :padded], sums[:, padded:]
-    mean = jnp.sum(gate[:, local_hidden:] + up[:, local_hidden:], axis=-1, keepdims=True) / D
-    scale = lax.rsqrt(mean + epsilon)
-    activated = jax.nn.silu(gate[:, :local_hidden] * scale) * (up[:, :local_hidden] * scale)
+    terms, state = gateup_terms(group_terms(attn_terms), input_rows, gateup)
+    sums = jnp.sum(exchange(terms, "x").astype(jnp.float32), axis=0)
+    sums = sum_over(sums, "z", ZS)
+    mean = jnp.sum(sums[:, 2 * local_hidden :], axis=-1, keepdims=True) / D
+    sums = sums[:, : 2 * local_hidden] * lax.rsqrt(mean + epsilon)
+    activated = jax.nn.silu(sums[:, :local_hidden]) * sums[:, local_hidden:]
     hidden = collect(activated.astype(jnp.bfloat16), "z", ZS).reshape(x_rows, local_hidden)
     hidden = collect(hidden, "x", XS).reshape(rows, local_hidden)
     down_terms = jnp.dot(hidden, w_down, preferred_element_type=jnp.float32)
-    result = group_sum(down_terms, state).astype(jnp.bfloat16)
-    result = lax.all_gather(result, "core", axis=0, tiled=True)
-    outputs = (
-        result.reshape(XS * ZS, steps, local_rows, local_width)
-        .transpose(1, 0, 2, 3)
-        .reshape(steps, all_rows, local_width)
-    )
+    outputs = last_sum(group_terms(down_terms), state, steps)
     return (outputs, new_entries)
 
 

time: 214 us -> 208 us (0.972)
  waiting for transfers between devices: 33.6 us -> 26.1 us
  blocking collectives: 134 us -> 139 us
  starting transfers between devices: 29.7 us -> 26.2 us
  Pallas kernels: 0 us -> 3.08 us
  other arithmetic: 4.43 us -> 2.09 us
    all_gather x2, blocking collectives: 6.37 us -> 18.3 us  [group_terms(): lax.all_gather(total.astype(jnp.bfloat16), 'core', axis=0, tiled=False)]
    all_to_all x4 -> x3, waiting for transfers between devices: 33.6 us -> 26.1 us  [exchange(): return lax.all_to_all(blocks, axis, 0, 0, tiled=True)]
    all_to_all x8 -> x7, blocking collectives: 128 us -> 121 us  [exchange(): return lax.all_to_all(blocks, axis, 0, 0, tiled=True)]
    all_to_all x4 -> x3, starting transfers between devices: 29.7 us -> 26.2 us  [exchange(): return lax.all_to_all(blocks, axis, 0, 0, tiled=True)]
    unnamed x25, local copies, waits for them, and re-layouts: 1.07 us -> 4.36 us
    pallas_call x0 -> x3, Pallas kernels: none -> 3.08 us  [the longest x1 1.87 us: last_sum(): pl.pallas_call(last_kernel, out_shape=jax.ShapeDtypeStruct((steps, count...]
  transfers between devices with their start and end apart: 4 -> 3, of which waited for: 4 -> 3; matrix products, arithmetic and copies ran while one was open for 1% -> 0% of each run, Pallas kernels for 0% -> 0%
where the time goes in v5:
time: 208 us; the launch traced here: 207 us
  blocking collectives  139 us (67%)
  starting transfers between devices  26.2 us (13%)
  waiting for transfers between devices  26.1 us (13%)
  local copies, waits for them, and re-layouts  8.23 us (4%)
  Pallas kernels  3.08 us (1%)
  other arithmetic  2.09 us (1%)
    all_to_all x7, blocking collectives, exchange(): return lax.all_to_all(blocks, axis, 0, 0, tiled=True)  121 us
    all_to_all x3, starting transfers between devices, exchange(): return lax.all_to_all(blocks, axis, 0, 0, tiled=True)  26.2 us
    all_to_all x3, waiting for transfers between devices, exchange(): return lax.all_to_all(blocks, axis, 0, 0, tiled=True)  26.1 us
    all_gather x2, blocking collectives, group_terms(): lax.all_gather(total.astype(jnp.bfloat16), 'core', axis=0, tiled=False)  18.3 us
    unnamed x25, local copies, waits for them, and re-layouts  4.36 us
  transfers between devices with their start and end apart: 3, of which 3 were waited for; matrix products, arithmetic and copies ran while one was open for 0% of the time, Pallas kernels for 0%

profile of v5, /device:TPU:1, one launch (start us, length us, event | category | flops | bytes accessed | tf_op | source)
XLA Modules:
  0.0 207.3 jit_solution(12854105849709555024)
XLA Ops:
  0.6 0.0 copy-start
  0.6 0.7 reshape.193.gain_ref
  1.4 1.2 copy-done.1
  2.6 0.9 copy-done.3
  3.5 0.9 copy-done.4
  4.4 0.6 first_terms.1
  5.0 17.0 %all_to_all.50 = bf16[4,64,2432]{2,1,0:T(8,128)(2,1)S(1)} all-to-all(bf16[4,64,2432]{2,1,0:T(8,128)(2,1)S(1)} %get-tuple-element.6), channel_id=1, replica_groups=mesh['x'=4,'z'=16,'y'=4,'core'=2] {'x'}, dimensions={0} | all-to-all | bytes 2490368 | tf_op jit(solution)/shard_map/all_to_all | solution.py:35
  22.1 0.2 reduce_sum.102
  22.3 0.0 copy-start.7
  22.3 0.8 reshape.195
  23.1 18.5 %all-to-all-start.1 = ((bf16[16,4,2432]{2,1,0:T(4,128)(2,1)}), bf16[16,4,2432]{2,1,0:T(4,128)(2,1)S(1)}, u32[]{:S(2)}, u32[]{:S(2)}) async-start(bf16[16,4,2432]{2,1,0:T(4,128)(2,1)} %reshape.195), calls=%async_computation.1 | async-start | bytes 622592 | tf_op jit(solution)/shard_map/all_to_all | solution.py:35
  41.7 0.1 add_convert_fusion.2
  41.7 0.1 iota_compare_fusion
  41.8 13.1 %all-to-all-done.1 = bf16[16,4,2432]{2,1,0:T(4,128)(2,1)S(1)} async-done(((bf16[16,4,2432]{2,1,0:T(4,128)(2,1)}), bf16[16,4,2432]{2,1,0:T(4,128)(2,1)S(1)}, u32[]{:S(2)}, u32[]{:S(2)}) %all-to-all-start.1) | async-done | bytes 311328 | tf_op jit(solution)/shard_map/all_to_all | solution.py:35
  54.9 0.1 convert_reduce_fusion
  55.0 0.1 slice_reduce_fusion.1
  55.2 0.1 slice_multiply_fusion
  55.3 0.1 fusion.18
  55.4 0.1 fusion.19
  55.5 0.1 subtract_convert_fusion.1
  55.6 0.1 pad_maximum_fusion
  55.7 0.0 copy-done.7
  55.7 0.3 fusion.20
  56.0 0.2 fusion.21
  56.3 0.2 fusion.6
  56.5 0.2 fusion.3
  56.7 0.2 fusion.1
  56.9 0.1 broadcast_in_dim.49
  57.1 24.6 %all_to_all.51 = bf16[16,4,2048]{2,1,0:T(4,128)(2,1)S(1)} all-to-all(bf16[16,4,2048]{2,1,0:T(4,128)(2,1)S(1)} %broadcast_in_dim.49), channel_id=1, replica_groups=mesh['x'=4,'z'=16,'y'=4,'core'=2] {'z'}, dimensions={0} | all-to-all | bytes 524288 | tf_op jit(solution)/shard_map/all_to_all | solution.py:35
  81.6 0.1 broadcast_in_dim.50
  81.7 0.1 broadcast_in_dim.51
  81.8 12.2 %all_to_all.52 = bf16[4,64,2048]{2,1,0:T(8,128)(2,1)S(1)} all-to-all(bf16[4,64,2048]{2,1,0:T(8,128)(2,1)S(1)} %broadcast_in_dim.51), channel_id=1, replica_groups=mesh['x'=4,'z'=16,'y'=4,'core'=2] {'x'}, dimensions={0} | all-to-all | bytes 2097152 | tf_op jit(solution)/shard_map/all_to_all | solution.py:35
  94.0 0.4 convolution_convert_fusion.1
  94.4 0.0 copy-start.10
  94.4 0.0 copy-start.5
  94.5 0.8 broadcast_in_dim.52
  95.3 4.2 %all-to-all-start.4 = ((bf16[4,256,256]{2,1,0:T(8,128)(2,1)}), bf16[4,256,256]{2,1,0:T(8,128)(2,1)S(1)}, u32[]{:S(2)}, u32[]{:S(2)}) async-start(bf16[4,256,256]{2,1,0:T(8,128)(2,1)} %broadcast_in_dim.52), calls=%async_computation.4 | async-start | bytes 1048576 | tf_op jit(solution)/shard_map/all_to_all | solution.py:35
  99.5 0.0 copy-done.10
  99.5 0.2 multiply_convert_fusion
  99.6 6.8 %all-to-all-done.4 = bf16[4,256,256]{2,1,0:T(8,128)(2,1)S(1)} async-done(((bf16[4,256,256]{2,1,0:T(8,128)(2,1)}), bf16[4,256,256]{2,1,0:T(8,128)(2,1)S(1)}, u32[]{:S(2)}, u32[]{:S(2)}) %all-to-all-start.4) | async-done | bytes 524320 | tf_op jit(solution)/shard_map/all_to_all | solution.py:35
  106.4 0.1 reduce_sum.107
  106.5 11.0 %all-gather = bf16[512,256]{1,0:T(8,128)(2,1)S(1)} all-gather(bf16[256,256]{1,0:T(8,128)(2,1)S(1)} %reduce_sum.107), channel_id=2, replica_groups=mesh['x'=4,'z'=16,'y'=4,'core'=2] {'core'}, dimensions={0}, use_global_device_ids=true | all-gather | bytes 393216 | tf_op jit(solution)/shard_map/all_gather | solution.py:50
  117.4 0.6 gateup_terms.1
  118.1 0.7 copy-done.2
  118.8 15.9 %all_to_all.53 = bf16[4,64,1792]{2,1,0:T(8,128)(2,1)S(1)} all-to-all(bf16[4,64,1792]{2,1,0:T(8,128)(2,1)S(1)} %get-tuple-element.8), channel_id=1, replica_groups=mesh['x'=4,'z'=16,'y'=4,'core'=2] {'x'}, dimensions={0} | all-to-all | bytes 1835008 | tf_op jit(solution)/shard_map/all_to_all | solution.py:35
  134.6 0.2 reduce_sum.108
  134.8 0.1 reshape.202
  134.8 20.7 %all_to_all.54 = bf16[16,4,1792]{2,1,0:T(4,128)(2,1)S(1)} all-to-all(bf16[16,4,1792]{2,1,0:T(4,128)(2,1)S(1)} %reshape.202), channel_id=1, replica_groups=mesh['x'=4,'z'=16,'y'=4,'core'=2] {'z'}, dimensions={0} | all-to-all | bytes 458752 | tf_op jit(solution)/shard_map/all_to_all | solution.py:35
  155.6 0.1 convert_reduce_fusion.1
  155.6 0.1 slice_reduce_fusion
  155.8 0.1 slice_multiply_fusion.1
  155.8 0.1 fusion.10
  156.0 21.4 %all_to_all.55 = bf16[16,4,832]{2,1,0:T(4,128)(2,1)S(1)} all-to-all(bf16[16,4,832]{2,1,0:T(4,128)(2,1)S(1)} %broadcast_in_dim.53), channel_id=1, replica_groups=mesh['x'=4,'z'=16,'y'=4,'core'=2] {'z'}, dimensions={0} | all-to-all | bytes 212992 | tf_op jit(solution)/shard_map/all_to_all | solution.py:35
  177.4 0.1 broadcast_in_dim.54
  177.5 9.0 %all_to_all.56 = bf16[4,64,832]{2,1,0:T(8,128)(2,1)S(1)} all-to-all(bf16[4,64,832]{2,1,0:T(8,128)(2,1)S(1)} %broadcast_in_dim.94), channel_id=1, replica_groups=mesh['x'=4,'z'=16,'y'=4,'core'=2] {'x'}, dimensions={0} | all-to-all | bytes 851968 | tf_op jit(solution)/shard_map/all_to_all | solution.py:35
  186.5 0.3 convolution_convert_fusion
  186.8 0.8 broadcast_in_dim.95
  187.6 3.5 %all-to-all-start.9 = ((bf16[4,256,256]{2,1,0:T(8,128)(2,1)}), bf16[4,256,256]{2,1,0:T(8,128)(2,1)S(1)}, u32[]{:S(2)}, u32[]{:S(2)}) async-start(bf16[4,256,256]{2,1,0:T(8,128)(2,1)} %broadcast_in_dim.95), calls=%async_computation.9 | async-start | bytes 1048576 | tf_op jit(solution)/shard_map/all_to_all | solution.py:35
  191.1 0.1 maximum_bitcast_fusion
  191.2 0.6 copy.54
  191.8 6.2 %all-to-all-done.9 = bf16[4,256,256]{2,1,0:T(8,128)(2,1)S(1)} async-done(((bf16[4,256,256]{2,1,0:T(8,128)(2,1)}), bf16[4,256,256]{2,1,0:T(8,128)(2,1)S(1)}, u32[]{:S(2)}, u32[]{:S(2)}) %all-to-all-start.9) | async-done | bytes 524320 | tf_op jit(solution)/shard_map/all_to_all | solution.py:35
  198.0 0.1 reduce_sum.111
  198.1 7.4 %all-gather.1 = bf16[512,256]{1,0:T(8,128)(2,1)} all-gather(bf16[256,256]{1,0:T(8,128)(2,1)S(1)} %reduce_sum.111), channel_id=3, replica_groups=mesh['x'=4,'z'=16,'y'=4,'core'=2] {'core'}, dimensions={0}, use_global_device_ids=true | all-gather | bytes 393216 | tf_op jit(solution)/shard_map/all_gather | solution.py:50
  205.4 1.9 last_sum.1
  (31 shorter events, 0.3 us)
Async XLA Ops:
  0.6 93.3 %copy-start = (bf16[2048,256]{1,0:T(8,128)(2,1)S(1)}, bf16[2048,256]{1,0:T(8,128)(2,1)}, u32[]{:S(2)}) copy-start(bf16[2048,256]{1,0:T(8,128)(2,1)} %param.15) | copy-start | bytes 3145732
  1.4 1.2 copy-start.1
  2.6 0.9 copy-start.3
  3.5 0.9 copy-start.4
  22.1 19.6 %copy-start.9 = (s32[2]{0:T(128)S(1)}, s32[2]{0:T(128)}, u32[]{:S(2)}) copy-start(s32[2]{0:T(128)} %param.21) | copy-start | bytes 28
  22.1 19.7 %copy-start.8 = (s32[2]{0:T(128)S(1)}, s32[2]{0:T(128)}, u32[]{:S(2)}) copy-start(s32[2]{0:T(128)} %param.20) | copy-start | bytes 28
  22.3 33.4 %copy-start.7 = (bf16[2,768,1,256]{3,1,2,0:T(8,128)(2,1)S(1)}, bf16[2,768,1,256]{3,1,2,0:T(8,128)(2,1)}, u32[]{:S(2)}) copy-start(bf16[2,768,1,256]{3,1,2,0:T(8,128)(2,1)} %param.19) | copy-start | bytes 2359300
  23.1 31.8 %all-to-all-start.1 = ((bf16[16,4,2432]{2,1,0:T(4,128)(2,1)}), bf16[16,4,2432]{2,1,0:T(4,128)(2,1)S(1)}, u32[]{:S(2)}, u32[]{:S(2)}) async-start(bf16[16,4,2432]{2,1,0:T(4,128)(2,1)} %reshape.195), calls=%async_computation.1 | async-start | bytes 622592 | tf_op jit(solution)/shard_map/all_to_all | solution.py:35
  94.4 5.0 %copy-start.10 = (bf16[256]{0:T(256)(128)(2,1)S(1)}, bf16[256]{0:T(256)(128)(2,1)}, u32[]{:S(2)}) copy-start(bf16[256]{0:T(256)(128)(2,1)} %param.16) | copy-start | bytes 1540
  94.4 5.0 %copy-start.5 = (bf16[256,2,832]{0,2,1:T(8,128)(2,1)S(1)}, bf16[256,2,832]{0,2,1:T(8,128)(2,1)}, u32[]{:S(2)}) copy-start(bf16[256,2,832]{0,2,1:T(8,128)(2,1)} %param.17) | copy-start | bytes 2555908
  95.3 11.1 %all-to-all-start.4 = ((bf16[4,256,256]{2,1,0:T(8,128)(2,1)}), bf16[4,256,256]{2,1,0:T(8,128)(2,1)S(1)}, u32[]{:S(2)}, u32[]{:S(2)}) async-start(bf16[4,256,256]{2,1,0:T(8,128)(2,1)} %broadcast_in_dim.52), calls=%async_computation.4 | async-start | bytes 1048576 | tf_op jit(solution)/shard_map/all_to_all | solution.py:35
  118.1 0.7 copy-start.2
  155.6 30.9 %copy-start.6 = (bf16[832,256]{1,0:T(8,128)(2,1)S(1)}, bf16[832,256]{1,0:T(8,128)(2,1)}, u32[]{:S(2)}) copy-start(bf16[832,256]{1,0:T(8,128)(2,1)} %param.18) | copy-start | bytes 1277956
  187.6 10.4 %all-to-all-start.9 = ((bf16[4,256,256]{2,1,0:T(8,128)(2,1)}), bf16[4,256,256]{2,1,0:T(8,128)(2,1)S(1)}, u32[]{:S(2)}, u32[]{:S(2)}) async-start(bf16[4,256,256]{2,1,0:T(8,128)(2,1)} %broadcast_in_dim.95), calls=%async_computation.9 | async-start | bytes 1048576 | tf_op jit(solution)/shard_map/all_to_all | solution.py:35

commit v6 on v5

--- a/solution.py
+++ b/solution.py
@@ -1,3 +1,5 @@
+import functools
+
 import jax
 import jax.numpy as jnp
 from jax import lax
@@ -15,6 +17,8 @@
 WIDE = ("x", "z")
 MP = ("y", "core")
 XS, ZS, YS, CORES = 4, 16, 4, 2
+EARLY = 896
+EARLY_CUT, LATE_CUT, DOWN_CUT = 512, 384, 384
 
 
 def rotate(vectors, offsets):
@@ -45,9 +49,32 @@
     return exchange(jnp.broadcast_to(block[None], (size,) + block.shape), axis)
 
 
-def group_terms(terms):
-    total = jnp.sum(collect(terms.astype(jnp.bfloat16), "y", YS).astype(jnp.float32), axis=0)
+def group_terms(blocks):
+    shape = blocks.shape
+    copies = jnp.broadcast_to(blocks[:, None], (XS, YS) + shape[1:])
+    return exchange(copies.reshape((XS * YS,) + shape[1:]), ("x", "y"))
+
+
+def pair_terms(received):
+    blocks = received.reshape((XS, YS) + received.shape[1:])
+    total = jnp.sum(blocks.astype(jnp.float32), axis=1)
     return lax.all_gather(total.astype(jnp.bfloat16), "core", axis=0, tiled=False)
+
+
+def shift(block, by):
+    return lax.ppermute(block, "x", [(at, (at + by) % XS) for at in range(XS)])
+
+
+def both_ways(block):
+    return shift(block, -1), shift(block, 1)
+
+
+def far_block(after, before, cut):
+    return shift(before[:cut], 1), shift(after[cut:], -1)
+
+
+def together(*values):
+    return lax.optimization_barrier(values)
 
 
 def to_row_order(count, back):
@@ -89,65 +116,96 @@
             jax.ShapeDtypeStruct((XS, steps * all_rows // XS, columns), jnp.bfloat16),
             jax.ShapeDtypeStruct((steps * all_rows, width), jnp.bfloat16),
         ),
-        compiler_params=pltpu.CompilerParams(vmem_limit_bytes=24 * 1024 * 1024),
+        compiler_params=pltpu.CompilerParams(vmem_limit_bytes=56 * 1024 * 1024),
         name="first_terms",
     )(inputs, gain.reshape(1, width), w_query, w_keyval)
 
 
-def gateup_kernel(pair_ref, rows_ref, weights_ref, terms_ref, state_ref):
-    state = (
-        pair_ref[0].astype(jnp.float32) + pair_ref[1].astype(jnp.float32) + rows_ref[...].astype(jnp.float32)
-    )
-    state_ref[...] = state
-    squares = state * state
-    squares = squares[:, :128] + squares[:, 128:]
-    hidden = weights_ref.shape[0]
-    terms_ref[:, :, hidden:] = squares.astype(jnp.bfloat16).reshape(XS, -1, 128)
-    state = state.astype(jnp.bfloat16)
+def gateup_kernel(cuts, at_ref, pair_ref, *refs):
+    pieces, (terms_ref, state_ref) = refs[:-2], refs[-2:]
+    total = 0.0
+    states = []
+    for step in range(XS):
+        block = (at_ref[0] + step) & (XS - 1)
+        state = pair_ref[0, block].astype(jnp.float32) + pair_ref[1, block].astype(jnp.float32)
+        state_ref[step] = state
+        total += state * state
+        states.append(state.astype(jnp.bfloat16))
+    hidden = terms_ref.shape[1] - 128
+    terms_ref[:, hidden:] = (total[:, :128] + total[:, 128:]).astype(jnp.bfloat16)
     for start in range(0, hidden, 128):
-        product = lax.dot_general(
-            state,
-            weights_ref[start : start + 128],
-            (((1,), (1,)), ((), ())),
-            preferred_element_type=jnp.float32,
-        )
-        terms_ref[:, :, start : start + 128] = product.astype(jnp.bfloat16).reshape(XS, -1, 128)
-
-
-def gateup_terms(pair, rows, weights):
-    count, width = rows.shape
+        product = 0.0
+        for (step, base), piece_ref in zip(cuts, pieces):
+            if base <= start < base + piece_ref.shape[0]:
+                product += lax.dot_general(
+                    states[step],
+                    piece_ref[start - base : start - base + 128],
+                    (((1,), (1,)), ((), ())),
+                    preferred_element_type=jnp.float32,
+                )
+        terms_ref[:, start : start + 128] = product.astype(jnp.bfloat16)
+
+
+def in_vmem(count):
+    return [pl.BlockSpec(memory_space=pltpu.VMEM)] * count
+
+
+def gateup_terms(at, pair, hidden, cuts, pieces):
+    _, blocks, count, width = pair.shape
     return pl.pallas_call(
-        gateup_kernel,
+        functools.partial(gateup_kernel, cuts),
         out_shape=(
-            jax.ShapeDtypeStruct((XS, count // XS, weights.shape[0] + 128), jnp.bfloat16),
-            jax.ShapeDtypeStruct((count, width), jnp.float32),
+            jax.ShapeDtypeStruct((count, hidden + 128), jnp.bfloat16),
+            jax.ShapeDtypeStruct((blocks, count, width), jnp.float32),
         ),
+        in_specs=[pl.BlockSpec(memory_space=pltpu.SMEM)] + in_vmem(1 + len(pieces)),
         compiler_params=pltpu.CompilerParams(vmem_limit_bytes=24 * 1024 * 1024),
         name="gateup_terms",
-    )(pair, rows, weights)
-
-
-def last_kernel(pair_ref, state_ref, outputs_ref):
+    )(at, pair, *pieces)
+
+
+def down_kernel(cuts, at_ref, hidden_ref, state_ref, *refs):
+    pieces, terms_ref = refs[:-1], refs[-1]
+    for step in range(XS):
+        product = state_ref[step] * (1.0 / (YS * CORES))
+        for (owner, base), piece_ref in zip(cuts, pieces):
+            if owner == step:
+                product += jnp.dot(
+                    hidden_ref[:, base : base + piece_ref.shape[0]],
+                    piece_ref[...],
+                    preferred_element_type=jnp.float32,
+                )
+        terms_ref[(at_ref[0] + step) & (XS - 1)] = product.astype(jnp.bfloat16)
+
+
+def down_terms(at, hidden, state, cuts, pieces):
+    return pl.pallas_call(
+        functools.partial(down_kernel, cuts),
+        out_shape=jax.ShapeDtypeStruct(state.shape, jnp.bfloat16),
+        in_specs=[pl.BlockSpec(memory_space=pltpu.SMEM)] + in_vmem(2 + len(pieces)),
+        compiler_params=pltpu.CompilerParams(vmem_limit_bytes=24 * 1024 * 1024),
+        name="down_terms",
+    )(at, hidden, state, *pieces)
+
+
+def last_kernel(pair_ref, outputs_ref):
     group = outputs_ref.shape[1] // XS
     order = to_row_order(2 * group, True)
     for at in range(XS):
-        here = slice(2 * group * at, 2 * group * (at + 1))
-        values = (
-            pair_ref[0, here].astype(jnp.float32) + pair_ref[1, here].astype(jnp.float32) + state_ref[here]
-        )
+        values = pair_ref[0, at].astype(jnp.float32) + pair_ref[1, at].astype(jnp.float32)
         values = jnp.dot(order, values.astype(jnp.bfloat16), preferred_element_type=jnp.float32)
         values = values.astype(jnp.bfloat16)
         for step in range(2):
             outputs_ref[step, group * at : group * (at + 1)] = values[group * step : group * (step + 1)]
 
 
-def last_sum(pair, state, steps):
-    count, width = state.shape
+def last_sum(pair, steps):
+    _, blocks, count, width = pair.shape
     return pl.pallas_call(
         last_kernel,
-        out_shape=jax.ShapeDtypeStruct((steps, count // steps, width), jnp.bfloat16),
+        out_shape=jax.ShapeDtypeStruct((steps, blocks * count // steps, width), jnp.bfloat16),
         name="last_sum",
-    )(pair, state)
+    )(pair)
 
 
 def attend(queries, kv_cache, lengths, fresh_keys, fresh_values, score_scale):
@@ -203,12 +261,20 @@
     squares_at = keyvals_at + 2 * head_dim
     rows = steps * all_rows
     x_rows = rows // XS
-    gateup = w_gateup.transpose(1, 2, 0).astype(jnp.float32) * ffn_gain.astype(jnp.float32)
-    gateup = gateup.astype(jnp.bfloat16).reshape(2 * local_hidden, local_width)
+    gateup = w_gateup.transpose(1, 2, 0).reshape(2 * local_hidden, local_width)
+    gain = ffn_gain.astype(jnp.float32)
+    early = (gateup[:EARLY].astype(jnp.float32) * gain).astype(jnp.bfloat16)
+    late = (gateup[EARLY:].astype(jnp.float32) * gain).astype(jnp.bfloat16)
 
     terms, input_rows = first_terms(inputs, attn_gain, w_query, keyval_weight)
-    sums = jnp.sum(exchange(terms, "x").astype(jnp.float32), axis=0)
-    sums = sum_over(sums, "z", ZS)
+    sums = jnp.sum(exchange(terms, "x").astype(jnp.float32), axis=0).astype(jnp.bfloat16)
+    sums, early = together(sums, early)
+    early_after, early_before = both_ways(early)
+    sums = exchange(sums.reshape(ZS, -1, sums.shape[1]), "z")
+    sums, early_after, early_before, late = together(sums, early_after, early_before, late)
+    early_far = far_block(early_after, early_before, EARLY_CUT)
+    late_after, late_before = both_ways(late)
+    sums = jnp.sum(sums.astype(jnp.float32), axis=0)
     mean = jnp.sum(sums[:, squares_at:], axis=-1, keepdims=True) / D
     sums = (sums[:, :squares_at] * lax.rsqrt(mean + epsilon)).reshape(steps, local_rows, squares_at)
     offsets = positions[None, :] + jnp.arange(steps)[:, None]
@@ -228,20 +294,48 @@
     )
     heads = mixed.astype(jnp.bfloat16).transpose(1, 0, 2, 3).reshape(steps * local_rows, keyvals_at)
 
-    all_heads = collect(collect(heads, "z", ZS).reshape(x_rows, keyvals_at), "x", XS)
-    attn_terms = jnp.dot(
-        all_heads.reshape(rows, keyvals_at), w_out, preferred_element_type=jnp.float32
-    )
-    terms, state = gateup_terms(group_terms(attn_terms), input_rows, gateup)
-    sums = jnp.sum(exchange(terms, "x").astype(jnp.float32), axis=0)
-    sums = sum_over(sums, "z", ZS)
+    all_heads = collect(heads, "z", ZS)
+    all_heads, late_after, late_before, *early_far = together(
+        all_heads, late_after, late_before, *early_far
+    )
+    all_heads = collect(all_heads.reshape(x_rows, keyvals_at), "x", XS).reshape(rows, keyvals_at)
+    attn_terms = jnp.dot(all_heads, w_out, preferred_element_type=jnp.float32) + (
+        input_rows.astype(jnp.float32) * (1.0 / (YS * CORES))
+    )
+    attn_terms = attn_terms.astype(jnp.bfloat16).reshape(XS, x_rows, local_width)
+    attn_terms, late_after, late_before = together(attn_terms, late_after, late_before)
+    late_far = far_block(late_after, late_before, LATE_CUT)
+    received = group_terms(attn_terms)
+    received, *late_far = together(received, *late_far)
+    at = lax.axis_index("x")[None]
+    cuts = ((0, 0), (0, EARLY), (1, 0), (1, EARLY), (3, 0), (3, EARLY))
+    cuts += ((2, 0), (2, EARLY_CUT), (2, EARLY), (2, EARLY + LATE_CUT))
+    terms, state = gateup_terms(
+        at,
+        pair_terms(received),
+        2 * local_hidden,
+        cuts,
+        (early, late, early_after, late_after, early_before, late_before, *early_far, *late_far),
+    )
+    terms, w_down = together(terms, w_down)
+    down_after, down_before = both_ways(w_down)
+    sums = exchange(terms.reshape(ZS, -1, terms.shape[1]), "z")
+    sums, down_after, down_before = together(sums, down_after, down_before)
+    down_far = far_block(down_after, down_before, DOWN_CUT)
+    sums = jnp.sum(sums.astype(jnp.float32), axis=0)
     mean = jnp.sum(sums[:, 2 * local_hidden :], axis=-1, keepdims=True) / D
     sums = sums[:, : 2 * local_hidden] * lax.rsqrt(mean + epsilon)
     activated = jax.nn.silu(sums[:, :local_hidden]) * sums[:, local_hidden:]
-    hidden = collect(activated.astype(jnp.bfloat16), "z", ZS).reshape(x_rows, local_hidden)
-    hidden = collect(hidden, "x", XS).reshape(rows, local_hidden)
-    down_terms = jnp.dot(hidden, w_down, preferred_element_type=jnp.float32)
-    outputs = last_sum(group_terms(down_terms), state, steps)
+    hidden = collect(activated.astype(jnp.bfloat16), "z", ZS)
+    hidden, *down_far = together(hidden, *down_far)
+    blocks = down_terms(
+        at,
+        hidden.reshape(x_rows, local_hidden),
+        state,
+        ((0, 0), (1, 0), (3, 0), (2, 0), (2, DOWN_CUT)),
+        (w_down, down_after, down_before, *down_far),
+    )
+    outputs = last_sum(pair_terms(group_terms(blocks)), steps)
     return (outputs, new_entries)
 
 

time: 208 us -> 227 us (1.091)
  blocking collectives: 139 us -> 30.9 us
  starting transfers between devices: 26.2 us -> 109 us
  waiting for transfers between devices: 26.1 us -> 50.3 us
  local copies, waits for them, and re-layouts: 8.23 us -> 17.8 us
  Pallas kernels: 3.08 us -> 7.5 us
  other arithmetic: 2.09 us -> 5.02 us
    all_to_all x7 -> x1, blocking collectives: 121 us -> 16 us  [exchange(): return lax.all_to_all(blocks, axis, 0, 0, tiled=True)]
    all_to_all x3 -> x7, starting transfers between devices: 26.2 us -> 69 us  [exchange(): return lax.all_to_all(blocks, axis, 0, 0, tiled=True)]
    ppermute x0 -> x12, starting transfers between devices: none -> 40.1 us  [shift(): return lax.ppermute(block, 'x', [(at, (at + by) % XS) for at in range(XS)])]
    ppermute x0 -> x12, waiting for transfers between devices: none -> 31.7 us  [shift(): return lax.ppermute(block, 'x', [(at, (at + by) % XS) for at in range(XS)])]
    all_to_all x3 -> x7, waiting for transfers between devices: 26.1 us -> 18.7 us  [exchange(): return lax.all_to_all(blocks, axis, 0, 0, tiled=True)]
    all_gather x2, blocking collectives: 18.3 us -> 14.9 us  [pair_terms(): lax.all_gather(total.astype(jnp.bfloat16), 'core', axis=0, tiled=False)]
    unnamed x25 -> x33, local copies, waits for them, and re-layouts: 4.36 us -> 7.03 us
    pallas_call x1, Pallas kernels: 0.6 us -> 2.99 us  [first_terms(): pl.pallas_call(first_kernel, out_shape=(jax.ShapeDtypeStruct((XS, steps *...]
  transfers between devices with their start and end apart: 3 -> 19, of which waited for: 3 -> 10; matrix products, arithmetic and copies ran while one was open for 0% -> 2% of each run, Pallas kernels for 0% -> 0%
where the time goes in v6:
time: 227 us; the launch traced here: 225 us
  starting transfers between devices  109 us (48%)
  waiting for transfers between devices  50.3 us (22%)
  blocking collectives  30.9 us (14%)
  local copies, waits for them, and re-layouts  17.8 us (8%)
  Pallas kernels  7.5 us (3%)
  other arithmetic  5.02 us (2%)
  matrix products  3.41 us (2%)
    all_to_all x7, starting transfers between devices, exchange(): return lax.all_to_all(blocks, axis, 0, 0, tiled=True)  69 us
    ppermute x12, starting transfers between devices, shift(): return lax.ppermute(block, 'x', [(at, (at + by) % XS) for at in range(XS)])  40.1 us
    ppermute x12, waiting for transfers between devices, shift(): return lax.ppermute(block, 'x', [(at, (at + by) % XS) for at in range(XS)])  31.7 us
    all_to_all x7, waiting for transfers between devices, exchange(): return lax.all_to_all(blocks, axis, 0, 0, tiled=True)  18.7 us
    all_to_all x1, blocking collectives, exchange(): return lax.all_to_all(blocks, axis, 0, 0, tiled=True)  16 us
    all_gather x2, blocking collectives, pair_terms(): lax.all_gather(total.astype(jnp.bfloat16), 'core', axis=0, tiled=False)  14.9 us
    unnamed x33, local copies, waits for them, and re-layouts  7.03 us
  transfers between devices with their start and end apart: 19, of which 10 were waited for; matrix products, arithmetic and copies ran while one was open for 2% of the time, Pallas kernels for 0%

profile of v6, /device:TPU:1, one launch (start us, length us, event | category | flops | bytes accessed | tf_op | source)
XLA Modules:
  0.0 225.1 jit_solution(13470104612511007733)
XLA Ops:
  0.6 1.3 reshape.207.gain_ref
  2.0 3.0 %first_terms.1 = (bf16[4,64,2432]{2,1,0:T(8,128)(2,1)}, bf16[256,256]{1,0:T(8,128)(2,1)}) custom-call(bf16[2,128,256]{2,1,0:T(8,128)(2,1)} %inputs_ref.1, bf16[1,256]{1,0:T(2,128)(2,1)} %reshape.207.gain_ref, bf16[256,2048]{1,0:T(8,128)(2,1)} %query_ref.1, bf16[256,256]{1,0:T(8,128)(2,1)} %bitcast.48), custom_call_target="tpu_custom_call" | custom-call | tf_op jit(solution)/shard_map/first_terms/pallas_call | solution.py:113
  4.9 5.0 %all-to-all-start = ((bf16[4,64,2432]{2,1,0:T(8,128)(2,1)}), bf16[4,64,2432]{2,1,0:T(8,128)(2,1)S(1)}, u32[]{:S(2)}, u32[]{:S(2)}) async-start(bf16[4,64,2432]{2,1,0:T(8,128)(2,1)} %get-tuple-element.31), calls=%async_computation | async-start | bytes 2490368 | tf_op jit(solution)/shard_map/all_to_all | solution.py:39
  9.9 1.1 multiply_convert_fusion.refs_0_
  11.1 10.3 %all-to-all-done = bf16[4,64,2432]{2,1,0:T(8,128)(2,1)S(1)} async-done(((bf16[4,64,2432]{2,1,0:T(8,128)(2,1)}), bf16[4,64,2432]{2,1,0:T(8,128)(2,1)S(1)}, u32[]{:S(2)}, u32[]{:S(2)}) %all-to-all-start) | async-done | bytes 1245216 | tf_op jit(solution)/shard_map/all_to_all | solution.py:39
  21.3 0.2 reduce_sum.90
  21.6 0.8 reshape.210
  22.3 19.8 %all-to-all-start.1 = ((bf16[16,4,2432]{2,1,0:T(4,128)(2,1)}), bf16[16,4,2432]{2,1,0:T(4,128)(2,1)S(1)}, u32[]{:S(2)}, u32[]{:S(2)}) async-start(bf16[16,4,2432]{2,1,0:T(4,128)(2,1)} %reshape.210), calls=%async_computation.1 | async-start | bytes 622592 | tf_op jit(solution)/shard_map/all_to_all | solution.py:39
  42.3 2.2 collective-permute-start.1
  44.5 4.3 %collective-permute-start = (bf16[896,256]{1,0:T(8,128)(2,1)S(1)}, bf16[896,256]{1,0:T(8,128)(2,1)S(1)}, u32[]{:S(2)}, u32[]{:S(2)}) collective-permute-start(bf16[896,256]{1,0:T(8,128)(2,1)S(1)} %multiply_convert_fusion.refs_0_), channel_id=1, source_target_pairs={{0,384},{128,0},{256,128},{384,256},{1,385},{129,1},{257,129},{385... | collective-permute-start | bytes 1376264 | tf_op jit(solution)/shard_map/ppermute | solution.py:65
  48.9 1.1 multiply_convert_fusion.1.refs_1_
  49.9 5.4 %collective-permute-done.1.refs_4_ = bf16[896,256]{1,0:T(8,128)(2,1)S(1)} collective-permute-done((bf16[896,256]{1,0:T(8,128)(2,1)S(1)}, bf16[896,256]{1,0:T(8,128)(2,1)S(1)}, u32[]{:S(2)}, u32[]{:S(2)}) %collective-permute-start.1) | collective-permute-done | bytes 458784 | tf_op jit(solution)/shard_map/ppermute | solution.py:65
  55.3 0.9 collective-permute-done.refs_2_
  57.0 1.3 fusion.21
  58.3 0.2 fusion.22
  58.8 1.2 fusion.4
  60.0 0.2 fusion.2
  60.3 0.8 broadcast_in_dim.48
  61.1 11.3 %all-to-all-start.2 = ((bf16[16,4,2048]{2,1,0:T(4,128)(2,1)}), bf16[16,4,2048]{2,1,0:T(4,128)(2,1)}, u32[]{:S(2)}, u32[]{:S(2)}) async-start(bf16[16,4,2048]{2,1,0:T(4,128)(2,1)} %broadcast_in_dim.48), calls=%async_computation.2 | async-start | bytes 524288 | tf_op jit(solution)/shard_map/all_to_all | solution.py:39
  72.4 2.2 collective-permute-start.3
  74.6 5.0 %collective-permute-start.2 = (bf16[768,256]{1,0:T(8,128)(2,1)S(1)}, bf16[768,256]{1,0:T(8,128)(2,1)}, u32[]{:S(2)}, u32[]{:S(2)}) collective-permute-start(bf16[768,256]{1,0:T(8,128)(2,1)S(1)} %multiply_convert_fusion.1.refs_1_), channel_id=1, source_target_pairs={{0,384},{128,0},{256,128},{384,256},{1,385},{129,1},{257,129},{385... | collective-permute-start | bytes 1179656 | tf_op jit(solution)/shard_map/ppermute | solution.py:65
  79.6 1.9 collective-permute-start.4
  81.5 4.6 %collective-permute-start.5 = (bf16[384,256]{1,0:T(8,128)(2,1)S(1)}, bf16[384,256]{1,0:T(8,128)(2,1)S(1)}, u32[]{:S(2)}, u32[]{:S(2)}) collective-permute-start(bf16[384,256]{1,0:T(8,128)(2,1)S(1)} %slice.83), channel_id=1, source_target_pairs={{0,384},{128,0},{256,128},{384,256},{1,385},{129,1},{257,129},{385... | collective-permute-start | bytes 589832 | tf_op jit(solution)/shard_map/ppermute | solution.py:65
  86.1 4.7 %collective-permute-done.5.refs_7_ = bf16[384,256]{1,0:T(8,128)(2,1)S(1)} collective-permute-done((bf16[384,256]{1,0:T(8,128)(2,1)S(1)}, bf16[384,256]{1,0:T(8,128)(2,1)S(1)}, u32[]{:S(2)}, u32[]{:S(2)}) %collective-permute-start.5) | collective-permute-done | bytes 196640 | tf_op jit(solution)/shard_map/ppermute | solution.py:65
  90.8 0.7 copy-done.7
  91.5 0.7 copy-done.2
  92.2 1.0 broadcast_in_dim.49
  93.3 16.0 %all_to_all.40 = bf16[4,64,2048]{2,1,0:T(8,128)(2,1)S(1)} all-to-all(bf16[4,64,2048]{2,1,0:T(8,128)(2,1)S(1)} %broadcast_in_dim.50), channel_id=1, replica_groups=mesh['x'=4,'z'=16,'y'=4,'core'=2] {'x'}, dimensions={0} | all-to-all | bytes 2097152 | tf_op jit(solution)/shard_map/all_to_all | solution.py:39
  109.3 0.4 fusion
  109.8 0.9 broadcast_in_dim.51
  110.7 5.0 %all-to-all-start.4 = ((bf16[16,64,256]{2,1,0:T(8,128)(2,1)}), bf16[16,64,256]{2,1,0:T(8,128)(2,1)}, u32[]{:S(2)}, u32[]{:S(2)}) async-start(bf16[16,64,256]{2,1,0:T(8,128)(2,1)} %bitcast.41), calls=%async_computation.4 | async-start | bytes 1048576 | tf_op jit(solution)/shard_map/all_to_all | solution.py:39
  115.6 0.7 slice.84
  116.3 1.6 slice.85
  117.9 4.4 %collective-permute-start.7 = (bf16[384,256]{1,0:T(8,128)(2,1)}, bf16[384,256]{1,0:T(8,128)(2,1)S(1)}, u32[]{:S(2)}, u32[]{:S(2)}) collective-permute-start(bf16[384,256]{1,0:T(8,128)(2,1)} %slice.85), channel_id=1, source_target_pairs={{0,384},{128,0},{256,128},{384,256},{1,385},{129,1},{257,129},{385... | collective-permute-start | bytes 589832 | tf_op jit(solution)/shard_map/ppermute | solution.py:65
  122.3 1.9 collective-permute-start.6
  124.3 2.3 %collective-permute-done.7.refs_9_ = bf16[384,256]{1,0:T(8,128)(2,1)S(1)} collective-permute-done((bf16[384,256]{1,0:T(8,128)(2,1)}, bf16[384,256]{1,0:T(8,128)(2,1)S(1)}, u32[]{:S(2)}, u32[]{:S(2)}) %collective-permute-start.7) | collective-permute-done | bytes 196640 | tf_op jit(solution)/shard_map/ppermute | solution.py:65
  126.6 3.9 %collective-permute-done.6.refs_8_ = bf16[384,256]{1,0:T(8,128)(2,1)} collective-permute-done((bf16[384,256]{1,0:T(8,128)(2,1)}, bf16[384,256]{1,0:T(8,128)(2,1)}, u32[]{:S(2)}, u32[]{:S(2)}) %collective-permute-start.6) | collective-permute-done | bytes 196640 | tf_op jit(solution)/shard_map/ppermute | solution.py:65
  130.5 1.1 bitcast_reduce_fusion.1
  131.6 8.1 %all-gather = bf16[8,64,256]{2,1,0:T(8,128)(2,1)S(1)} all-gather(bf16[4,64,256]{2,1,0:T(8,128)(2,1)S(1)} %bitcast_reduce_fusion.1), channel_id=2, replica_groups=mesh['x'=4,'z'=16,'y'=4,'core'=2] {'core'}, dimensions={0}, use_global_device_ids=true | all-gather | bytes 393216 | tf_op jit(solution)/shard_map/all_gather | solution.py:61
  139.7 0.9 copy-done.3
  140.7 0.9 copy-done.8
  141.6 0.9 copy-done.10
  142.5 2.3 %gateup_terms.1 = (bf16[64,1792]{1,0:T(8,128)(2,1)S(1)}, f32[4,64,256]{2,1,0:T(8,128)S(1)}) custom-call(s32[1]{0:T(128)} %bitcast.at_ref, bf16[2,4,64,256]{3,2,1,0:T(8,128)(2,1)S(1)} %bitcast.40, bf16[896,256]{1,0:T(8,128)(2,1)S(1)} %multiply_convert_fusion.refs_0_, bf16[768,256]{1,0:T(8,128)(2,1)S(1)} %multiply_convert_fusion.1.refs_1_, ...), custom_call_target="tpu_custom_call" | custom-call | tf_op jit(solution)/shard_map/gateup_terms/pallas_call | solution.py:155
  144.9 0.7 copy-done.4
  145.5 1.7 reshape.219
  147.3 11.5 %all-to-all-start.5 = ((bf16[16,4,1792]{2,1,0:T(4,128)(2,1)}), bf16[16,4,1792]{2,1,0:T(4,128)(2,1)S(1)}, u32[]{:S(2)}, u32[]{:S(2)}) async-start(bf16[16,4,1792]{2,1,0:T(4,128)(2,1)} %reshape.219), calls=%async_computation.5 | async-start | bytes 458752 | tf_op jit(solution)/shard_map/all_to_all | solution.py:39
  158.8 1.9 collective-permute-start.9
  160.8 4.6 %collective-permute-start.8 = (bf16[832,256]{1,0:T(8,128)(2,1)}, bf16[832,256]{1,0:T(8,128)(2,1)S(1)}, u32[]{:S(2)}, u32[]{:S(2)}) collective-permute-start(bf16[832,256]{1,0:T(8,128)(2,1)} %refs_0_), channel_id=1, source_target_pairs={{0,384},{128,0},{256,128},{384,256},{1,385},{129,1},{257,129},{385... | collective-permute-start | bytes 1277960 | tf_op jit(solution)/shard_map/ppermute | solution.py:65
  165.3 7.5 %collective-permute-done.9.refs_2_ = bf16[832,256]{1,0:T(8,128)(2,1)S(1)} collective-permute-done((bf16[832,256]{1,0:T(8,128)(2,1)}, bf16[832,256]{1,0:T(8,128)(2,1)S(1)}, u32[]{:S(2)}, u32[]{:S(2)}) %collective-permute-start.9) | collective-permute-done | bytes 426016 | tf_op jit(solution)/shard_map/ppermute | solution.py:65
  172.9 1.0 collective-permute-done.8.refs_1_
  174.2 0.7 broadcast_in_dim.52
  174.9 11.2 %all-to-all-start.6 = ((bf16[16,4,832]{2,1,0:T(4,128)(2,1)}), bf16[16,4,832]{2,1,0:T(4,128)(2,1)S(1)}, u32[]{:S(2)}, u32[]{:S(2)}) async-start(bf16[16,4,832]{2,1,0:T(4,128)(2,1)} %broadcast_in_dim.52), calls=%async_computation.6 | async-start | bytes 229376 | tf_op jit(solution)/shard_map/all_to_all | solution.py:39
  186.1 5.2 %collective-permute-start.11 = (bf16[448,256]{1,0:T(8,128)(2,1)S(1)}, bf16[448,256]{1,0:T(8,128)(2,1)S(1)}, u32[]{:S(2)}, u32[]{:S(2)}) collective-permute-start(bf16[448,256]{1,0:T(8,128)(2,1)S(1)} %slice.91), channel_id=1, source_target_pairs={{0,384},{128,0},{256,128},{384,256},{1,385},{129,1},{257,129},{385... | collective-permute-start | bytes 688136 | tf_op jit(solution)/shard_map/ppermute | solution.py:65
  191.4 1.9 collective-permute-start.10
  193.3 6.0 %collective-permute-done.10.refs_3_ = bf16[384,256]{1,0:T(8,128)(2,1)S(1)} collective-permute-done((bf16[384,256]{1,0:T(8,128)(2,1)S(1)}, bf16[384,256]{1,0:T(8,128)(2,1)S(1)}, u32[]{:S(2)}, u32[]{:S(2)}) %collective-permute-start.10) | collective-permute-done | bytes 196640 | tf_op jit(solution)/shard_map/ppermute | solution.py:65
  199.4 0.6 copy-done.5
  200.0 0.9 copy-done.6
  200.9 0.4 down_terms.1
  201.3 0.8 broadcast_in_dim.53
  202.2 5.2 %all-to-all-start.7 = ((bf16[16,64,256]{2,1,0:T(8,128)(2,1)}), bf16[16,64,256]{2,1,0:T(8,128)(2,1)S(1)}, u32[]{:S(2)}, u32[]{:S(2)}) async-start(bf16[16,64,256]{2,1,0:T(8,128)(2,1)} %bitcast.18), calls=%async_computation.7 | async-start | bytes 1048576 | tf_op jit(solution)/shard_map/all_to_all | solution.py:39
  207.5 0.6 copy.42
  208.1 8.4 %all-to-all-done.7 = bf16[16,64,256]{2,1,0:T(8,128)(2,1)S(1)} async-done(((bf16[16,64,256]{2,1,0:T(8,128)(2,1)}), bf16[16,64,256]{2,1,0:T(8,128)(2,1)S(1)}, u32[]{:S(2)}, u32[]{:S(2)}) %all-to-all-start.7) | async-done | bytes 524320 | tf_op jit(solution)/shard_map/all_to_all | solution.py:39
  216.5 6.8 %all-gather.1 = bf16[8,64,256]{2,1,0:T(8,128)(2,1)} all-gather(bf16[4,64,256]{2,1,0:T(8,128)(2,1)S(1)} %bitcast_reduce_fusion), channel_id=3, replica_groups=mesh['x'=4,'z'=16,'y'=4,'core'=2] {'core'}, dimensions={0}, use_global_device_ids=true | all-gather | bytes 393216 | tf_op jit(solution)/shard_map/all_gather | solution.py:61
  223.4 1.8 last_sum.1
  (70 shorter events, 2.0 us)
Async XLA Ops:
  0.6 108.7 %copy-start = (bf16[2048,256]{1,0:T(8,128)(2,1)S(1)}, bf16[2048,256]{1,0:T(8,128)(2,1)}, u32[]{:S(2)}) copy-start(bf16[2048,256]{1,0:T(8,128)(2,1)} %param.15) | copy-start | bytes 3145732
  4.9 5.0 %copy-start.13 = (bf16[256]{0:T(256)(128)(2,1)S(1)}, bf16[256]{0:T(256)(128)(2,1)}, u32[]{:S(2)}) copy-start(bf16[256]{0:T(256)(128)(2,1)} %param.16) | copy-start | bytes 1540
  4.9 16.4 %all-to-all-start = ((bf16[4,64,2432]{2,1,0:T(8,128)(2,1)}), bf16[4,64,2432]{2,1,0:T(8,128)(2,1)S(1)}, u32[]{:S(2)}, u32[]{:S(2)}) async-start(bf16[4,64,2432]{2,1,0:T(8,128)(2,1)} %get-tuple-element.31), calls=%async_computation | async-start | bytes 2490368 | tf_op jit(solution)/shard_map/all_to_all | solution.py:39
  11.0 31.2 %copy-start.14 = (s32[2]{0:T(128)S(1)}, s32[2]{0:T(128)}, u32[]{:S(2)}) copy-start(s32[2]{0:T(128)} %param.21) | copy-start | bytes 28
  11.0 31.2 %copy-start.11 = (s32[2]{0:T(128)S(1)}, s32[2]{0:T(128)}, u32[]{:S(2)}) copy-start(s32[2]{0:T(128)} %param.20) | copy-start | bytes 28
  22.3 33.9 %all-to-all-start.1 = ((bf16[16,4,2432]{2,1,0:T(4,128)(2,1)}), bf16[16,4,2432]{2,1,0:T(4,128)(2,1)S(1)}, u32[]{:S(2)}, u32[]{:S(2)}) async-start(bf16[16,4,2432]{2,1,0:T(4,128)(2,1)} %reshape.210), calls=%async_computation.1 | async-start | bytes 622592 | tf_op jit(solution)/shard_map/all_to_all | solution.py:39
  42.3 13.0 %collective-permute-start.1 = (bf16[896,256]{1,0:T(8,128)(2,1)S(1)}, bf16[896,256]{1,0:T(8,128)(2,1)S(1)}, u32[]{:S(2)}, u32[]{:S(2)}) collective-permute-start(bf16[896,256]{1,0:T(8,128)(2,1)S(1)} %multiply_convert_fusion.refs_0_), channel_id=1, source_target_pairs={{0,128},{128,256},{256,384},{384,0},{1,129},{129,257},{257,385},{3... | collective-permute-start | bytes 1376264 | tf_op jit(solution)/shard_map/ppermute | solution.py:65
  44.5 11.7 %collective-permute-start = (bf16[896,256]{1,0:T(8,128)(2,1)S(1)}, bf16[896,256]{1,0:T(8,128)(2,1)S(1)}, u32[]{:S(2)}, u32[]{:S(2)}) collective-permute-start(bf16[896,256]{1,0:T(8,128)(2,1)S(1)} %multiply_convert_fusion.refs_0_), channel_id=1, source_target_pairs={{0,384},{128,0},{256,128},{384,256},{1,385},{129,1},{257,129},{385... | collective-permute-start | bytes 1376264 | tf_op jit(solution)/shard_map/ppermute | solution.py:65
  61.1 31.1 %all-to-all-start.2 = ((bf16[16,4,2048]{2,1,0:T(4,128)(2,1)}), bf16[16,4,2048]{2,1,0:T(4,128)(2,1)}, u32[]{:S(2)}, u32[]{:S(2)}) async-start(bf16[16,4,2048]{2,1,0:T(4,128)(2,1)} %broadcast_in_dim.48), calls=%async_computation.2 | async-start | bytes 524288 | tf_op jit(solution)/shard_map/all_to_all | solution.py:39
  72.4 19.8 %collective-permute-start.3 = (bf16[768,256]{1,0:T(8,128)(2,1)S(1)}, bf16[768,256]{1,0:T(8,128)(2,1)S(1)}, u32[]{:S(2)}, u32[]{:S(2)}) collective-permute-start(bf16[768,256]{1,0:T(8,128)(2,1)S(1)} %multiply_convert_fusion.1.refs_1_), channel_id=1, source_target_pairs={{0,128},{128,256},{256,384},{384,0},{1,129},{129,257},{257,385},{3... | collective-permute-start | bytes 1179656 | tf_op jit(solution)/shard_map/ppermute | solution.py:65
  74.6 17.6 %collective-permute-start.2 = (bf16[768,256]{1,0:T(8,128)(2,1)S(1)}, bf16[768,256]{1,0:T(8,128)(2,1)}, u32[]{:S(2)}, u32[]{:S(2)}) collective-permute-start(bf16[768,256]{1,0:T(8,128)(2,1)S(1)} %multiply_convert_fusion.1.refs_1_), channel_id=1, source_target_pairs={{0,384},{128,0},{256,128},{384,256},{1,385},{129,1},{257,129},{385... | collective-permute-start | bytes 1179656 | tf_op jit(solution)/shard_map/ppermute | solution.py:65
  79.6 11.9 %collective-permute-start.4 = (bf16[512,256]{1,0:T(8,128)(2,1)S(1)}, bf16[512,256]{1,0:T(8,128)(2,1)S(1)}, u32[]{:S(2)}, u32[]{:S(2)}) collective-permute-start(bf16[512,256]{1,0:T(8,128)(2,1)S(1)} %slice.82), channel_id=1, source_target_pairs={{0,128},{128,256},{256,384},{384,0},{1,129},{129,257},{257,385},{3... | collective-permute-start | bytes 786440 | tf_op jit(solution)/shard_map/ppermute | solution.py:65
  81.5 9.3 %collective-permute-start.5 = (bf16[384,256]{1,0:T(8,128)(2,1)S(1)}, bf16[384,256]{1,0:T(8,128)(2,1)S(1)}, u32[]{:S(2)}, u32[]{:S(2)}) collective-permute-start(bf16[384,256]{1,0:T(8,128)(2,1)S(1)} %slice.83), channel_id=1, source_target_pairs={{0,384},{128,0},{256,128},{384,256},{1,385},{129,1},{257,129},{385... | collective-permute-start | bytes 589832 | tf_op jit(solution)/shard_map/ppermute | solution.py:65
  90.8 0.7 copy-start.7
  91.5 0.7 copy-start.2
  93.3 16.0 %copy-start.12 = (bf16[256,256]{1,0:T(8,128)(2,1)S(1)}, bf16[256,256]{1,0:T(8,128)(2,1)}, u32[]{:S(2)}) copy-start(bf16[256,256]{1,0:T(8,128)(2,1)} %get-tuple-element.39) | copy-start | bytes 393220
  110.7 19.8 %all-to-all-start.4 = ((bf16[16,64,256]{2,1,0:T(8,128)(2,1)}), bf16[16,64,256]{2,1,0:T(8,128)(2,1)}, u32[]{:S(2)}, u32[]{:S(2)}) async-start(bf16[16,64,256]{2,1,0:T(8,128)(2,1)} %bitcast.41), calls=%async_computation.4 | async-start | bytes 1048576 | tf_op jit(solution)/shard_map/all_to_all | solution.py:39
  117.9 8.7 %collective-permute-start.7 = (bf16[384,256]{1,0:T(8,128)(2,1)}, bf16[384,256]{1,0:T(8,128)(2,1)S(1)}, u32[]{:S(2)}, u32[]{:S(2)}) collective-permute-start(bf16[384,256]{1,0:T(8,128)(2,1)} %slice.85), channel_id=1, source_target_pairs={{0,384},{128,0},{256,128},{384,256},{1,385},{129,1},{257,129},{385... | collective-permute-start | bytes 589832 | tf_op jit(solution)/shard_map/ppermute | solution.py:65
  122.3 8.1 %collective-permute-start.6 = (bf16[384,256]{1,0:T(8,128)(2,1)}, bf16[384,256]{1,0:T(8,128)(2,1)}, u32[]{:S(2)}, u32[]{:S(2)}) collective-permute-start(bf16[384,256]{1,0:T(8,128)(2,1)} %slice.84), channel_id=1, source_target_pairs={{0,128},{128,256},{256,384},{384,0},{1,129},{129,257},{257,385},{3... | collective-permute-start | bytes 589832 | tf_op jit(solution)/shard_map/ppermute | solution.py:65
  126.6 13.1 %copy-start.9 = (bf16[384,256]{1,0:T(8,128)(2,1)}, bf16[384,256]{1,0:T(8,128)(2,1)S(1)}, u32[]{:S(2)}) copy-start(bf16[384,256]{1,0:T(8,128)(2,1)S(1)} %collective-permute-done.7.refs_9_) | copy-start | bytes 589828
  139.7 1.0 copy-start.3
  140.7 0.9 copy-start.8
  141.6 0.9 copy-start.10
  144.8 0.7 copy-start.4
  145.5 54.4 %copy-start.1 = (bf16[832,256]{1,0:T(8,128)(2,1)S(1)}, bf16[832,256]{1,0:T(8,128)(2,1)}, u32[]{:S(2)}) copy-start(bf16[832,256]{1,0:T(8,128)(2,1)} %refs_0_) | copy-start | bytes 1277956
  147.3 26.6 %all-to-all-start.5 = ((bf16[16,4,1792]{2,1,0:T(4,128)(2,1)}), bf16[16,4,1792]{2,1,0:T(4,128)(2,1)S(1)}, u32[]{:S(2)}, u32[]{:S(2)}) async-start(bf16[16,4,1792]{2,1,0:T(4,128)(2,1)} %reshape.219), calls=%async_computation.5 | async-start | bytes 458752 | tf_op jit(solution)/shard_map/all_to_all | solution.py:39
  158.8 14.0 %collective-permute-start.9 = (bf16[832,256]{1,0:T(8,128)(2,1)}, bf16[832,256]{1,0:T(8,128)(2,1)S(1)}, u32[]{:S(2)}, u32[]{:S(2)}) collective-permute-start(bf16[832,256]{1,0:T(8,128)(2,1)} %refs_0_), channel_id=1, source_target_pairs={{0,128},{128,256},{256,384},{384,0},{1,129},{129,257},{257,385},{3... | collective-permute-start | bytes 1277960 | tf_op jit(solution)/shard_map/ppermute | solution.py:65
  160.8 13.1 %collective-permute-start.8 = (bf16[832,256]{1,0:T(8,128)(2,1)}, bf16[832,256]{1,0:T(8,128)(2,1)S(1)}, u32[]{:S(2)}, u32[]{:S(2)}) collective-permute-start(bf16[832,256]{1,0:T(8,128)(2,1)} %refs_0_), channel_id=1, source_target_pairs={{0,384},{128,0},{256,128},{384,256},{1,385},{129,1},{257,129},{385... | collective-permute-start | bytes 1277960 | tf_op jit(solution)/shard_map/ppermute | solution.py:65
  174.9 24.4 %all-to-all-start.6 = ((bf16[16,4,832]{2,1,0:T(4,128)(2,1)}), bf16[16,4,832]{2,1,0:T(4,128)(2,1)S(1)}, u32[]{:S(2)}, u32[]{:S(2)}) async-start(bf16[16,4,832]{2,1,0:T(4,128)(2,1)} %broadcast_in_dim.52), calls=%async_computation.6 | async-start | bytes 229376 | tf_op jit(solution)/shard_map/all_to_all | solution.py:39
  186.1 13.2 %collective-permute-start.11 = (bf16[448,256]{1,0:T(8,128)(2,1)S(1)}, bf16[448,256]{1,0:T(8,128)(2,1)S(1)}, u32[]{:S(2)}, u32[]{:S(2)}) collective-permute-start(bf16[448,256]{1,0:T(8,128)(2,1)S(1)} %slice.91), channel_id=1, source_target_pairs={{0,384},{128,0},{256,128},{384,256},{1,385},{129,1},{257,129},{385... | collective-permute-start | bytes 688136 | tf_op jit(solution)/shard_map/ppermute | solution.py:65
  191.4 7.9 %collective-permute-start.10 = (bf16[384,256]{1,0:T(8,128)(2,1)S(1)}, bf16[384,256]{1,0:T(8,128)(2,1)S(1)}, u32[]{:S(2)}, u32[]{:S(2)}) collective-permute-start(bf16[384,256]{1,0:T(8,128)(2,1)S(1)} %slice.90), channel_id=1, source_target_pairs={{0,128},{128,256},{256,384},{384,0},{1,129},{129,257},{257,385},{3... | collective-permute-start | bytes 589832 | tf_op jit(solution)/shard_map/ppermute | solution.py:65
  199.3 0.7 copy-start.5
  200.0 0.9 copy-start.6
  202.2 14.3 %all-to-all-start.7 = ((bf16[16,64,256]{2,1,0:T(8,128)(2,1)}), bf16[16,64,256]{2,1,0:T(8,128)(2,1)S(1)}, u32[]{:S(2)}, u32[]{:S(2)}) async-start(bf16[16,64,256]{2,1,0:T(8,128)(2,1)} %bitcast.18), calls=%async_computation.7 | async-start | bytes 1048576 | tf_op jit(solution)/shard_map/all_to_all | solution.py:39

commit v7 on v5

--- a/solution.py
+++ b/solution.py
@@ -15,6 +15,7 @@
 WIDE = ("x", "z")
 MP = ("y", "core")
 XS, ZS, YS, CORES = 4, 16, 4, 2
+QUERY_CHUNKS = 4
 
 
 def rotate(vectors, offsets):
@@ -45,25 +46,36 @@
     return exchange(jnp.broadcast_to(block[None], (size,) + block.shape), axis)
 
 
-def group_terms(terms):
-    total = jnp.sum(collect(terms.astype(jnp.bfloat16), "y", YS).astype(jnp.float32), axis=0)
+def group_terms(copies):
+    total = jnp.sum(exchange(copies, "y").astype(jnp.float32), axis=0)
     return lax.all_gather(total.astype(jnp.bfloat16), "core", axis=0, tiled=False)
 
 
-def to_row_order(count, back):
+def to_row_order(count):
     dims = (count, count)
-    mixed = lax.broadcasted_iota(jnp.int32, dims, 1 if back else 0)
-    plain = lax.broadcasted_iota(jnp.int32, dims, 0 if back else 1)
+    mixed = lax.broadcasted_iota(jnp.int32, dims, 0)
+    plain = lax.broadcasted_iota(jnp.int32, dims, 1)
     source = (mixed >> 2) * 2 + (mixed & 1) + ((mixed >> 1) & 1) * (count // 2)
     return jnp.where(source == plain, 1.0, 0.0).astype(jnp.bfloat16)
 
 
-def first_kernel(inputs_ref, gain_ref, query_ref, keyval_ref, terms_ref, rows_ref):
+def first_kernel(
+    inputs_hbm, gain_ref, query_hbm, keyval_hbm, terms_ref, rows_ref, inputs_ref, query_ref, keyval_ref, sems
+):
     group = inputs_ref.shape[1] // XS
-    order = to_row_order(2 * group, False)
-    gain = gain_ref[...].astype(jnp.float32)
     queries = query_ref.shape[1]
     keyvals = keyval_ref.shape[1]
+    chunk = queries // QUERY_CHUNKS
+    copies = [pltpu.make_async_copy(inputs_hbm, inputs_ref, sems.at[0])]
+    for at in range(QUERY_CHUNKS):
+        here = slice(chunk * at, chunk * (at + 1))
+        copies.append(pltpu.make_async_copy(query_hbm.at[:, here], query_ref.at[:, here], sems.at[1 + at]))
+    copies.append(pltpu.make_async_copy(keyval_hbm, keyval_ref, sems.at[1 + QUERY_CHUNKS]))
+    for copy in copies:
+        copy.start()
+    order = to_row_order(2 * group)
+    gain = gain_ref[...].astype(jnp.float32)
+    copies[0].wait()
     scaled = []
     for at in range(XS):
         block = jnp.concatenate([inputs_ref[step, group * at : group * (at + 1)] for step in range(2)], axis=0)
@@ -73,8 +85,11 @@
         terms_ref[at, :, queries + keyvals :] = (squares[:, :128] + squares[:, 128:]).astype(jnp.bfloat16)
         scaled.append((values * gain).astype(jnp.bfloat16))
     scaled = jnp.concatenate(scaled, axis=0)
-    for weights_ref, base in ((query_ref, 0), (keyval_ref, queries)):
-        for start in range(0, weights_ref.shape[1], 256):
+    for at in range(QUERY_CHUNKS + 1):
+        copies[1 + at].wait()
+        last = at == QUERY_CHUNKS
+        weights_ref, base = (keyval_ref, queries) if last else (query_ref, 0)
+        for start in range(0, keyvals, 256) if last else range(chunk * at, chunk * (at + 1), 256):
             product = jnp.dot(scaled, weights_ref[:, start : start + 256], preferred_element_type=jnp.float32)
             product = product.astype(jnp.bfloat16).reshape(XS, 2 * group, 256)
             terms_ref[:, :, base + start : base + start + 256] = product
@@ -83,15 +98,39 @@
 def first_terms(inputs, gain, w_query, w_keyval):
     steps, all_rows, width = inputs.shape
     columns = w_query.shape[1] + w_keyval.shape[1] + 128
+    anywhere = pl.BlockSpec(memory_space=pl.ANY)
     return pl.pallas_call(
         first_kernel,
         out_shape=(
             jax.ShapeDtypeStruct((XS, steps * all_rows // XS, columns), jnp.bfloat16),
             jax.ShapeDtypeStruct((steps * all_rows, width), jnp.bfloat16),
         ),
-        compiler_params=pltpu.CompilerParams(vmem_limit_bytes=24 * 1024 * 1024),
+        in_specs=[anywhere, pl.BlockSpec(memory_space=pltpu.VMEM), anywhere, anywhere],
+        scratch_shapes=[
+            pltpu.VMEM(inputs.shape, jnp.bfloat16),
+            pltpu.VMEM(w_query.shape, jnp.bfloat16),
+            pltpu.VMEM(w_keyval.shape, jnp.bfloat16),
+            pltpu.SemaphoreType.DMA((QUERY_CHUNKS + 2,)),
+        ],
+        compiler_params=pltpu.CompilerParams(vmem_limit_bytes=56 * 1024 * 1024),
         name="first_terms",
     )(inputs, gain.reshape(1, width), w_query, w_keyval)
+
+
+def spread_kernel(rows_ref, weights_ref, copies_ref):
+    product = jnp.dot(rows_ref[...], weights_ref[...], preferred_element_type=jnp.float32)
+    product = product.astype(jnp.bfloat16)
+    for at in range(copies_ref.shape[0]):
+        copies_ref[at] = product
+
+
+def spread_dot(rows, weights, copies):
+    return pl.pallas_call(
+        spread_kernel,
+        out_shape=jax.ShapeDtypeStruct((copies, rows.shape[0], weights.shape[1]), jnp.bfloat16),
+        compiler_params=pltpu.CompilerParams(vmem_limit_bytes=24 * 1024 * 1024),
+        name="spread_dot",
+    )(rows, weights)
 
 
 def gateup_kernel(pair_ref, rows_ref, weights_ref, terms_ref, state_ref):
@@ -125,29 +164,6 @@
         compiler_params=pltpu.CompilerParams(vmem_limit_bytes=24 * 1024 * 1024),
         name="gateup_terms",
     )(pair, rows, weights)
-
-
-def last_kernel(pair_ref, state_ref, outputs_ref):
-    group = outputs_ref.shape[1] // XS
-    order = to_row_order(2 * group, True)
-    for at in range(XS):
-        here = slice(2 * group * at, 2 * group * (at + 1))
-        values = (
-            pair_ref[0, here].astype(jnp.float32) + pair_ref[1, here].astype(jnp.float32) + state_ref[here]
-        )
-        values = jnp.dot(order, values.astype(jnp.bfloat16), preferred_element_type=jnp.float32)
-        values = values.astype(jnp.bfloat16)
-        for step in range(2):
-            outputs_ref[step, group * at : group * (at + 1)] = values[group * step : group * (step + 1)]
-
-
-def last_sum(pair, state, steps):
-    count, width = state.shape
-    return pl.pallas_call(
-        last_kernel,
-        out_shape=jax.ShapeDtypeStruct((steps, count // steps, width), jnp.bfloat16),
-        name="last_sum",
-    )(pair, state)
 
 
 def attend(queries, kv_cache, lengths, fresh_keys, fresh_values, score_scale):
@@ -229,10 +245,8 @@
     heads = mixed.astype(jnp.bfloat16).transpose(1, 0, 2, 3).reshape(steps * local_rows, keyvals_at)
 
     all_heads = collect(collect(heads, "z", ZS).reshape(x_rows, keyvals_at), "x", XS)
-    attn_terms = jnp.dot(
-        all_heads.reshape(rows, keyvals_at), w_out, preferred_element_type=jnp.float32
-    )
-    terms, state = gateup_terms(group_terms(attn_terms), input_rows, gateup)
+    pair = group_terms(spread_dot(all_heads.reshape(rows, keyvals_at), w_out, YS))
+    terms, state = gateup_terms(pair, input_rows, gateup)
     sums = jnp.sum(exchange(terms, "x").astype(jnp.float32), axis=0)
     sums = sum_over(sums, "z", ZS)
     mean = jnp.sum(sums[:, 2 * local_hidden :], axis=-1, keepdims=True) / D
@@ -240,8 +254,13 @@
     activated = jax.nn.silu(sums[:, :local_hidden]) * sums[:, local_hidden:]
     hidden = collect(activated.astype(jnp.bfloat16), "z", ZS).reshape(x_rows, local_hidden)
     hidden = collect(hidden, "x", XS).reshape(rows, local_hidden)
-    down_terms = jnp.dot(hidden, w_down, preferred_element_type=jnp.float32)
-    outputs = last_sum(group_terms(down_terms), state, steps)
+    pair = group_terms(spread_dot(hidden, w_down, YS)).astype(jnp.float32)
+    result = (pair[0] + pair[1] + state).astype(jnp.bfloat16)
+    outputs = (
+        result.reshape(XS * ZS, steps, local_rows, local_width)
+        .transpose(1, 0, 2, 3)
+        .reshape(steps, all_rows, local_width)
+    )
     return (outputs, new_entries)
 
 

time: 208 us -> 207 us (level)
  local copies, waits for them, and re-layouts: 8.23 us -> 4.19 us
  Pallas kernels: 3.08 us -> 6.97 us
    unnamed x25 -> x19, local copies, waits for them, and re-layouts: 4.36 us -> 0.64 us
    pallas_call x1, Pallas kernels: 0.6 us -> 4.03 us  [first_terms(): pl.pallas_call(first_kernel, out_shape=(jax.ShapeDtypeStruct((XS, steps *...]
where the time goes in v7:
time: 207 us
  blocking collectives  139 us (67%)
  starting transfers between devices  26.9 us (13%)
  waiting for transfers between devices  26.1 us (13%)
  Pallas kernels  6.97 us (3%)
  local copies, waits for them, and re-layouts  4.19 us (2%)
  other arithmetic  2.18 us (1%)
    all_to_all x7, blocking collectives, exchange(): return lax.all_to_all(blocks, axis, 0, 0, tiled=True)  120 us
    all_to_all x3, starting transfers between devices, exchange(): return lax.all_to_all(blocks, axis, 0, 0, tiled=True)  26.9 us
    all_to_all x3, waiting for transfers between devices, exchange(): return lax.all_to_all(blocks, axis, 0, 0, tiled=True)  26.1 us
    all_gather x2, blocking collectives, group_terms(): lax.all_gather(total.astype(jnp.bfloat16), 'core', axis=0, tiled=False)  18.2 us
  transfers between devices with their start and end apart: 3, of which 3 were waited for; matrix products, arithmetic and copies ran while one was open for 0% of the time, Pallas kernels for 0%

profile of v7, /device:TPU:1, one launch (start us, length us, event | category | flops | bytes accessed | tf_op | source)
XLA Modules:
  0.0 206.7 jit_solution(17661992471264022976)
XLA Ops:
  0.6 1.2 reshape.198.gain_ref
  1.8 4.0 %first_terms.1 = (bf16[4,64,2432]{2,1,0:T(8,128)(2,1)}, bf16[256,256]{1,0:T(8,128)(2,1)}) custom-call(bf16[2,128,256]{2,1,0:T(8,128)(2,1)} %inputs_hbm.1, bf16[1,256]{1,0:T(2,128)(2,1)} %reshape.198.gain_ref, bf16[256,2048]{1,0:T(8,128)(2,1)} %query_hbm.1, bf16[256,256]{1,0:T(8,128)(2,1)} %bitcast.38), custom_call_target="tpu_custom_call" | custom-call | tf_op jit(solution)/shard_map/first_terms/pallas_call | solution.py:102
  5.9 16.6 %all_to_all.50 = bf16[4,64,2432]{2,1,0:T(8,128)(2,1)S(1)} all-to-all(bf16[4,64,2432]{2,1,0:T(8,128)(2,1)} %get-tuple-element.6), channel_id=1, replica_groups=mesh['x'=4,'z'=16,'y'=4,'core'=2] {'x'}, dimensions={0} | all-to-all | bytes 2490368 | tf_op jit(solution)/shard_map/all_to_all | solution.py:36
  22.5 0.2 reduce_sum.102
  22.7 0.0 copy-start.4
  22.7 0.8 reshape.200
  23.5 19.1 %all-to-all-start.1 = ((bf16[16,4,2432]{2,1,0:T(4,128)(2,1)}), bf16[16,4,2432]{2,1,0:T(4,128)(2,1)S(1)}, u32[]{:S(2)}, u32[]{:S(2)}) async-start(bf16[16,4,2432]{2,1,0:T(4,128)(2,1)} %reshape.200), calls=%async_computation.1 | async-start | bytes 622592 | tf_op jit(solution)/shard_map/all_to_all | solution.py:36
  42.7 0.0 copy-done.6
  42.7 0.1 add_convert_fusion.2
  42.8 0.0 copy-done.5
  42.8 0.1 iota_compare_fusion
  42.8 13.1 %all-to-all-done.1 = bf16[16,4,2432]{2,1,0:T(4,128)(2,1)S(1)} async-done(((bf16[16,4,2432]{2,1,0:T(4,128)(2,1)}), bf16[16,4,2432]{2,1,0:T(4,128)(2,1)S(1)}, u32[]{:S(2)}, u32[]{:S(2)}) %all-to-all-start.1) | async-done | bytes 311328 | tf_op jit(solution)/shard_map/all_to_all | solution.py:36
  55.9 0.1 convert_reduce_fusion
  56.0 0.1 slice_reduce_fusion.1
  56.2 0.1 slice_multiply_fusion
  56.3 0.1 fusion.20
  56.4 0.1 fusion.21
  56.5 0.1 subtract_convert_fusion.1
  56.6 0.1 pad_maximum_fusion
  56.7 0.0 copy-done.4
  56.7 0.3 fusion.22
  57.0 0.2 fusion.23
  57.3 0.2 fusion.8
  57.5 0.2 fusion.3
  57.7 0.2 fusion.1
  58.0 0.1 broadcast_in_dim.45
  58.1 24.6 %all_to_all.51 = bf16[16,4,2048]{2,1,0:T(4,128)(2,1)S(1)} all-to-all(bf16[16,4,2048]{2,1,0:T(4,128)(2,1)S(1)} %broadcast_in_dim.45), channel_id=1, replica_groups=mesh['x'=4,'z'=16,'y'=4,'core'=2] {'z'}, dimensions={0} | all-to-all | bytes 524288 | tf_op jit(solution)/shard_map/all_to_all | solution.py:36
  82.6 0.1 broadcast_in_dim.46
  82.7 0.1 broadcast_in_dim.78
  82.8 0.0 copy-start
  82.8 12.3 %all_to_all.52 = bf16[4,64,2048]{2,1,0:T(8,128)(2,1)S(1)} all-to-all(bf16[4,64,2048]{2,1,0:T(8,128)(2,1)S(1)} %broadcast_in_dim.78), channel_id=1, replica_groups=mesh['x'=4,'z'=16,'y'=4,'core'=2] {'x'}, dimensions={0} | all-to-all | bytes 2097152 | tf_op jit(solution)/shard_map/all_to_all | solution.py:36
  95.1 0.0 copy-done
  95.2 1.2 spread_dot.2
  96.4 4.3 %all-to-all-start.4 = ((bf16[4,256,256]{2,1,0:T(8,128)(2,1)}), bf16[4,256,256]{2,1,0:T(8,128)(2,1)S(1)}, u32[]{:S(2)}, u32[]{:S(2)}) async-start(bf16[4,256,256]{2,1,0:T(8,128)(2,1)} %spread_dot.2), calls=%async_computation.4 | async-start | bytes 1048576 | tf_op jit(solution)/shard_map/all_to_all | solution.py:36
  100.6 0.0 copy-done.7
  100.6 0.0 copy-done.3
  100.7 0.0 copy-start.2
  100.7 0.2 multiply_convert_fusion
  100.8 6.7 %all-to-all-done.4 = bf16[4,256,256]{2,1,0:T(8,128)(2,1)S(1)} async-done(((bf16[4,256,256]{2,1,0:T(8,128)(2,1)}), bf16[4,256,256]{2,1,0:T(8,128)(2,1)S(1)}, u32[]{:S(2)}, u32[]{:S(2)}) %all-to-all-start.4) | async-done | bytes 524320 | tf_op jit(solution)/shard_map/all_to_all | solution.py:36
  107.6 0.1 reduce_sum.107
  107.7 11.0 %all-gather = bf16[512,256]{1,0:T(8,128)(2,1)S(1)} all-gather(bf16[256,256]{1,0:T(8,128)(2,1)S(1)} %reduce_sum.107), channel_id=2, replica_groups=mesh['x'=4,'z'=16,'y'=4,'core'=2] {'core'}, dimensions={0}, use_global_device_ids=true | all-gather | bytes 393216 | tf_op jit(solution)/shard_map/all_gather | solution.py:51
  118.6 0.6 gateup_terms.1
  119.2 15.9 %all_to_all.53 = bf16[4,64,1792]{2,1,0:T(8,128)(2,1)S(1)} all-to-all(bf16[4,64,1792]{2,1,0:T(8,128)(2,1)S(1)} %get-tuple-element.8), channel_id=1, replica_groups=mesh['x'=4,'z'=16,'y'=4,'core'=2] {'x'}, dimensions={0} | all-to-all | bytes 1835008 | tf_op jit(solution)/shard_map/all_to_all | solution.py:36
  135.1 0.2 reduce_sum.108
  135.3 0.1 reshape.207
  135.3 20.7 %all_to_all.54 = bf16[16,4,1792]{2,1,0:T(4,128)(2,1)S(1)} all-to-all(bf16[16,4,1792]{2,1,0:T(4,128)(2,1)S(1)} %reshape.207), channel_id=1, replica_groups=mesh['x'=4,'z'=16,'y'=4,'core'=2] {'z'}, dimensions={0} | all-to-all | bytes 458752 | tf_op jit(solution)/shard_map/all_to_all | solution.py:36
  156.0 0.1 convert_reduce_fusion.1
  156.1 0.1 slice_reduce_fusion
  156.3 0.1 slice_multiply_fusion.1
  156.3 0.1 fusion.12
  156.5 21.4 %all_to_all.55 = bf16[16,4,832]{2,1,0:T(4,128)(2,1)S(1)} all-to-all(bf16[16,4,832]{2,1,0:T(4,128)(2,1)S(1)} %broadcast_in_dim.79), channel_id=1, replica_groups=mesh['x'=4,'z'=16,'y'=4,'core'=2] {'z'}, dimensions={0} | all-to-all | bytes 212992 | tf_op jit(solution)/shard_map/all_to_all | solution.py:36
  177.9 0.1 broadcast_in_dim.80
  178.0 9.0 %all_to_all.56 = bf16[4,64,832]{2,1,0:T(8,128)(2,1)S(1)} all-to-all(bf16[4,64,832]{2,1,0:T(8,128)(2,1)S(1)} %broadcast_in_dim.81), channel_id=1, replica_groups=mesh['x'=4,'z'=16,'y'=4,'core'=2] {'x'}, dimensions={0} | all-to-all | bytes 851968 | tf_op jit(solution)/shard_map/all_to_all | solution.py:36
  187.0 1.1 spread_dot.3
  188.1 3.5 %all-to-all-start.9 = ((bf16[4,256,256]{2,1,0:T(8,128)(2,1)}), bf16[4,256,256]{2,1,0:T(8,128)(2,1)S(1)}, u32[]{:S(2)}, u32[]{:S(2)}) async-start(bf16[4,256,256]{2,1,0:T(8,128)(2,1)} %spread_dot.3), calls=%async_computation.9 | async-start | bytes 1048576 | tf_op jit(solution)/shard_map/all_to_all | solution.py:36
  191.6 0.1 maximum_bitcast_fusion
  191.6 0.6 copy.60
  192.2 6.2 %all-to-all-done.9 = bf16[4,256,256]{2,1,0:T(8,128)(2,1)S(1)} async-done(((bf16[4,256,256]{2,1,0:T(8,128)(2,1)}), bf16[4,256,256]{2,1,0:T(8,128)(2,1)S(1)}, u32[]{:S(2)}, u32[]{:S(2)}) %all-to-all-start.9) | async-done | bytes 524320 | tf_op jit(solution)/shard_map/all_to_all | solution.py:36
  198.4 0.1 reduce_sum.111
  198.5 7.2 %all-gather.1 = bf16[512,256]{1,0:T(8,128)(2,1)S(1)} all-gather(bf16[256,256]{1,0:T(8,128)(2,1)S(1)} %reduce_sum.111), channel_id=3, replica_groups=mesh['x'=4,'z'=16,'y'=4,'core'=2] {'core'}, dimensions={0}, use_global_device_ids=true | all-gather | bytes 393216 | tf_op jit(solution)/shard_map/all_gather | solution.py:51
  205.8 0.1 fusion.7
  205.9 0.1 reshape.209
  205.9 0.1 copy.59
  206.0 0.7 reshape.210
  (27 shorter events, 0.3 us)
Async XLA Ops:
  22.5 20.2 %copy-start.6 = (s32[2]{0:T(128)S(1)}, s32[2]{0:T(128)}, u32[]{:S(2)}) copy-start(s32[2]{0:T(128)} %param.21) | copy-start | bytes 28
  22.5 20.3 %copy-start.5 = (s32[2]{0:T(128)S(1)}, s32[2]{0:T(128)}, u32[]{:S(2)}) copy-start(s32[2]{0:T(128)} %param.20) | copy-start | bytes 28
  22.7 34.0 %copy-start.4 = (bf16[2,768,1,256]{3,1,2,0:T(8,128)(2,1)S(1)}, bf16[2,768,1,256]{3,1,2,0:T(8,128)(2,1)}, u32[]{:S(2)}) copy-start(bf16[2,768,1,256]{3,1,2,0:T(8,128)(2,1)} %param.19) | copy-start | bytes 2359300
  23.5 32.4 %all-to-all-start.1 = ((bf16[16,4,2432]{2,1,0:T(4,128)(2,1)}), bf16[16,4,2432]{2,1,0:T(4,128)(2,1)S(1)}, u32[]{:S(2)}, u32[]{:S(2)}) async-start(bf16[16,4,2432]{2,1,0:T(4,128)(2,1)} %reshape.200), calls=%async_computation.1 | async-start | bytes 622592 | tf_op jit(solution)/shard_map/all_to_all | solution.py:36
  82.8 12.3 %copy-start = (bf16[2048,256]{1,0:T(8,128)(2,1)S(1)}, bf16[2048,256]{1,0:T(8,128)(2,1)}, u32[]{:S(2)}) copy-start(bf16[2048,256]{1,0:T(8,128)(2,1)} %weights_ref.2) | copy-start | bytes 3145732
  95.1 5.5 %copy-start.7 = (bf16[256]{0:T(256)(128)(2,1)S(1)}, bf16[256]{0:T(256)(128)(2,1)}, u32[]{:S(2)}) copy-start(bf16[256]{0:T(256)(128)(2,1)} %param.16) | copy-start | bytes 1540
  95.1 5.5 %copy-start.3 = (bf16[256,2,832]{0,2,1:T(8,128)(2,1)S(1)}, bf16[256,2,832]{0,2,1:T(8,128)(2,1)}, u32[]{:S(2)}) copy-start(bf16[256,2,832]{0,2,1:T(8,128)(2,1)} %param.17) | copy-start | bytes 2555908
  96.4 11.2 %all-to-all-start.4 = ((bf16[4,256,256]{2,1,0:T(8,128)(2,1)}), bf16[4,256,256]{2,1,0:T(8,128)(2,1)S(1)}, u32[]{:S(2)}, u32[]{:S(2)}) async-start(bf16[4,256,256]{2,1,0:T(8,128)(2,1)} %spread_dot.2), calls=%async_computation.4 | async-start | bytes 1048576 | tf_op jit(solution)/shard_map/all_to_all | solution.py:36
  100.7 18.0 %copy-start.2 = (bf16[256,256]{1,0:T(8,128)(2,1)S(1)}, bf16[256,256]{1,0:T(8,128)(2,1)}, u32[]{:S(2)}) copy-start(bf16[256,256]{1,0:T(8,128)(2,1)} %get-tuple-element.7.rows_ref) | copy-start | bytes 393220
  156.0 30.9 %copy-start.1 = (bf16[832,256]{1,0:T(8,128)(2,1)S(1)}, bf16[832,256]{1,0:T(8,128)(2,1)}, u32[]{:S(2)}) copy-start(bf16[832,256]{1,0:T(8,128)(2,1)} %weights_ref.3) | copy-start | bytes 1277956
  188.1 10.4 %all-to-all-start.9 = ((bf16[4,256,256]{2,1,0:T(8,128)(2,1)}), bf16[4,256,256]{2,1,0:T(8,128)(2,1)S(1)}, u32[]{:S(2)}, u32[]{:S(2)}) async-start(bf16[4,256,256]{2,1,0:T(8,128)(2,1)} %spread_dot.3), calls=%async_computation.9 | async-start | bytes 1048576 | tf_op jit(solution)/shard_map/all_to_all | solution.py:36

commit v8 on v7

--- a/solution.py
+++ b/solution.py
@@ -60,22 +60,27 @@
 
 
 def first_kernel(
-    inputs_hbm, gain_ref, query_hbm, keyval_hbm, terms_ref, rows_ref, inputs_ref, query_ref, keyval_ref, sems
+    inputs_hbm, gain_hbm, query_hbm, keyval_hbm, terms_hbm, rows_hbm,
+    inputs_ref, gain_ref, query_ref, keyval_ref, terms_ref, rows_ref, sems, out_sems,
 ):
     group = inputs_ref.shape[1] // XS
     queries = query_ref.shape[1]
     keyvals = keyval_ref.shape[1]
     chunk = queries // QUERY_CHUNKS
-    copies = [pltpu.make_async_copy(inputs_hbm, inputs_ref, sems.at[0])]
-    for at in range(QUERY_CHUNKS):
-        here = slice(chunk * at, chunk * (at + 1))
-        copies.append(pltpu.make_async_copy(query_hbm.at[:, here], query_ref.at[:, here], sems.at[1 + at]))
-    copies.append(pltpu.make_async_copy(keyval_hbm, keyval_ref, sems.at[1 + QUERY_CHUNKS]))
+    parts = [slice(chunk * at, chunk * (at + 1)) for at in range(QUERY_CHUNKS)]
+    copies = [
+        pltpu.make_async_copy(inputs_hbm, inputs_ref, sems.at[0]),
+        pltpu.make_async_copy(gain_hbm, gain_ref, sems.at[1]),
+        pltpu.make_async_copy(keyval_hbm, keyval_ref, sems.at[2]),
+    ]
+    for at, here in enumerate(parts):
+        copies.append(pltpu.make_async_copy(query_hbm.at[:, here], query_ref.at[:, here], sems.at[3 + at]))
     for copy in copies:
         copy.start()
     order = to_row_order(2 * group)
-    gain = gain_ref[...].astype(jnp.float32)
     copies[0].wait()
+    copies[1].wait()
+    gain = gain_ref[...].astype(jnp.float32)[None]
     scaled = []
     for at in range(XS):
         block = jnp.concatenate([inputs_ref[step, group * at : group * (at + 1)] for step in range(2)], axis=0)
@@ -85,36 +90,50 @@
         terms_ref[at, :, queries + keyvals :] = (squares[:, :128] + squares[:, 128:]).astype(jnp.bfloat16)
         scaled.append((values * gain).astype(jnp.bfloat16))
     scaled = jnp.concatenate(scaled, axis=0)
-    for at in range(QUERY_CHUNKS + 1):
-        copies[1 + at].wait()
-        last = at == QUERY_CHUNKS
-        weights_ref, base = (keyval_ref, queries) if last else (query_ref, 0)
-        for start in range(0, keyvals, 256) if last else range(chunk * at, chunk * (at + 1), 256):
-            product = jnp.dot(scaled, weights_ref[:, start : start + 256], preferred_element_type=jnp.float32)
-            product = product.astype(jnp.bfloat16).reshape(XS, 2 * group, 256)
-            terms_ref[:, :, base + start : base + start + 256] = product
+    results = [pltpu.make_async_copy(rows_ref, rows_hbm, out_sems.at[0])]
+    results[0].start()
+    copies[2].wait()
+    product = jnp.dot(scaled, keyval_ref[...], preferred_element_type=jnp.float32)
+    terms_ref[:, :, queries : queries + keyvals] = product.astype(jnp.bfloat16).reshape(XS, 2 * group, keyvals)
+    for at, here in enumerate([slice(queries, terms_ref.shape[2])] + parts):
+        if at > 0:
+            copies[2 + at].wait()
+            for start in range(here.start, here.stop, 256):
+                product = jnp.dot(scaled, query_ref[:, start : start + 256], preferred_element_type=jnp.float32)
+                product = product.astype(jnp.bfloat16).reshape(XS, 2 * group, 256)
+                terms_ref[:, :, start : start + 256] = product
+        results.append(
+            pltpu.make_async_copy(terms_ref.at[:, :, here], terms_hbm.at[:, :, here], out_sems.at[1 + at])
+        )
+        results[-1].start()
+    for result in results:
+        result.wait()
 
 
 def first_terms(inputs, gain, w_query, w_keyval):
     steps, all_rows, width = inputs.shape
     columns = w_query.shape[1] + w_keyval.shape[1] + 128
     anywhere = pl.BlockSpec(memory_space=pl.ANY)
+    terms = (XS, steps * all_rows // XS, columns)
+    rows = (steps * all_rows, width)
     return pl.pallas_call(
         first_kernel,
-        out_shape=(
-            jax.ShapeDtypeStruct((XS, steps * all_rows // XS, columns), jnp.bfloat16),
-            jax.ShapeDtypeStruct((steps * all_rows, width), jnp.bfloat16),
-        ),
-        in_specs=[anywhere, pl.BlockSpec(memory_space=pltpu.VMEM), anywhere, anywhere],
+        out_shape=(jax.ShapeDtypeStruct(terms, jnp.bfloat16), jax.ShapeDtypeStruct(rows, jnp.bfloat16)),
+        in_specs=[anywhere] * 4,
+        out_specs=(anywhere, anywhere),
         scratch_shapes=[
             pltpu.VMEM(inputs.shape, jnp.bfloat16),
+            pltpu.VMEM(gain.shape, jnp.bfloat16),
             pltpu.VMEM(w_query.shape, jnp.bfloat16),
             pltpu.VMEM(w_keyval.shape, jnp.bfloat16),
+            pltpu.VMEM(terms, jnp.bfloat16),
+            pltpu.VMEM(rows, jnp.bfloat16),
+            pltpu.SemaphoreType.DMA((QUERY_CHUNKS + 3,)),
             pltpu.SemaphoreType.DMA((QUERY_CHUNKS + 2,)),
         ],
         compiler_params=pltpu.CompilerParams(vmem_limit_bytes=56 * 1024 * 1024),
         name="first_terms",
-    )(inputs, gain.reshape(1, width), w_query, w_keyval)
+    )(inputs, gain, w_query, w_keyval)
 
 
 def spread_kernel(rows_ref, weights_ref, copies_ref):
@@ -219,12 +238,14 @@
     squares_at = keyvals_at + 2 * head_dim
     rows = steps * all_rows
     x_rows = rows // XS
+    terms, input_rows = first_terms(inputs, attn_gain, w_query, keyval_weight)
+    sums = jnp.sum(exchange(terms, "x").astype(jnp.float32), axis=0).astype(jnp.bfloat16)
+    sums, w_gateup = lax.optimization_barrier((sums, w_gateup))
     gateup = w_gateup.transpose(1, 2, 0).astype(jnp.float32) * ffn_gain.astype(jnp.float32)
     gateup = gateup.astype(jnp.bfloat16).reshape(2 * local_hidden, local_width)
-
-    terms, input_rows = first_terms(inputs, attn_gain, w_query, keyval_weight)
-    sums = jnp.sum(exchange(terms, "x").astype(jnp.float32), axis=0)
-    sums = sum_over(sums, "z", ZS)
+    sums = exchange(sums.reshape(ZS, -1, sums.shape[1]), "z")
+    sums, gateup = lax.optimization_barrier((sums, gateup))
+    sums = jnp.sum(sums.astype(jnp.float32), axis=0)
     mean = jnp.sum(sums[:, squares_at:], axis=-1, keepdims=True) / D
     sums = (sums[:, :squares_at] * lax.rsqrt(mean + epsilon)).reshape(steps, local_rows, squares_at)
     offsets = positions[None, :] + jnp.arange(steps)[:, None]

time: 207 us -> 204 us (0.986)
  blocking collectives: 139 us -> 150 us
  waiting for transfers between devices: 26.1 us -> 19.1 us
  starting transfers between devices: 26.9 us -> 22.7 us
    all_to_all x7 -> x8, blocking collectives: 120 us -> 131 us  [exchange(): return lax.all_to_all(blocks, axis, 0, 0, tiled=True)]
    all_to_all x3 -> x2, waiting for transfers between devices: 26.1 us -> 19.1 us  [exchange(): return lax.all_to_all(blocks, axis, 0, 0, tiled=True)]
    all_to_all x3 -> x2, starting transfers between devices: 26.9 us -> 22.7 us  [exchange(): return lax.all_to_all(blocks, axis, 0, 0, tiled=True)]
  transfers between devices with their start and end apart: 3 -> 2, of which waited for: 3 -> 2; matrix products, arithmetic and copies ran while one was open for 0% -> 0% of each run, Pallas kernels for 0% -> 0%
where the time goes in v8:
time: 204 us
  blocking collectives  150 us (74%)
  starting transfers between devices  22.7 us (11%)
  waiting for transfers between devices  19.1 us (9%)
  Pallas kernels  5.17 us (3%)
  local copies, waits for them, and re-layouts  2.97 us (1%)
  other arithmetic  2.21 us (1%)
    all_to_all x8, blocking collectives, exchange(): return lax.all_to_all(blocks, axis, 0, 0, tiled=True)  131 us
    all_to_all x2, starting transfers between devices, exchange(): return lax.all_to_all(blocks, axis, 0, 0, tiled=True)  22.7 us
    all_to_all x2, waiting for transfers between devices, exchange(): return lax.all_to_all(blocks, axis, 0, 0, tiled=True)  19.1 us
    all_gather x2, blocking collectives, group_terms(): lax.all_gather(total.astype(jnp.bfloat16), 'core', axis=0, tiled=False)  18.2 us
  transfers between devices with their start and end apart: 2, of which 2 were waited for; matrix products, arithmetic and copies ran while one was open for 0% of the time, Pallas kernels for 0%

profile of v8, /device:TPU:1, one launch (start us, length us, event | category | flops | bytes accessed | tf_op | source)
XLA Modules:
  0.0 203.7 jit_solution(3760263918289058596)
XLA Ops:
  0.6 3.0 %first_terms.1 = (bf16[4,64,2432]{2,1,0:T(8,128)(2,1)}, bf16[256,256]{1,0:T(8,128)(2,1)}) custom-call(bf16[2,128,256]{2,1,0:T(8,128)(2,1)} %inputs_hbm.1, bf16[256]{0:T(256)(128)(2,1)} %gain_hbm.1, bf16[256,2048]{1,0:T(8,128)(2,1)} %query_hbm.1, bf16[256,256]{1,0:T(8,128)(2,1)} %bitcast.38), custom_call_target="tpu_custom_call" | custom-call | tf_op jit(solution)/shard_map/first_terms/pallas_call | solution.py:119
  3.7 16.5 %all_to_all.50 = bf16[4,64,2432]{2,1,0:T(8,128)(2,1)S(1)} all-to-all(bf16[4,64,2432]{2,1,0:T(8,128)(2,1)} %get-tuple-element.10), channel_id=1, replica_groups=mesh['x'=4,'z'=16,'y'=4,'core'=2] {'x'}, dimensions={0} | all-to-all | bytes 2490368 | tf_op jit(solution)/shard_map/all_to_all | solution.py:36
  20.2 0.0 copy-start.6
  20.2 0.2 reduce_sum.102
  20.4 0.8 reshape.196
  21.2 19.3 %all-to-all-start.1 = ((bf16[16,4,2432]{2,1,0:T(4,128)(2,1)}), bf16[16,4,2432]{2,1,0:T(4,128)(2,1)S(1)}, u32[]{:S(2)}, u32[]{:S(2)}) async-start(bf16[16,4,2432]{2,1,0:T(4,128)(2,1)} %reshape.196), calls=%async_computation.1 | async-start | bytes 622592 | tf_op jit(solution)/shard_map/all_to_all | solution.py:36
  40.5 0.0 copy-done.6
  40.6 0.0 copy-done.7
  40.6 0.1 add_convert_fusion.2
  40.7 0.0 copy-done.5
  40.7 0.1 iota_compare_fusion
  40.7 0.0 copy-done.3
  40.7 0.2 multiply_convert_fusion
  40.9 12.9 %all-to-all-done.1 = bf16[16,4,2432]{2,1,0:T(4,128)(2,1)S(1)} async-done(((bf16[16,4,2432]{2,1,0:T(4,128)(2,1)}), bf16[16,4,2432]{2,1,0:T(4,128)(2,1)S(1)}, u32[]{:S(2)}, u32[]{:S(2)}) %all-to-all-start.1) | async-done | bytes 311328 | tf_op jit(solution)/shard_map/all_to_all | solution.py:36
  53.8 0.1 convert_reduce_fusion
  53.9 0.1 slice_reduce_fusion.1
  54.1 0.1 slice_multiply_fusion
  54.2 0.1 fusion.20
  54.3 0.1 fusion.21
  54.4 0.1 subtract_convert_fusion.1
  54.5 0.1 pad_maximum_fusion
  54.6 0.0 copy-done.4
  54.6 0.3 fusion.22
  54.9 0.2 fusion.23
  55.2 0.2 fusion.8
  55.4 0.2 fusion.3
  55.6 0.2 fusion.1
  55.9 0.1 broadcast_in_dim.45
  56.0 24.6 %all_to_all.51 = bf16[16,4,2048]{2,1,0:T(4,128)(2,1)S(1)} all-to-all(bf16[16,4,2048]{2,1,0:T(4,128)(2,1)S(1)} %broadcast_in_dim.45), channel_id=1, replica_groups=mesh['x'=4,'z'=16,'y'=4,'core'=2] {'z'}, dimensions={0} | all-to-all | bytes 524288 | tf_op jit(solution)/shard_map/all_to_all | solution.py:36
  80.5 0.1 broadcast_in_dim.46
  80.6 0.1 broadcast_in_dim.78
  80.7 0.0 copy-start
  80.7 12.3 %all_to_all.52 = bf16[4,64,2048]{2,1,0:T(8,128)(2,1)S(1)} all-to-all(bf16[4,64,2048]{2,1,0:T(8,128)(2,1)S(1)} %broadcast_in_dim.78), channel_id=1, replica_groups=mesh['x'=4,'z'=16,'y'=4,'core'=2] {'x'}, dimensions={0} | all-to-all | bytes 2097152 | tf_op jit(solution)/shard_map/all_to_all | solution.py:36
  93.0 0.0 copy-done
  93.0 0.4 spread_dot.2
  93.5 0.0 copy-start.2
  93.5 11.1 %all_to_all.53 = bf16[4,256,256]{2,1,0:T(8,128)(2,1)S(1)} all-to-all(bf16[4,256,256]{2,1,0:T(8,128)(2,1)S(1)} %spread_dot.2), channel_id=1, replica_groups=mesh['x'=4,'z'=16,'y'=4,'core'=2] {'y'}, dimensions={0} | all-to-all | bytes 1048576 | tf_op jit(solution)/shard_map/all_to_all | solution.py:36
  104.6 0.1 reduce_sum.107
  104.6 11.0 %all-gather = bf16[512,256]{1,0:T(8,128)(2,1)S(1)} all-gather(bf16[256,256]{1,0:T(8,128)(2,1)S(1)} %reduce_sum.107), channel_id=2, replica_groups=mesh['x'=4,'z'=16,'y'=4,'core'=2] {'core'}, dimensions={0}, use_global_device_ids=true | all-gather | bytes 393216 | tf_op jit(solution)/shard_map/all_gather | solution.py:51
  115.6 0.0 copy-done.2
  115.6 0.6 gateup_terms.1
  116.2 15.9 %all_to_all.54 = bf16[4,64,1792]{2,1,0:T(8,128)(2,1)S(1)} all-to-all(bf16[4,64,1792]{2,1,0:T(8,128)(2,1)S(1)} %get-tuple-element.16), channel_id=1, replica_groups=mesh['x'=4,'z'=16,'y'=4,'core'=2] {'x'}, dimensions={0} | all-to-all | bytes 1835008 | tf_op jit(solution)/shard_map/all_to_all | solution.py:36
  132.1 0.2 reduce_sum.108
  132.3 0.1 reshape.203
  132.3 20.7 %all_to_all.55 = bf16[16,4,1792]{2,1,0:T(4,128)(2,1)S(1)} all-to-all(bf16[16,4,1792]{2,1,0:T(4,128)(2,1)S(1)} %reshape.203), channel_id=1, replica_groups=mesh['x'=4,'z'=16,'y'=4,'core'=2] {'z'}, dimensions={0} | all-to-all | bytes 458752 | tf_op jit(solution)/shard_map/all_to_all | solution.py:36
  153.0 0.1 convert_reduce_fusion.1
  153.1 0.1 slice_reduce_fusion
  153.2 0.1 slice_multiply_fusion.1
  153.3 0.1 fusion.12
  153.4 21.4 %all_to_all.56 = bf16[16,4,832]{2,1,0:T(4,128)(2,1)S(1)} all-to-all(bf16[16,4,832]{2,1,0:T(4,128)(2,1)S(1)} %broadcast_in_dim.79), channel_id=1, replica_groups=mesh['x'=4,'z'=16,'y'=4,'core'=2] {'z'}, dimensions={0} | all-to-all | bytes 212992 | tf_op jit(solution)/shard_map/all_to_all | solution.py:36
  174.9 0.1 broadcast_in_dim.80
  175.0 9.0 %all_to_all.57 = bf16[4,64,832]{2,1,0:T(8,128)(2,1)S(1)} all-to-all(bf16[4,64,832]{2,1,0:T(8,128)(2,1)S(1)} %broadcast_in_dim.81), channel_id=1, replica_groups=mesh['x'=4,'z'=16,'y'=4,'core'=2] {'x'}, dimensions={0} | all-to-all | bytes 851968 | tf_op jit(solution)/shard_map/all_to_all | solution.py:36
  183.9 0.0 copy-done.1
  183.9 1.1 spread_dot.3
  185.0 3.5 %all-to-all-start.9 = ((bf16[4,256,256]{2,1,0:T(8,128)(2,1)}), bf16[4,256,256]{2,1,0:T(8,128)(2,1)S(1)}, u32[]{:S(2)}, u32[]{:S(2)}) async-start(bf16[4,256,256]{2,1,0:T(8,128)(2,1)} %spread_dot.3), calls=%async_computation.9 | async-start | bytes 1048576 | tf_op jit(solution)/shard_map/all_to_all | solution.py:36
  188.5 0.1 maximum_bitcast_fusion
  188.6 0.6 copy.60
  189.2 6.2 %all-to-all-done.9 = bf16[4,256,256]{2,1,0:T(8,128)(2,1)S(1)} async-done(((bf16[4,256,256]{2,1,0:T(8,128)(2,1)}), bf16[4,256,256]{2,1,0:T(8,128)(2,1)S(1)}, u32[]{:S(2)}, u32[]{:S(2)}) %all-to-all-start.9) | async-done | bytes 524320 | tf_op jit(solution)/shard_map/all_to_all | solution.py:36
  195.4 0.1 reduce_sum.111
  195.5 7.2 %all-gather.1 = bf16[512,256]{1,0:T(8,128)(2,1)S(1)} all-gather(bf16[256,256]{1,0:T(8,128)(2,1)S(1)} %reduce_sum.111), channel_id=3, replica_groups=mesh['x'=4,'z'=16,'y'=4,'core'=2] {'core'}, dimensions={0}, use_global_device_ids=true | all-gather | bytes 393216 | tf_op jit(solution)/shard_map/all_gather | solution.py:51
  202.8 0.1 fusion.7
  202.8 0.1 reshape.205
  202.9 0.1 copy.59
  203.0 0.7 reshape.206
  (25 shorter events, 0.3 us)
Async XLA Ops:
  20.2 20.3 %copy-start.6 = (bf16[256]{0:T(256)(128)(2,1)S(1)}, bf16[256]{0:T(256)(128)(2,1)}, u32[]{:S(2)}) copy-start(bf16[256]{0:T(256)(128)(2,1)} %param.16) | copy-start | bytes 1540
  20.2 20.4 %copy-start.7 = (s32[2]{0:T(128)S(1)}, s32[2]{0:T(128)}, u32[]{:S(2)}) copy-start(s32[2]{0:T(128)} %param.21) | copy-start | bytes 28
  20.2 20.4 %copy-start.5 = (s32[2]{0:T(128)S(1)}, s32[2]{0:T(128)}, u32[]{:S(2)}) copy-start(s32[2]{0:T(128)} %param.20) | copy-start | bytes 28
  20.2 20.5 %copy-start.3 = (bf16[256,2,832]{0,2,1:T(8,128)(2,1)S(1)}, bf16[256,2,832]{0,2,1:T(8,128)(2,1)}, u32[]{:S(2)}) copy-start(bf16[256,2,832]{0,2,1:T(8,128)(2,1)} %param.17) | copy-start | bytes 2555908
  21.2 32.6 %all-to-all-start.1 = ((bf16[16,4,2432]{2,1,0:T(4,128)(2,1)}), bf16[16,4,2432]{2,1,0:T(4,128)(2,1)S(1)}, u32[]{:S(2)}, u32[]{:S(2)}) async-start(bf16[16,4,2432]{2,1,0:T(4,128)(2,1)} %reshape.196), calls=%async_computation.1 | async-start | bytes 622592 | tf_op jit(solution)/shard_map/all_to_all | solution.py:36
  40.7 13.9 %copy-start.4 = (bf16[2,768,1,256]{3,1,2,0:T(8,128)(2,1)S(1)}, bf16[2,768,1,256]{3,1,2,0:T(8,128)(2,1)}, u32[]{:S(2)}) copy-start(bf16[2,768,1,256]{3,1,2,0:T(8,128)(2,1)} %param.19) | copy-start | bytes 2359300
  80.7 12.3 %copy-start = (bf16[2048,256]{1,0:T(8,128)(2,1)S(1)}, bf16[2048,256]{1,0:T(8,128)(2,1)}, u32[]{:S(2)}) copy-start(bf16[2048,256]{1,0:T(8,128)(2,1)} %weights_ref.2) | copy-start | bytes 3145732
  93.5 22.1 %copy-start.2 = (bf16[256,256]{1,0:T(8,128)(2,1)S(1)}, bf16[256,256]{1,0:T(8,128)(2,1)}, u32[]{:S(2)}) copy-start(bf16[256,256]{1,0:T(8,128)(2,1)} %get-tuple-element.14.rows_ref) | copy-start | bytes 393220
  153.0 30.9 %copy-start.1 = (bf16[832,256]{1,0:T(8,128)(2,1)S(1)}, bf16[832,256]{1,0:T(8,128)(2,1)}, u32[]{:S(2)}) copy-start(bf16[832,256]{1,0:T(8,128)(2,1)} %weights_ref.3) | copy-start | bytes 1277956
  185.0 10.4 %all-to-all-start.9 = ((bf16[4,256,256]{2,1,0:T(8,128)(2,1)}), bf16[4,256,256]{2,1,0:T(8,128)(2,1)S(1)}, u32[]{:S(2)}, u32[]{:S(2)}) async-start(bf16[4,256,256]{2,1,0:T(8,128)(2,1)} %spread_dot.3), calls=%async_computation.9 | async-start | bytes 1048576 | tf_op jit(solution)/shard_map/all_to_all | solution.py:36

commit v9 on v8

--- a/solution.py
+++ b/solution.py
@@ -18,12 +18,15 @@
 QUERY_CHUNKS = 4
 
 
-def rotate(vectors, offsets):
+def angles_of(offsets, head_dim):
+    half_size = head_dim // 2
+    freqs = rope_base ** (-(jnp.arange(half_size, dtype=jnp.float32) * 2.0 / head_dim))
+    angles = offsets.astype(jnp.float32)[..., None] * freqs
+    return jnp.cos(angles), jnp.sin(angles)
+
+
+def rotate(vectors, cosine, sine):
     half_size = vectors.shape[-1] // 2
-    freqs = rope_base ** (-(jnp.arange(half_size, dtype=jnp.float32) * 2.0 / vectors.shape[-1]))
-    angles = offsets.astype(jnp.float32)[..., None] * freqs
-    cosine = jnp.cos(angles)
-    sine = jnp.sin(angles)
     first_half = vectors[..., :half_size]
     second_half = vectors[..., half_size:]
     return jnp.concatenate(
@@ -185,15 +188,14 @@
     )(pair, rows, weights)
 
 
-def attend(queries, kv_cache, lengths, fresh_keys, fresh_values, score_scale):
+def attend(queries, kv_cache, live, fresh_keys, fresh_values, score_scale):
     rows, steps, heads, head_dim = queries.shape
     merged = queries.reshape(rows, steps * heads, head_dim)
     scores = (
         jnp.einsum("rgd,rld->rgl", merged, kv_cache[..., :head_dim], preferred_element_type=jnp.float32)
         * score_scale
     )
-    live = jnp.arange(kv_cache.shape[1])[None, None, :] < lengths[:, None, None]
-    scores = jnp.where(live, scores, masked_score)
+    scores = jnp.where(live[:, None, :] > 0.0, scores, masked_score)
     fresh_scores = (
         jnp.einsum("rgd,rtd->rgt", merged, fresh_keys, preferred_element_type=jnp.float32) * score_scale
     )
@@ -239,26 +241,29 @@
     rows = steps * all_rows
     x_rows = rows // XS
     terms, input_rows = first_terms(inputs, attn_gain, w_query, keyval_weight)
-    sums = jnp.sum(exchange(terms, "x").astype(jnp.float32), axis=0).astype(jnp.bfloat16)
-    sums, w_gateup = lax.optimization_barrier((sums, w_gateup))
+    terms, w_gateup, positions, lengths = lax.optimization_barrier((terms, w_gateup, positions, lengths))
     gateup = w_gateup.transpose(1, 2, 0).astype(jnp.float32) * ffn_gain.astype(jnp.float32)
     gateup = gateup.astype(jnp.bfloat16).reshape(2 * local_hidden, local_width)
-    sums = exchange(sums.reshape(ZS, -1, sums.shape[1]), "z")
-    sums, gateup = lax.optimization_barrier((sums, gateup))
+    cosine, sine = angles_of(positions[None, :] + jnp.arange(steps)[:, None], head_dim)
+    live = (jnp.arange(kv_cache.shape[1])[None, :] < lengths[:, None]).astype(jnp.float32)
+    sums = exchange(terms, "x")
+    sums, gateup, cosine, sine, live = lax.optimization_barrier((sums, gateup, cosine, sine, live))
     sums = jnp.sum(sums.astype(jnp.float32), axis=0)
+    sums = sum_over(sums, "z", ZS)
     mean = jnp.sum(sums[:, squares_at:], axis=-1, keepdims=True) / D
     sums = (sums[:, :squares_at] * lax.rsqrt(mean + epsilon)).reshape(steps, local_rows, squares_at)
-    offsets = positions[None, :] + jnp.arange(steps)[:, None]
     queries = rotate(
-        sums[..., :keyvals_at].reshape(steps, local_rows, local_queries, head_dim), offsets[..., None]
+        sums[..., :keyvals_at].reshape(steps, local_rows, local_queries, head_dim),
+        cosine[..., None, :],
+        sine[..., None, :],
     ).astype(jnp.bfloat16)
-    keys_new = rotate(sums[..., keyvals_at : keyvals_at + head_dim], offsets).astype(jnp.bfloat16)
+    keys_new = rotate(sums[..., keyvals_at : keyvals_at + head_dim], cosine, sine).astype(jnp.bfloat16)
     values_new = sums[..., keyvals_at + head_dim :].astype(jnp.bfloat16)
     new_entries = jnp.concatenate([keys_new, values_new], axis=-1)[:, :, None, :]
     mixed = attend(
         queries.transpose(1, 0, 2, 3),
         kv_cache.reshape(local_rows, -1, 2 * head_dim),
-        lengths,
+        live,
         keys_new.transpose(1, 0, 2),
         values_new.transpose(1, 0, 2),
         score_scale,

time: 204 us -> 205 us (level)
  blocking collectives: 150 us -> 133 us
  waiting for transfers between devices: 19.1 us -> 30.7 us
  starting transfers between devices: 22.7 us -> 28.3 us
    all_to_all x8 -> x7, blocking collectives: 131 us -> 115 us  [exchange(): return lax.all_to_all(blocks, axis, 0, 0, tiled=True)]
    all_to_all x2 -> x3, waiting for transfers between devices: 19.1 us -> 30.7 us  [exchange(): return lax.all_to_all(blocks, axis, 0, 0, tiled=True)]
    all_to_all x2 -> x3, starting transfers between devices: 22.7 us -> 28.3 us  [exchange(): return lax.all_to_all(blocks, axis, 0, 0, tiled=True)]
  transfers between devices with their start and end apart: 2 -> 3, of which waited for: 2 -> 3; matrix products, arithmetic and copies ran while one was open for 0% -> 1% of each run, Pallas kernels for 0% -> 0%
where the time goes in v9:
time: 205 us; the launch traced here: 204 us
  blocking collectives  133 us (65%)
  waiting for transfers between devices  30.7 us (15%)
  starting transfers between devices  28.3 us (14%)
  Pallas kernels  5.17 us (3%)
  local copies, waits for them, and re-layouts  2.98 us (1%)
  other arithmetic  2.19 us (1%)
    all_to_all x7, blocking collectives, exchange(): return lax.all_to_all(blocks, axis, 0, 0, tiled=True)  115 us
    all_to_all x3, waiting for transfers between devices, exchange(): return lax.all_to_all(blocks, axis, 0, 0, tiled=True)  30.7 us
    all_to_all x3, starting transfers between devices, exchange(): return lax.all_to_all(blocks, axis, 0, 0, tiled=True)  28.3 us
    all_gather x2, blocking collectives, group_terms(): lax.all_gather(total.astype(jnp.bfloat16), 'core', axis=0, tiled=False)  18.2 us
  transfers between devices with their start and end apart: 3, of which 3 were waited for; matrix products, arithmetic and copies ran while one was open for 1% of the time, Pallas kernels for 0%

profile of v9, /device:TPU:1, one launch (start us, length us, event | category | flops | bytes accessed | tf_op | source)
XLA Modules:
  0.0 204.0 jit_solution(7772972041910350262)
XLA Ops:
  0.6 3.0 %first_terms.1 = (bf16[4,64,2432]{2,1,0:T(8,128)(2,1)}, bf16[256,256]{1,0:T(8,128)(2,1)}) custom-call(bf16[2,128,256]{2,1,0:T(8,128)(2,1)} %inputs_hbm.1, bf16[256]{0:T(256)(128)(2,1)} %gain_hbm.1, bf16[256,2048]{1,0:T(8,128)(2,1)} %query_hbm.1, bf16[256,256]{1,0:T(8,128)(2,1)} %bitcast.38), custom_call_target="tpu_custom_call" | custom-call | tf_op jit(solution)/shard_map/first_terms/pallas_call | solution.py:122
  3.7 0.0 copy-start.6
  3.7 0.0 copy-start.7
  3.7 0.0 copy-start.5
  3.7 0.0 copy-start.3
  3.7 5.0 %all-to-all-start = ((bf16[4,64,2432]{2,1,0:T(8,128)(2,1)}), bf16[4,64,2432]{2,1,0:T(8,128)(2,1)S(1)}, u32[]{:S(2)}, u32[]{:S(2)}) async-start(bf16[4,64,2432]{2,1,0:T(8,128)(2,1)} %get-tuple-element.16), calls=%async_computation | async-start | bytes 2490368 | tf_op jit(solution)/shard_map/all_to_all | solution.py:39
  8.7 0.0 copy-done.6
  8.7 0.0 copy-done.7
  8.7 0.1 add_convert_fusion.2
  8.8 0.1 multiply_sine_fusion
  8.9 0.0 copy-done.5
  8.9 0.1 compare_convert_fusion
  9.0 0.2 multiply_convert_fusion
  9.2 10.9 %all-to-all-done = bf16[4,64,2432]{2,1,0:T(8,128)(2,1)S(1)} async-done(((bf16[4,64,2432]{2,1,0:T(8,128)(2,1)}), bf16[4,64,2432]{2,1,0:T(8,128)(2,1)S(1)}, u32[]{:S(2)}, u32[]{:S(2)}) %all-to-all-start) | async-done | bytes 1245216 | tf_op jit(solution)/shard_map/all_to_all | solution.py:39
  20.1 0.2 reduce_sum.102
  20.3 0.0 copy-start.4
  20.3 0.8 reshape.143
  21.1 19.9 %all-to-all-start.1 = ((bf16[16,4,2432]{2,1,0:T(4,128)(2,1)}), bf16[16,4,2432]{2,1,0:T(4,128)(2,1)S(1)}, u32[]{:S(2)}, u32[]{:S(2)}) async-start(bf16[16,4,2432]{2,1,0:T(4,128)(2,1)} %reshape.143), calls=%async_computation.1 | async-start | bytes 622592 | tf_op jit(solution)/shard_map/all_to_all | solution.py:39
  41.0 13.5 %all-to-all-done.1 = bf16[16,4,2432]{2,1,0:T(4,128)(2,1)S(1)} async-done(((bf16[16,4,2432]{2,1,0:T(4,128)(2,1)}), bf16[16,4,2432]{2,1,0:T(4,128)(2,1)S(1)}, u32[]{:S(2)}, u32[]{:S(2)}) %all-to-all-start.1) | async-done | bytes 311328 | tf_op jit(solution)/shard_map/all_to_all | solution.py:39
  54.6 0.1 convert_reduce_fusion
  54.7 0.1 slice_reduce_fusion.1
  54.8 0.1 slice_multiply_fusion
  54.9 0.1 fusion.20
  55.0 0.1 fusion.21
  55.2 0.1 pad_maximum_fusion
  55.2 0.3 fusion.22
  55.6 0.2 fusion.23
  55.8 0.2 fusion.8
  56.0 0.2 fusion.3
  56.3 0.2 fusion.1
  56.5 0.1 broadcast_in_dim.45
  56.6 24.3 %all_to_all.50 = bf16[16,4,2048]{2,1,0:T(4,128)(2,1)S(1)} all-to-all(bf16[16,4,2048]{2,1,0:T(4,128)(2,1)S(1)} %broadcast_in_dim.45), channel_id=1, replica_groups=mesh['x'=4,'z'=16,'y'=4,'core'=2] {'z'}, dimensions={0} | all-to-all | bytes 524288 | tf_op jit(solution)/shard_map/all_to_all | solution.py:39
  80.9 0.1 broadcast_in_dim.46
  80.9 0.1 broadcast_in_dim.78
  81.1 0.0 copy-start
  81.1 12.3 %all_to_all.51 = bf16[4,64,2048]{2,1,0:T(8,128)(2,1)S(1)} all-to-all(bf16[4,64,2048]{2,1,0:T(8,128)(2,1)S(1)} %broadcast_in_dim.78), channel_id=1, replica_groups=mesh['x'=4,'z'=16,'y'=4,'core'=2] {'x'}, dimensions={0} | all-to-all | bytes 2097152 | tf_op jit(solution)/shard_map/all_to_all | solution.py:39
  93.4 0.4 spread_dot.2
  93.8 0.0 copy-start.2
  93.8 11.1 %all_to_all.52 = bf16[4,256,256]{2,1,0:T(8,128)(2,1)S(1)} all-to-all(bf16[4,256,256]{2,1,0:T(8,128)(2,1)S(1)} %spread_dot.2), channel_id=1, replica_groups=mesh['x'=4,'z'=16,'y'=4,'core'=2] {'y'}, dimensions={0} | all-to-all | bytes 1048576 | tf_op jit(solution)/shard_map/all_to_all | solution.py:39
  104.9 0.1 reduce_sum.107
  105.0 11.0 %all-gather = bf16[512,256]{1,0:T(8,128)(2,1)S(1)} all-gather(bf16[256,256]{1,0:T(8,128)(2,1)S(1)} %reduce_sum.107), channel_id=2, replica_groups=mesh['x'=4,'z'=16,'y'=4,'core'=2] {'core'}, dimensions={0}, use_global_device_ids=true | all-gather | bytes 393216 | tf_op jit(solution)/shard_map/all_gather | solution.py:54
  115.9 0.6 gateup_terms.1
  116.6 15.9 %all_to_all.53 = bf16[4,64,1792]{2,1,0:T(8,128)(2,1)S(1)} all-to-all(bf16[4,64,1792]{2,1,0:T(8,128)(2,1)S(1)} %get-tuple-element.26), channel_id=1, replica_groups=mesh['x'=4,'z'=16,'y'=4,'core'=2] {'x'}, dimensions={0} | all-to-all | bytes 1835008 | tf_op jit(solution)/shard_map/all_to_all | solution.py:39
  132.4 0.2 reduce_sum.108
  132.6 0.1 reshape.149
  132.7 20.7 %all_to_all.54 = bf16[16,4,1792]{2,1,0:T(4,128)(2,1)S(1)} all-to-all(bf16[16,4,1792]{2,1,0:T(4,128)(2,1)S(1)} %reshape.149), channel_id=1, replica_groups=mesh['x'=4,'z'=16,'y'=4,'core'=2] {'z'}, dimensions={0} | all-to-all | bytes 458752 | tf_op jit(solution)/shard_map/all_to_all | solution.py:39
  153.4 0.1 convert_reduce_fusion.1
  153.4 0.1 slice_reduce_fusion
  153.6 0.1 slice_multiply_fusion.1
  153.6 0.1 fusion.12
  153.8 21.4 %all_to_all.55 = bf16[16,4,832]{2,1,0:T(4,128)(2,1)S(1)} all-to-all(bf16[16,4,832]{2,1,0:T(4,128)(2,1)S(1)} %broadcast_in_dim.79), channel_id=1, replica_groups=mesh['x'=4,'z'=16,'y'=4,'core'=2] {'z'}, dimensions={0} | all-to-all | bytes 212992 | tf_op jit(solution)/shard_map/all_to_all | solution.py:39
  175.2 0.1 broadcast_in_dim.80
  175.3 9.0 %all_to_all.56 = bf16[4,64,832]{2,1,0:T(8,128)(2,1)S(1)} all-to-all(bf16[4,64,832]{2,1,0:T(8,128)(2,1)S(1)} %broadcast_in_dim.81), channel_id=1, replica_groups=mesh['x'=4,'z'=16,'y'=4,'core'=2] {'x'}, dimensions={0} | all-to-all | bytes 851968 | tf_op jit(solution)/shard_map/all_to_all | solution.py:39
  184.3 1.1 spread_dot.3
  185.4 3.5 %all-to-all-start.9 = ((bf16[4,256,256]{2,1,0:T(8,128)(2,1)}), bf16[4,256,256]{2,1,0:T(8,128)(2,1)S(1)}, u32[]{:S(2)}, u32[]{:S(2)}) async-start(bf16[4,256,256]{2,1,0:T(8,128)(2,1)} %spread_dot.3), calls=%async_computation.9 | async-start | bytes 1048576 | tf_op jit(solution)/shard_map/all_to_all | solution.py:39
  188.9 0.1 maximum_bitcast_fusion
  188.9 0.6 copy.60
  189.5 6.2 %all-to-all-done.9 = bf16[4,256,256]{2,1,0:T(8,128)(2,1)S(1)} async-done(((bf16[4,256,256]{2,1,0:T(8,128)(2,1)}), bf16[4,256,256]{2,1,0:T(8,128)(2,1)S(1)}, u32[]{:S(2)}, u32[]{:S(2)}) %all-to-all-start.9) | async-done | bytes 524320 | tf_op jit(solution)/shard_map/all_to_all | solution.py:39
  195.8 0.1 reduce_sum.111
  195.8 7.2 %all-gather.1 = bf16[512,256]{1,0:T(8,128)(2,1)S(1)} all-gather(bf16[256,256]{1,0:T(8,128)(2,1)S(1)} %reduce_sum.111), channel_id=3, replica_groups=mesh['x'=4,'z'=16,'y'=4,'core'=2] {'core'}, dimensions={0}, use_global_device_ids=true | all-gather | bytes 393216 | tf_op jit(solution)/shard_map/all_gather | solution.py:54
  203.1 0.1 fusion.7
  203.2 0.1 reshape.151
  203.2 0.1 copy.59
  203.3 0.7 reshape.152
  (28 shorter events, 0.3 us)
Async XLA Ops:
  3.7 5.0 %copy-start.6 = (bf16[256]{0:T(256)(128)(2,1)S(1)}, bf16[256]{0:T(256)(128)(2,1)}, u32[]{:S(2)}) copy-start(bf16[256]{0:T(256)(128)(2,1)} %param.16) | copy-start | bytes 1540
  3.7 5.1 %copy-start.7 = (s32[2]{0:T(128)S(1)}, s32[2]{0:T(128)}, u32[]{:S(2)}) copy-start(s32[2]{0:T(128)} %param.21) | copy-start | bytes 28
  3.7 5.2 %copy-start.5 = (s32[2]{0:T(128)S(1)}, s32[2]{0:T(128)}, u32[]{:S(2)}) copy-start(s32[2]{0:T(128)} %param.20) | copy-start | bytes 28
  3.7 5.3 %copy-start.3 = (bf16[256,2,832]{0,2,1:T(8,128)(2,1)S(1)}, bf16[256,2,832]{0,2,1:T(8,128)(2,1)}, u32[]{:S(2)}) copy-start(bf16[256,2,832]{0,2,1:T(8,128)(2,1)} %param.17) | copy-start | bytes 2555908
  3.7 16.4 %all-to-all-start = ((bf16[4,64,2432]{2,1,0:T(8,128)(2,1)}), bf16[4,64,2432]{2,1,0:T(8,128)(2,1)S(1)}, u32[]{:S(2)}, u32[]{:S(2)}) async-start(bf16[4,64,2432]{2,1,0:T(8,128)(2,1)} %get-tuple-element.16), calls=%async_computation | async-start | bytes 2490368 | tf_op jit(solution)/shard_map/all_to_all | solution.py:39
  20.3 34.9 %copy-start.4 = (bf16[2,768,1,256]{3,1,2,0:T(8,128)(2,1)S(1)}, bf16[2,768,1,256]{3,1,2,0:T(8,128)(2,1)}, u32[]{:S(2)}) copy-start(bf16[2,768,1,256]{3,1,2,0:T(8,128)(2,1)} %param.19) | copy-start | bytes 2359300
  21.1 33.4 %all-to-all-start.1 = ((bf16[16,4,2432]{2,1,0:T(4,128)(2,1)}), bf16[16,4,2432]{2,1,0:T(4,128)(2,1)S(1)}, u32[]{:S(2)}, u32[]{:S(2)}) async-start(bf16[16,4,2432]{2,1,0:T(4,128)(2,1)} %reshape.143), calls=%async_computation.1 | async-start | bytes 622592 | tf_op jit(solution)/shard_map/all_to_all | solution.py:39
  81.1 12.3 %copy-start = (bf16[2048,256]{1,0:T(8,128)(2,1)S(1)}, bf16[2048,256]{1,0:T(8,128)(2,1)}, u32[]{:S(2)}) copy-start(bf16[2048,256]{1,0:T(8,128)(2,1)} %weights_ref.2) | copy-start | bytes 3145732
  93.8 22.1 %copy-start.2 = (bf16[256,256]{1,0:T(8,128)(2,1)S(1)}, bf16[256,256]{1,0:T(8,128)(2,1)}, u32[]{:S(2)}) copy-start(bf16[256,256]{1,0:T(8,128)(2,1)} %get-tuple-element.24.rows_ref) | copy-start | bytes 393220
  153.4 30.9 %copy-start.1 = (bf16[832,256]{1,0:T(8,128)(2,1)S(1)}, bf16[832,256]{1,0:T(8,128)(2,1)}, u32[]{:S(2)}) copy-start(bf16[832,256]{1,0:T(8,128)(2,1)} %weights_ref.3) | copy-start | bytes 1277956
  185.4 10.4 %all-to-all-start.9 = ((bf16[4,256,256]{2,1,0:T(8,128)(2,1)}), bf16[4,256,256]{2,1,0:T(8,128)(2,1)S(1)}, u32[]{:S(2)}, u32[]{:S(2)}) async-start(bf16[4,256,256]{2,1,0:T(8,128)(2,1)} %spread_dot.3), calls=%async_computation.9 | async-start | bytes 1048576 | tf_op jit(solution)/shard_map/all_to_all | solution.py:39

commit v10 on v8

--- a/solution.py
+++ b/solution.py
@@ -136,6 +136,25 @@
     )(inputs, gain, w_query, w_keyval)
 
 
+def parts_kernel(received_ref, blocks_ref):
+    count = blocks_ref.shape[1]
+    total = received_ref[0].astype(jnp.float32)
+    for at in range(1, received_ref.shape[0]):
+        total += received_ref[at].astype(jnp.float32)
+    for at in range(blocks_ref.shape[0]):
+        blocks_ref[at] = total[count * at : count * (at + 1)].astype(jnp.bfloat16)
+
+
+def sum_parts(received, blocks):
+    _, rows, columns = received.shape
+    return pl.pallas_call(
+        parts_kernel,
+        out_shape=jax.ShapeDtypeStruct((blocks, rows // blocks, columns), jnp.bfloat16),
+        compiler_params=pltpu.CompilerParams(vmem_limit_bytes=24 * 1024 * 1024),
+        name="sum_parts",
+    )(received)
+
+
 def spread_kernel(rows_ref, weights_ref, copies_ref):
     product = jnp.dot(rows_ref[...], weights_ref[...], preferred_element_type=jnp.float32)
     product = product.astype(jnp.bfloat16)
@@ -239,11 +258,11 @@
     rows = steps * all_rows
     x_rows = rows // XS
     terms, input_rows = first_terms(inputs, attn_gain, w_query, keyval_weight)
-    sums = jnp.sum(exchange(terms, "x").astype(jnp.float32), axis=0).astype(jnp.bfloat16)
+    sums = sum_parts(exchange(terms, "x"), ZS)
     sums, w_gateup = lax.optimization_barrier((sums, w_gateup))
     gateup = w_gateup.transpose(1, 2, 0).astype(jnp.float32) * ffn_gain.astype(jnp.float32)
     gateup = gateup.astype(jnp.bfloat16).reshape(2 * local_hidden, local_width)
-    sums = exchange(sums.reshape(ZS, -1, sums.shape[1]), "z")
+    sums = exchange(sums, "z")
     sums, gateup = lax.optimization_barrier((sums, gateup))
     sums = jnp.sum(sums.astype(jnp.float32), axis=0)
     mean = jnp.sum(sums[:, squares_at:], axis=-1, keepdims=True) / D

time: 204 us -> 204 us (level)
  no operation moved by 1% of the time
where the time goes in v10:
time: 204 us
  blocking collectives  150 us (74%)
  starting transfers between devices  22.7 us (11%)
  waiting for transfers between devices  19.1 us (9%)
  Pallas kernels  6.05 us (3%)
  local copies, waits for them, and re-layouts  2.18 us (1%)
    all_to_all x8, blocking collectives, exchange(): return lax.all_to_all(blocks, axis, 0, 0, tiled=True)  131 us
    all_to_all x2, starting transfers between devices, exchange(): return lax.all_to_all(blocks, axis, 0, 0, tiled=True)  22.7 us
    all_to_all x2, waiting for transfers between devices, exchange(): return lax.all_to_all(blocks, axis, 0, 0, tiled=True)  19.1 us
    all_gather x2, blocking collectives, group_terms(): lax.all_gather(total.astype(jnp.bfloat16), 'core', axis=0, tiled=False)  18.2 us
  transfers between devices with their start and end apart: 2, of which 2 were waited for; matrix products, arithmetic and copies ran while one was open for 0% of the time, Pallas kernels for 0%

profile of v10, /device:TPU:1, one launch (start us, length us, event | category | flops | bytes accessed | tf_op | source)
XLA Modules:
  0.0 203.6 jit_solution(17265600295076808234)
XLA Ops:
  0.6 3.0 %first_terms.1 = (bf16[4,64,2432]{2,1,0:T(8,128)(2,1)}, bf16[256,256]{1,0:T(8,128)(2,1)}) custom-call(bf16[2,128,256]{2,1,0:T(8,128)(2,1)} %inputs_hbm.1, bf16[256]{0:T(256)(128)(2,1)} %gain_hbm.1, bf16[256,2048]{1,0:T(8,128)(2,1)} %query_hbm.1, bf16[256,256]{1,0:T(8,128)(2,1)} %bitcast.38), custom_call_target="tpu_custom_call" | custom-call | tf_op jit(solution)/shard_map/first_terms/pallas_call | solution.py:119
  3.7 16.5 %all_to_all.50.received_ref = bf16[4,64,2432]{2,1,0:T(8,128)(2,1)S(1)} all-to-all(bf16[4,64,2432]{2,1,0:T(8,128)(2,1)} %get-tuple-element.10), channel_id=1, replica_groups=mesh['x'=4,'z'=16,'y'=4,'core'=2] {'x'}, dimensions={0} | all-to-all | bytes 2490368 | tf_op jit(solution)/shard_map/all_to_all | solution.py:36
  20.2 0.0 copy-start.6
  20.2 0.0 copy-start.5
  20.2 0.9 sum_parts.1
  21.1 19.3 %all-to-all-start.1 = ((bf16[16,4,2432]{2,1,0:T(4,128)(2,1)}), bf16[16,4,2432]{2,1,0:T(4,128)(2,1)S(1)}, u32[]{:S(2)}, u32[]{:S(2)}) async-start(bf16[16,4,2432]{2,1,0:T(4,128)(2,1)} %sum_parts.1), calls=%async_computation.1 | async-start | bytes 622592 | tf_op jit(solution)/shard_map/all_to_all | solution.py:36
  40.4 0.0 copy-done.6
  40.4 0.0 copy-done.7
  40.4 0.1 add_convert_fusion.2
  40.5 0.0 copy-done.5
  40.5 0.1 iota_compare_fusion
  40.6 0.0 copy-done.3
  40.6 0.2 multiply_convert_fusion
  40.8 12.9 %all-to-all-done.1 = bf16[16,4,2432]{2,1,0:T(4,128)(2,1)S(1)} async-done(((bf16[16,4,2432]{2,1,0:T(4,128)(2,1)}), bf16[16,4,2432]{2,1,0:T(4,128)(2,1)S(1)}, u32[]{:S(2)}, u32[]{:S(2)}) %all-to-all-start.1) | async-done | bytes 311328 | tf_op jit(solution)/shard_map/all_to_all | solution.py:36
  53.7 0.1 convert_reduce_fusion
  53.8 0.1 slice_reduce_fusion.1
  53.9 0.1 slice_multiply_fusion
  54.1 0.1 fusion.20
  54.2 0.1 fusion.21
  54.2 0.1 subtract_convert_fusion.1
  54.4 0.1 pad_maximum_fusion
  54.5 0.0 copy-done.4
  54.5 0.3 fusion.22
  54.8 0.2 fusion.23
  55.1 0.2 fusion.8
  55.2 0.2 fusion.3
  55.5 0.2 fusion.1
  55.7 0.1 broadcast_in_dim.45
  55.8 24.6 %all_to_all.51 = bf16[16,4,2048]{2,1,0:T(4,128)(2,1)S(1)} all-to-all(bf16[16,4,2048]{2,1,0:T(4,128)(2,1)S(1)} %broadcast_in_dim.45), channel_id=1, replica_groups=mesh['x'=4,'z'=16,'y'=4,'core'=2] {'z'}, dimensions={0} | all-to-all | bytes 524288 | tf_op jit(solution)/shard_map/all_to_all | solution.py:36
  80.4 0.1 broadcast_in_dim.46
  80.5 0.1 broadcast_in_dim.78
  80.6 0.0 copy-start
  80.6 12.3 %all_to_all.52 = bf16[4,64,2048]{2,1,0:T(8,128)(2,1)S(1)} all-to-all(bf16[4,64,2048]{2,1,0:T(8,128)(2,1)S(1)} %broadcast_in_dim.78), channel_id=1, replica_groups=mesh['x'=4,'z'=16,'y'=4,'core'=2] {'x'}, dimensions={0} | all-to-all | bytes 2097152 | tf_op jit(solution)/shard_map/all_to_all | solution.py:36
  92.9 0.0 copy-done
  92.9 0.4 spread_dot.2
  93.3 0.0 copy-start.2
  93.4 11.1 %all_to_all.53 = bf16[4,256,256]{2,1,0:T(8,128)(2,1)S(1)} all-to-all(bf16[4,256,256]{2,1,0:T(8,128)(2,1)S(1)} %spread_dot.2), channel_id=1, replica_groups=mesh['x'=4,'z'=16,'y'=4,'core'=2] {'y'}, dimensions={0} | all-to-all | bytes 1048576 | tf_op jit(solution)/shard_map/all_to_all | solution.py:36
  104.4 0.1 reduce_sum.94
  104.5 11.0 %all-gather = bf16[512,256]{1,0:T(8,128)(2,1)S(1)} all-gather(bf16[256,256]{1,0:T(8,128)(2,1)S(1)} %reduce_sum.94), channel_id=2, replica_groups=mesh['x'=4,'z'=16,'y'=4,'core'=2] {'core'}, dimensions={0}, use_global_device_ids=true | all-gather | bytes 393216 | tf_op jit(solution)/shard_map/all_gather | solution.py:51
  115.5 0.0 copy-done.2
  115.5 0.6 gateup_terms.1
  116.1 15.9 %all_to_all.54 = bf16[4,64,1792]{2,1,0:T(8,128)(2,1)S(1)} all-to-all(bf16[4,64,1792]{2,1,0:T(8,128)(2,1)S(1)} %get-tuple-element.16), channel_id=1, replica_groups=mesh['x'=4,'z'=16,'y'=4,'core'=2] {'x'}, dimensions={0} | all-to-all | bytes 1835008 | tf_op jit(solution)/shard_map/all_to_all | solution.py:36
  132.0 0.2 reduce_sum.95
  132.1 0.1 reshape.199
  132.2 20.7 %all_to_all.55 = bf16[16,4,1792]{2,1,0:T(4,128)(2,1)S(1)} all-to-all(bf16[16,4,1792]{2,1,0:T(4,128)(2,1)S(1)} %reshape.199), channel_id=1, replica_groups=mesh['x'=4,'z'=16,'y'=4,'core'=2] {'z'}, dimensions={0} | all-to-all | bytes 458752 | tf_op jit(solution)/shard_map/all_to_all | solution.py:36
  152.9 0.1 convert_reduce_fusion.1
  153.0 0.1 slice_reduce_fusion
  153.1 0.1 slice_multiply_fusion.1
  153.2 0.1 fusion.12
  153.3 21.4 %all_to_all.56 = bf16[16,4,832]{2,1,0:T(4,128)(2,1)S(1)} all-to-all(bf16[16,4,832]{2,1,0:T(4,128)(2,1)S(1)} %broadcast_in_dim.79), channel_id=1, replica_groups=mesh['x'=4,'z'=16,'y'=4,'core'=2] {'z'}, dimensions={0} | all-to-all | bytes 212992 | tf_op jit(solution)/shard_map/all_to_all | solution.py:36
  174.7 0.1 broadcast_in_dim.80
  174.8 9.0 %all_to_all.57 = bf16[4,64,832]{2,1,0:T(8,128)(2,1)S(1)} all-to-all(bf16[4,64,832]{2,1,0:T(8,128)(2,1)S(1)} %broadcast_in_dim.81), channel_id=1, replica_groups=mesh['x'=4,'z'=16,'y'=4,'core'=2] {'x'}, dimensions={0} | all-to-all | bytes 851968 | tf_op jit(solution)/shard_map/all_to_all | solution.py:36
  183.8 0.0 copy-done.1
  183.8 1.1 spread_dot.3
  184.9 3.5 %all-to-all-start.9 = ((bf16[4,256,256]{2,1,0:T(8,128)(2,1)}), bf16[4,256,256]{2,1,0:T(8,128)(2,1)S(1)}, u32[]{:S(2)}, u32[]{:S(2)}) async-start(bf16[4,256,256]{2,1,0:T(8,128)(2,1)} %spread_dot.3), calls=%async_computation.9 | async-start | bytes 1048576 | tf_op jit(solution)/shard_map/all_to_all | solution.py:36
  188.4 0.1 maximum_bitcast_fusion
  188.5 0.6 copy.57
  189.1 6.2 %all-to-all-done.9 = bf16[4,256,256]{2,1,0:T(8,128)(2,1)S(1)} async-done(((bf16[4,256,256]{2,1,0:T(8,128)(2,1)}), bf16[4,256,256]{2,1,0:T(8,128)(2,1)S(1)}, u32[]{:S(2)}, u32[]{:S(2)}) %all-to-all-start.9) | async-done | bytes 524320 | tf_op jit(solution)/shard_map/all_to_all | solution.py:36
  195.3 0.1 reduce_sum.98
  195.4 7.2 %all-gather.1 = bf16[512,256]{1,0:T(8,128)(2,1)S(1)} all-gather(bf16[256,256]{1,0:T(8,128)(2,1)S(1)} %reduce_sum.98), channel_id=3, replica_groups=mesh['x'=4,'z'=16,'y'=4,'core'=2] {'core'}, dimensions={0}, use_global_device_ids=true | all-gather | bytes 393216 | tf_op jit(solution)/shard_map/all_gather | solution.py:51
  202.6 0.1 fusion.7
  202.7 0.1 reshape.201
  202.8 0.1 copy.56
  202.9 0.7 reshape.202
  (24 shorter events, 0.3 us)
Async XLA Ops:
  20.2 20.2 %copy-start.6 = (bf16[256]{0:T(256)(128)(2,1)S(1)}, bf16[256]{0:T(256)(128)(2,1)}, u32[]{:S(2)}) copy-start(bf16[256]{0:T(256)(128)(2,1)} %param.16) | copy-start | bytes 1540
  20.2 20.2 %copy-start.7 = (s32[2]{0:T(128)S(1)}, s32[2]{0:T(128)}, u32[]{:S(2)}) copy-start(s32[2]{0:T(128)} %param.21) | copy-start | bytes 28
  20.2 20.3 %copy-start.5 = (s32[2]{0:T(128)S(1)}, s32[2]{0:T(128)}, u32[]{:S(2)}) copy-start(s32[2]{0:T(128)} %param.20) | copy-start | bytes 28
  20.2 20.4 %copy-start.3 = (bf16[256,2,832]{0,2,1:T(8,128)(2,1)S(1)}, bf16[256,2,832]{0,2,1:T(8,128)(2,1)}, u32[]{:S(2)}) copy-start(bf16[256,2,832]{0,2,1:T(8,128)(2,1)} %param.17) | copy-start | bytes 2555908
  21.1 32.6 %all-to-all-start.1 = ((bf16[16,4,2432]{2,1,0:T(4,128)(2,1)}), bf16[16,4,2432]{2,1,0:T(4,128)(2,1)S(1)}, u32[]{:S(2)}, u32[]{:S(2)}) async-start(bf16[16,4,2432]{2,1,0:T(4,128)(2,1)} %sum_parts.1), calls=%async_computation.1 | async-start | bytes 622592 | tf_op jit(solution)/shard_map/all_to_all | solution.py:36
  40.6 13.9 %copy-start.4 = (bf16[2,768,1,256]{3,1,2,0:T(8,128)(2,1)S(1)}, bf16[2,768,1,256]{3,1,2,0:T(8,128)(2,1)}, u32[]{:S(2)}) copy-start(bf16[2,768,1,256]{3,1,2,0:T(8,128)(2,1)} %param.19) | copy-start | bytes 2359300
  80.6 12.3 %copy-start = (bf16[2048,256]{1,0:T(8,128)(2,1)S(1)}, bf16[2048,256]{1,0:T(8,128)(2,1)}, u32[]{:S(2)}) copy-start(bf16[2048,256]{1,0:T(8,128)(2,1)} %weights_ref.2) | copy-start | bytes 3145732
  93.3 22.1 %copy-start.2 = (bf16[256,256]{1,0:T(8,128)(2,1)S(1)}, bf16[256,256]{1,0:T(8,128)(2,1)}, u32[]{:S(2)}) copy-start(bf16[256,256]{1,0:T(8,128)(2,1)} %get-tuple-element.14.rows_ref) | copy-start | bytes 393220
  152.9 30.9 %copy-start.1 = (bf16[832,256]{1,0:T(8,128)(2,1)S(1)}, bf16[832,256]{1,0:T(8,128)(2,1)}, u32[]{:S(2)}) copy-start(bf16[832,256]{1,0:T(8,128)(2,1)} %weights_ref.3) | copy-start | bytes 1277956
  184.9 10.4 %all-to-all-start.9 = ((bf16[4,256,256]{2,1,0:T(8,128)(2,1)}), bf16[4,256,256]{2,1,0:T(8,128)(2,1)S(1)}, u32[]{:S(2)}, u32[]{:S(2)}) async-start(bf16[4,256,256]{2,1,0:T(8,128)(2,1)} %spread_dot.3), calls=%async_computation.9 | async-start | bytes 1048576 | tf_op jit(solution)/shard_map/all_to_all | solution.py:36

commit v11 on v8

--- a/solution.py
+++ b/solution.py
@@ -15,7 +15,7 @@
 WIDE = ("x", "z")
 MP = ("y", "core")
 XS, ZS, YS, CORES = 4, 16, 4, 2
-QUERY_CHUNKS = 4
+QUERY_CHUNKS = 8
 
 
 def rotate(vectors, offsets):

time: 204 us -> 205 us (level)
  no operation moved by 1% of the time
where the time goes in v11:
time: 205 us
  blocking collectives  150 us (73%)
  starting transfers between devices  22.7 us (11%)
  waiting for transfers between devices  19.1 us (9%)
  Pallas kernels  6.02 us (3%)
  local copies, waits for them, and re-layouts  2.97 us (1%)
  other arithmetic  2.21 us (1%)
    all_to_all x8, blocking collectives, exchange(): return lax.all_to_all(blocks, axis, 0, 0, tiled=True)  131 us
    all_to_all x2, starting transfers between devices, exchange(): return lax.all_to_all(blocks, axis, 0, 0, tiled=True)  22.7 us
    all_to_all x2, waiting for transfers between devices, exchange(): return lax.all_to_all(blocks, axis, 0, 0, tiled=True)  19.1 us
    all_gather x2, blocking collectives, group_terms(): lax.all_gather(total.astype(jnp.bfloat16), 'core', axis=0, tiled=False)  18.2 us
  transfers between devices with their start and end apart: 2, of which 2 were waited for; matrix products, arithmetic and copies ran while one was open for 0% of the time, Pallas kernels for 0%

profile of v11, /device:TPU:1, one launch (start us, length us, event | category | flops | bytes accessed | tf_op | source)
XLA Modules:
  0.0 204.5 jit_solution(2509963590428545127)
XLA Ops:
  0.6 3.9 %first_terms.1 = (bf16[4,64,2432]{2,1,0:T(8,128)(2,1)}, bf16[256,256]{1,0:T(8,128)(2,1)}) custom-call(bf16[2,128,256]{2,1,0:T(8,128)(2,1)} %inputs_hbm.1, bf16[256]{0:T(256)(128)(2,1)} %gain_hbm.1, bf16[256,2048]{1,0:T(8,128)(2,1)} %query_hbm.1, bf16[256,256]{1,0:T(8,128)(2,1)} %bitcast.38), custom_call_target="tpu_custom_call" | custom-call | tf_op jit(solution)/shard_map/first_terms/pallas_call | solution.py:119
  4.5 16.6 %all_to_all.50 = bf16[4,64,2432]{2,1,0:T(8,128)(2,1)S(1)} all-to-all(bf16[4,64,2432]{2,1,0:T(8,128)(2,1)} %get-tuple-element.10), channel_id=1, replica_groups=mesh['x'=4,'z'=16,'y'=4,'core'=2] {'x'}, dimensions={0} | all-to-all | bytes 2490368 | tf_op jit(solution)/shard_map/all_to_all | solution.py:36
  21.1 0.0 copy-start.6
  21.1 0.2 reduce_sum.102
  21.3 0.8 reshape.196
  22.1 19.2 %all-to-all-start.1 = ((bf16[16,4,2432]{2,1,0:T(4,128)(2,1)}), bf16[16,4,2432]{2,1,0:T(4,128)(2,1)S(1)}, u32[]{:S(2)}, u32[]{:S(2)}) async-start(bf16[16,4,2432]{2,1,0:T(4,128)(2,1)} %reshape.196), calls=%async_computation.1 | async-start | bytes 622592 | tf_op jit(solution)/shard_map/all_to_all | solution.py:36
  41.3 0.0 copy-done.6
  41.4 0.0 copy-done.7
  41.4 0.1 add_convert_fusion.2
  41.5 0.0 copy-done.5
  41.5 0.1 iota_compare_fusion
  41.5 0.0 copy-done.3
  41.5 0.2 multiply_convert_fusion
  41.7 12.9 %all-to-all-done.1 = bf16[16,4,2432]{2,1,0:T(4,128)(2,1)S(1)} async-done(((bf16[16,4,2432]{2,1,0:T(4,128)(2,1)}), bf16[16,4,2432]{2,1,0:T(4,128)(2,1)S(1)}, u32[]{:S(2)}, u32[]{:S(2)}) %all-to-all-start.1) | async-done | bytes 311328 | tf_op jit(solution)/shard_map/all_to_all | solution.py:36
  54.6 0.1 convert_reduce_fusion
  54.8 0.1 slice_reduce_fusion.1
  54.9 0.1 slice_multiply_fusion
  55.0 0.1 fusion.20
  55.1 0.1 fusion.21
  55.2 0.1 subtract_convert_fusion.1
  55.4 0.1 pad_maximum_fusion
  55.4 0.0 copy-done.4
  55.4 0.3 fusion.22
  55.8 0.2 fusion.23
  56.0 0.2 fusion.8
  56.2 0.2 fusion.3
  56.5 0.2 fusion.1
  56.7 0.1 broadcast_in_dim.45
  56.8 24.6 %all_to_all.51 = bf16[16,4,2048]{2,1,0:T(4,128)(2,1)S(1)} all-to-all(bf16[16,4,2048]{2,1,0:T(4,128)(2,1)S(1)} %broadcast_in_dim.45), channel_id=1, replica_groups=mesh['x'=4,'z'=16,'y'=4,'core'=2] {'z'}, dimensions={0} | all-to-all | bytes 524288 | tf_op jit(solution)/shard_map/all_to_all | solution.py:36
  81.4 0.1 broadcast_in_dim.46
  81.4 0.1 broadcast_in_dim.78
  81.5 0.0 copy-start
  81.6 12.3 %all_to_all.52 = bf16[4,64,2048]{2,1,0:T(8,128)(2,1)S(1)} all-to-all(bf16[4,64,2048]{2,1,0:T(8,128)(2,1)S(1)} %broadcast_in_dim.78), channel_id=1, replica_groups=mesh['x'=4,'z'=16,'y'=4,'core'=2] {'x'}, dimensions={0} | all-to-all | bytes 2097152 | tf_op jit(solution)/shard_map/all_to_all | solution.py:36
  93.9 0.0 copy-done
  93.9 0.4 spread_dot.2
  94.3 0.0 copy-start.2
  94.3 11.1 %all_to_all.53 = bf16[4,256,256]{2,1,0:T(8,128)(2,1)S(1)} all-to-all(bf16[4,256,256]{2,1,0:T(8,128)(2,1)S(1)} %spread_dot.2), channel_id=1, replica_groups=mesh['x'=4,'z'=16,'y'=4,'core'=2] {'y'}, dimensions={0} | all-to-all | bytes 1048576 | tf_op jit(solution)/shard_map/all_to_all | solution.py:36
  105.4 0.1 reduce_sum.107
  105.5 11.0 %all-gather = bf16[512,256]{1,0:T(8,128)(2,1)S(1)} all-gather(bf16[256,256]{1,0:T(8,128)(2,1)S(1)} %reduce_sum.107), channel_id=2, replica_groups=mesh['x'=4,'z'=16,'y'=4,'core'=2] {'core'}, dimensions={0}, use_global_device_ids=true | all-gather | bytes 393216 | tf_op jit(solution)/shard_map/all_gather | solution.py:51
  116.4 0.0 copy-done.2
  116.4 0.6 gateup_terms.1
  117.0 15.9 %all_to_all.54 = bf16[4,64,1792]{2,1,0:T(8,128)(2,1)S(1)} all-to-all(bf16[4,64,1792]{2,1,0:T(8,128)(2,1)S(1)} %get-tuple-element.16), channel_id=1, replica_groups=mesh['x'=4,'z'=16,'y'=4,'core'=2] {'x'}, dimensions={0} | all-to-all | bytes 1835008 | tf_op jit(solution)/shard_map/all_to_all | solution.py:36
  132.9 0.2 reduce_sum.108
  133.1 0.1 reshape.203
  133.1 20.7 %all_to_all.55 = bf16[16,4,1792]{2,1,0:T(4,128)(2,1)S(1)} all-to-all(bf16[16,4,1792]{2,1,0:T(4,128)(2,1)S(1)} %reshape.203), channel_id=1, replica_groups=mesh['x'=4,'z'=16,'y'=4,'core'=2] {'z'}, dimensions={0} | all-to-all | bytes 458752 | tf_op jit(solution)/shard_map/all_to_all | solution.py:36
  153.8 0.1 convert_reduce_fusion.1
  153.9 0.1 slice_reduce_fusion
  154.0 0.1 slice_multiply_fusion.1
  154.1 0.1 fusion.12
  154.3 21.4 %all_to_all.56 = bf16[16,4,832]{2,1,0:T(4,128)(2,1)S(1)} all-to-all(bf16[16,4,832]{2,1,0:T(4,128)(2,1)S(1)} %broadcast_in_dim.79), channel_id=1, replica_groups=mesh['x'=4,'z'=16,'y'=4,'core'=2] {'z'}, dimensions={0} | all-to-all | bytes 212992 | tf_op jit(solution)/shard_map/all_to_all | solution.py:36
  175.7 0.1 broadcast_in_dim.80
  175.8 9.0 %all_to_all.57 = bf16[4,64,832]{2,1,0:T(8,128)(2,1)S(1)} all-to-all(bf16[4,64,832]{2,1,0:T(8,128)(2,1)S(1)} %broadcast_in_dim.81), channel_id=1, replica_groups=mesh['x'=4,'z'=16,'y'=4,'core'=2] {'x'}, dimensions={0} | all-to-all | bytes 851968 | tf_op jit(solution)/shard_map/all_to_all | solution.py:36
  184.8 0.0 copy-done.1
  184.8 1.1 spread_dot.3
  185.9 3.5 %all-to-all-start.9 = ((bf16[4,256,256]{2,1,0:T(8,128)(2,1)}), bf16[4,256,256]{2,1,0:T(8,128)(2,1)S(1)}, u32[]{:S(2)}, u32[]{:S(2)}) async-start(bf16[4,256,256]{2,1,0:T(8,128)(2,1)} %spread_dot.3), calls=%async_computation.9 | async-start | bytes 1048576 | tf_op jit(solution)/shard_map/all_to_all | solution.py:36
  189.3 0.1 maximum_bitcast_fusion
  189.4 0.6 copy.60
  190.0 6.2 %all-to-all-done.9 = bf16[4,256,256]{2,1,0:T(8,128)(2,1)S(1)} async-done(((bf16[4,256,256]{2,1,0:T(8,128)(2,1)}), bf16[4,256,256]{2,1,0:T(8,128)(2,1)S(1)}, u32[]{:S(2)}, u32[]{:S(2)}) %all-to-all-start.9) | async-done | bytes 524320 | tf_op jit(solution)/shard_map/all_to_all | solution.py:36
  196.2 0.1 reduce_sum.111
  196.3 7.2 %all-gather.1 = bf16[512,256]{1,0:T(8,128)(2,1)S(1)} all-gather(bf16[256,256]{1,0:T(8,128)(2,1)S(1)} %reduce_sum.111), channel_id=3, replica_groups=mesh['x'=4,'z'=16,'y'=4,'core'=2] {'core'}, dimensions={0}, use_global_device_ids=true | all-gather | bytes 393216 | tf_op jit(solution)/shard_map/all_gather | solution.py:51
  203.6 0.1 fusion.7
  203.6 0.1 reshape.205
  203.7 0.1 copy.59
  203.8 0.7 reshape.206
  (25 shorter events, 0.3 us)
Async XLA Ops:
  21.1 20.2 %copy-start.6 = (bf16[256]{0:T(256)(128)(2,1)S(1)}, bf16[256]{0:T(256)(128)(2,1)}, u32[]{:S(2)}) copy-start(bf16[256]{0:T(256)(128)(2,1)} %param.16) | copy-start | bytes 1540
  21.1 20.3 %copy-start.7 = (s32[2]{0:T(128)S(1)}, s32[2]{0:T(128)}, u32[]{:S(2)}) copy-start(s32[2]{0:T(128)} %param.21) | copy-start | bytes 28
  21.1 20.4 %copy-start.5 = (s32[2]{0:T(128)S(1)}, s32[2]{0:T(128)}, u32[]{:S(2)}) copy-start(s32[2]{0:T(128)} %param.20) | copy-start | bytes 28
  21.1 20.5 %copy-start.3 = (bf16[256,2,832]{0,2,1:T(8,128)(2,1)S(1)}, bf16[256,2,832]{0,2,1:T(8,128)(2,1)}, u32[]{:S(2)}) copy-start(bf16[256,2,832]{0,2,1:T(8,128)(2,1)} %param.17) | copy-start | bytes 2555908
  22.1 32.5 %all-to-all-start.1 = ((bf16[16,4,2432]{2,1,0:T(4,128)(2,1)}), bf16[16,4,2432]{2,1,0:T(4,128)(2,1)S(1)}, u32[]{:S(2)}, u32[]{:S(2)}) async-start(bf16[16,4,2432]{2,1,0:T(4,128)(2,1)} %reshape.196), calls=%async_computation.1 | async-start | bytes 622592 | tf_op jit(solution)/shard_map/all_to_all | solution.py:36
  41.5 13.9 %copy-start.4 = (bf16[2,768,1,256]{3,1,2,0:T(8,128)(2,1)S(1)}, bf16[2,768,1,256]{3,1,2,0:T(8,128)(2,1)}, u32[]{:S(2)}) copy-start(bf16[2,768,1,256]{3,1,2,0:T(8,128)(2,1)} %param.19) | copy-start | bytes 2359300
  81.5 12.3 %copy-start = (bf16[2048,256]{1,0:T(8,128)(2,1)S(1)}, bf16[2048,256]{1,0:T(8,128)(2,1)}, u32[]{:S(2)}) copy-start(bf16[2048,256]{1,0:T(8,128)(2,1)} %weights_ref.2) | copy-start | bytes 3145732
  94.3 22.1 %copy-start.2 = (bf16[256,256]{1,0:T(8,128)(2,1)S(1)}, bf16[256,256]{1,0:T(8,128)(2,1)}, u32[]{:S(2)}) copy-start(bf16[256,256]{1,0:T(8,128)(2,1)} %get-tuple-element.14.rows_ref) | copy-start | bytes 393220
  153.8 30.9 %copy-start.1 = (bf16[832,256]{1,0:T(8,128)(2,1)S(1)}, bf16[832,256]{1,0:T(8,128)(2,1)}, u32[]{:S(2)}) copy-start(bf16[832,256]{1,0:T(8,128)(2,1)} %weights_ref.3) | copy-start | bytes 1277956
  185.9 10.4 %all-to-all-start.9 = ((bf16[4,256,256]{2,1,0:T(8,128)(2,1)}), bf16[4,256,256]{2,1,0:T(8,128)(2,1)S(1)}, u32[]{:S(2)}, u32[]{:S(2)}) async-start(bf16[4,256,256]{2,1,0:T(8,128)(2,1)} %spread_dot.3), calls=%async_computation.9 | async-start | bytes 1048576 | tf_op jit(solution)/shard_map/all_to_all | solution.py:36
